TPU v7x, 32 devices: a whole 2x2x4 slice. The times are simulated.
32 devices in a mesh: layer: 4 (over z), feat: 2 (over y), tok: 4 (over x, core).
Axes of the slice: x: 2, y: 2, z: 4, core: 2. Of those that a mesh axis runs over, the one named last changes fastest.
Arguments:
- sublevel_entries: bfloat16 [4, 1024, 1152], P('layer', 'tok'), may hold values from -6 to 6
- readin_matrix: bfloat16 [4, 1152, 8192], P('layer', None, ('feat', 'tok')), may hold values from -0.1875 to 0.1875
- readin_offset: float32 [4, 8192], P('layer', ('feat', 'tok')), may hold values from -3 to 3
- cutoff_exceeded: int32 [4, 1024, 8192], P('layer', None, ('feat', 'tok')), may hold values 0 or 1
- writeout_matrix: bfloat16 [4, 2, 8192, 1152], P('layer', None, ('feat', 'tok')), may hold values from -0.0625 to 0.0625
- hidden_block_result: bfloat16 [2, 1024, 1152], P(None, 'tok'), may hold values from -6 to 6
- writing_depth_number: int32 [2], replicated, may hold values from 0 to 3, as said below
Outputs:
- enc_grad: bfloat16 [4, 1152, 8192], P('layer', None, ('feat', 'tok'))
- dec_grad: bfloat16 [4, 2, 8192, 1152], P('layer', None, ('feat', 'tok'))
- bias_grad: float32 [4, 8192], P('layer', ('feat', 'tok'))
Inputs may be any that keep to these rules, and one draw needn't show every extreme that they name: `writing_depth_number`: one of the two entries is 3 and the other is smaller; either may come first.
All inputs are finite; a program needn't handle non-finite values. No bound on the sum of `cutoff_exceeded` on one device may be relied on, other than what follows from the above.
Results may differ from a plain program's by a relative error of at most 0.007.
Values may be sent and summed in bfloat16 or wider, within the bound.
No kernel may reach another device: no remote copies, remote signals or barrier semaphores. Data moves between devices by JAX's collectives and lax.ppermute only.
A program may use at most 128 MiB of HBM per device.

v0:
```python
import math

import jax
import jax.numpy as jnp
from jax import lax
from jax.sharding import PartitionSpec as P


def shards(
    sublevel_entries,
    readin_matrix,
    readin_offset,
    cutoff_exceeded,
    writeout_matrix,
    hidden_block_result,
    writing_depth_number,
):
    layer_index = lax.axis_index("layer")
    owner_flag = jnp.logical_and(layer_index == 0, lax.axis_index("feat") == 0).astype(jnp.float32)
    gathered = lax.all_gather(sublevel_entries, "tok", axis=1, tiled=True)[0]
    total_rows = gathered.shape[0]
    inverse = 1.0 / math.sqrt(total_rows)
    gate_choice_vector = cutoff_exceeded[0].astype(jnp.float32)
    encoded_prejump_signal = (
        jnp.dot(gathered, readin_matrix[0], preferred_element_type=jnp.float32)
        + readin_offset[0][None, :]
    )
    sparse_code_entries = (encoded_prejump_signal * gate_choice_vector).astype(jnp.bfloat16)
    live_mask = (layer_index <= writing_depth_number).astype(jnp.float32)
    target_count = writeout_matrix.shape[1]
    partials = jnp.stack(
        [
            jnp.dot(
                sparse_code_entries,
                writeout_matrix[0, desired_reconstruction],
                preferred_element_type=jnp.float32,
            )
            for desired_reconstruction in range(target_count)
        ]
    )
    goal_rows = hidden_block_result.shape[1]
    row_start = lax.axis_index("tok") * goal_rows
    current = lax.dynamic_slice_in_dim(partials, row_start, goal_rows, 1)
    partials = lax.dynamic_update_slice_in_dim(
        partials, current - owner_flag * hidden_block_result.astype(jnp.float32), row_start, 1
    )
    row_sums = lax.psum_scatter(
        partials * live_mask[:, None, None], ("feat", "tok"), scatter_dimension=1, tiled=True
    )
    summed = lax.psum(row_sums, "layer")
    scaled = lax.all_gather(
        (summed * inverse).astype(jnp.bfloat16), ("feat", "tok"), axis=1, tiled=True
    )
    dec_rows = []
    code_sensitivity = jnp.zeros(encoded_prejump_signal.shape, jnp.float32)
    for desired_reconstruction in range(target_count):
        dec_rows.append(
            (
                jnp.einsum(
                    "tf,td->fd",
                    sparse_code_entries,
                    scaled[desired_reconstruction],
                    preferred_element_type=jnp.float32,
                )
                * live_mask[desired_reconstruction]
            ).astype(jnp.bfloat16)
        )
        code_sensitivity = code_sensitivity + live_mask[desired_reconstruction] * jnp.einsum(
            "td,fd->tf",
            scaled[desired_reconstruction],
            writeout_matrix[0, desired_reconstruction],
            preferred_element_type=jnp.float32,
        )
    prejump_sensitivity = code_sensitivity * gate_choice_vector
    bias_grad = jnp.sum(prejump_sensitivity, axis=0)
    enc_grad = jnp.einsum(
        "td,tf->df",
        gathered,
        prejump_sensitivity.astype(jnp.bfloat16),
        preferred_element_type=jnp.float32,
    ).astype(jnp.bfloat16)
    return (enc_grad[None], jnp.stack(dec_rows)[None], bias_grad[None])


def solution(mesh):
    return jax.shard_map(
        shards,
        mesh=mesh,
        in_specs=(
            P("layer", "tok", None),
            P("layer", None, ("feat", "tok")),
            P("layer", ("feat", "tok")),
            P("layer", None, ("feat", "tok")),
            P("layer", None, ("feat", "tok"), None),
            P(None, "tok", None),
            P(),
        ),
        out_specs=(
            P("layer", None, ("feat", "tok")),
            P("layer", None, ("feat", "tok"), None),
            P("layer", ("feat", "tok")),
        ),
        check_vma=False,
    )
```

profile of v0, /device:TPU:0, one launch (start us, length us, event | category | flops | bytes accessed | tf_op | source)
XLA Modules:
  0.0 269.4 jit_solution(6062348699305379288)
XLA Ops:
  7.2 0.0 copy-start
  7.2 0.0 all-gather.3.cloned.1.call-start
  7.2 0.7 all-gather.3.cloned.1.call-update
  7.9 0.0 reduce-scatter.2.cloned.1.call-start
  8.0 0.7 compare_convert_fusion
  8.6 27.7 %all-gather.3.cloned.1.call-done = bf16[1,1024,1152]{2,1,0:T(8,128)(2,1)} async-done(((bf16[1,256,1152]{2,1,0:T(8,128)(2,1)}), bf16[1,1024,1152]{2,1,0:T(8,128)(2,1)}) %all-gather.3.cloned.1.call-update) | async-done | bytes 2359312 | tf_op jit(solution)/shard_map/all_gather | solution.py:20
  36.4 5.6 %fusion = bf16[1024,1024]{1,0:T(8,128)(2,1)S(1)} fusion(s32[1,1024,1024]{2,1,0:T(8,128)} %param.10, f32[1024]{0:T(1024)} %bitcast.66, bf16[1,1152,1024]{2,1,0:T(8,128)(2,1)S(1)} %copy-done, bf16[1,1024,1152]{2,1,0:T(8,128)(2,1)} %all-gather.3.cloned.1.call-done), kind=kOutput, calls=%fused_computation.11 | convolution fusion | flops 2420113408 | bytes 11014144 | tf_op jit(solution)/shard_map/dot_general | solution.py:25
  42.0 0.0 copy-done.2
  42.0 0.0 copy-start.6
  42.0 2.9 %convolution_bitcast_fusion = f32[1,1024,1152]{2,1,0:T(8,128)S(1)} fusion(bf16[1024,1024]{1,0:T(8,128)(2,1)S(1)} %fusion, bf16[1,2,1024,1152]{3,2,1,0:T(8,128)(2,1)S(1)} %copy-done.2), kind=kOutput, calls=%fused_computation.7 | convolution fusion | flops 2415919104 | bytes 9175040 | tf_op jit(solution)/shard_map/dot_general | solution.py:33
  44.9 2.9 %convolution_bitcast_fusion.1 = f32[1,1024,1152]{2,1,0:T(8,128)S(1)} fusion(bf16[1024,1024]{1,0:T(8,128)(2,1)S(1)} %fusion, bf16[1,2,1024,1152]{3,2,1,0:T(8,128)(2,1)S(1)} %copy-done.2), kind=kOutput, calls=%fused_computation.8 | convolution fusion | flops 2415919104 | bytes 9175040 | tf_op jit(solution)/shard_map/dot_general | solution.py:33
  47.7 0.6 pad_maximum_fusion
  48.4 1.8 fusion.8
  50.1 4.3 %broadcast_multiply_fusion = f32[2,1024,1152]{2,1,0:T(8,128)} fusion(f32[2,1024,1152]{2,1,0:T(8,128)S(1)} %fusion.8, f32[2]{0:T(128)S(1)} %compare_convert_fusion), kind=kLoop, calls=%fused_computation.6 | loop fusion | flops 2359296 | bytes 18874376 | tf_op jit(solution)/shard_map/mul | solution.py:48
  54.4 0.0 reduce-scatter.2.cloned.1.call-update
  54.5 0.0 all-reduce.2.cloned.1.call-start
  54.5 76.6 %reduce-scatter.2.cloned.1.call-done = f32[2,128,1152]{2,1,0:T(8,128)} async-done(((f32[2,1024,1152]{2,1,0:T(8,128)}), f32[2,128,1152]{2,1,0:T(8,128)}) %reduce-scatter.2.cloned.1.call-update) | async-done | bytes 1179664 | tf_op jit(solution)/shard_map/reduce_scatter | solution.py:47
  131.1 0.0 all-reduce.2.cloned.1.call-update
  131.1 0.2 all-gather.5.cloned.1.call-start
  131.4 58.1 %all-reduce.2.cloned.1.call-done = f32[2,128,1152]{2,1,0:T(8,128)} async-done(((f32[2,128,1152]{2,1,0:T(8,128)}), f32[2,128,1152]{2,1,0:T(8,128)}) %all-reduce.2.cloned.1.call-update) | async-done | bytes 1179664 | tf_op jit(solution)/shard_map/psum | solution.py:50
  189.4 2.2 multiply_convert_fusion
  191.6 0.0 all-gather.5.cloned.1.call-update
  191.6 0.6 fusion.30
  192.3 38.0 %all-gather.5.cloned.1.call-done = bf16[2,1024,1152]{2,1,0:T(8,128)(2,1)} async-done(((bf16[2,128,1152]{2,1,0:T(8,128)(2,1)}), bf16[2,1024,1152]{2,1,0:T(8,128)(2,1)}) %all-gather.5.cloned.1.call-update) | async-done | bytes 4718608 | tf_op jit(solution)/shard_map/all_gather | solution.py:51
  230.3 5.4 %fusion.9 = f32[1024,1024]{1,0:T(8,128)S(1)} fusion(bf16[2,1024,1152]{2,1,0:T(8,128)(2,1)} %all-gather.5.cloned.1.call-done, bf16[1,2,1024,1152]{3,2,1,0:T(8,128)(2,1)} %param.11), kind=kOutput, calls=%fused_computation.23 | convolution fusion | flops 2415919104 | bytes 8912896 | tf_op jit(solution)/shard_map/td,fd->tf/dot_general | solution.py:68
  235.7 7.1 %fusion.31 = (f32[1024]{0:T(1024)}, bf16[1024,1024]{1,0:T(8,128)(2,1)S(1)}) fusion(s32[1,1024,1024]{2,1,0:T(8,128)S(1)} %copy-done.4, f32[1024,1024]{1,0:T(8,128)S(1)} %fusion.9, f32[]{:T(128)} %bitcast.10, bf16[1,2,1024,1152]{3,2,1,0:T(8,128)(2,1)} %param.11, bf16[2,1024,1152]{2,1,0:T(8,128)(2,1)S(1)} %copy-done.3, f32[]{:T(128)} %bitcast), kind=kOutput, calls=%fused_computation.41 | convolution fusion | flops 2423258112 | bytes 15209472 | tf_op jit(solution)/shard_map/td,fd->tf/dot_general | solution.py:68
  242.8 3.2 %fusion.3 = bf16[1,1152,1024]{1,2,0:T(8,128)(2,1)S(1)} fusion(bf16[1,1024,1152]{2,1,0:T(8,128)(2,1)S(1)} %copy-done.5, bf16[1024,1024]{1,0:T(8,128)(2,1)S(1)} %get-tuple-element.9), kind=kOutput, calls=%fused_computation.15 | convolution fusion | flops 2417098752 | bytes 6815744 | tf_op jit(solution)/shard_map/td,tf->df/dot_general | solution.py:76
  246.0 2.5 copy.10
  248.5 6.0 %fusion.4 = bf16[1,1024,1152]{2,1,0:T(8,128)(2,1)S(1)} fusion(bf16[1024,1024]{1,0:T(8,128)(2,1)} %copy-done.6, f32[]{:T(128)} %bitcast.10, bf16[2,1024,1152]{2,1,0:T(8,128)(2,1)} %all-gather.5.cloned.1.call-done), kind=kOutput, calls=%fused_computation.16 | convolution fusion | flops 2418278400 | bytes 6816256 | tf_op jit(solution)/shard_map/tf,td->fd/dot_general | solution.py:59
  254.6 0.0 copy-start.1
  254.6 5.7 %fusion.5 = bf16[1,1024,1152]{2,1,0:T(8,128)(2,1)S(1)} fusion(bf16[1024,1024]{1,0:T(8,128)(2,1)S(1)} %copy-done.7, f32[]{:T(128)} %bitcast, bf16[2,1024,1152]{2,1,0:T(8,128)(2,1)} %all-gather.5.cloned.1.call-done), kind=kOutput, calls=%fused_computation.17 | convolution fusion | flops 2418278400 | bytes 6816256 | tf_op jit(solution)/shard_map/tf,td->fd/dot_general | solution.py:59
  260.2 2.7 maximum_bitcast_fusion
  (12 shorter events, 0.0 us)
Async XLA Ops:
  7.2 29.2 %copy-start = (bf16[1,1152,1024]{2,1,0:T(8,128)(2,1)S(1)}, bf16[1,1152,1024]{2,1,0:T(8,128)(2,1)}, u32[]{:S(2)}) copy-start(bf16[1,1152,1024]{2,1,0:T(8,128)(2,1)} %param.8) | copy-start | bytes 7077892
  7.2 29.2 %all-gather.3.cloned.1.call-start = ((), (), s32[]{:S(2)}) async-start(), calls=%async_computation.1 | async-start | bytes 2949120 | tf_op jit(solution)/shard_map/all_gather | solution.py:20
  7.9 123.2 %reduce-scatter.2.cloned.1.call-start = ((), (), s32[]{:S(2)}) async-start(), calls=%async_computation.2 | async-start | bytes 10616832 | tf_op jit(solution)/shard_map/reduce_scatter | solution.py:47
  36.4 5.6 %copy-start.2 = (bf16[1,2,1024,1152]{3,2,1,0:T(8,128)(2,1)S(1)}, bf16[1,2,1024,1152]{3,2,1,0:T(8,128)(2,1)}, u32[]{:S(2)}) copy-start(bf16[1,2,1024,1152]{3,2,1,0:T(8,128)(2,1)} %param.11) | copy-start | bytes 14155780
  42.0 2.9 %copy-start.6 = (bf16[1024,1024]{1,0:T(8,128)(2,1)}, bf16[1024,1024]{1,0:T(8,128)(2,1)S(1)}, u32[]{:S(2)}) copy-start(bf16[1024,1024]{1,0:T(8,128)(2,1)S(1)} %fusion) | copy-start | bytes 6291460
  54.5 135.0 %all-reduce.2.cloned.1.call-start = ((), (), s32[]{:S(2)}) async-start(), calls=%async_computation.3 | async-start | bytes 2359296 | tf_op jit(solution)/shard_map/psum | solution.py:50
  131.1 99.1 %all-gather.5.cloned.1.call-start = ((), (), s32[]{:S(2)}) async-start(), calls=%async_computation.4 | async-start | bytes 5308416 | tf_op jit(solution)/shard_map/all_gather | solution.py:51
  230.3 5.4 %copy-start.3 = (bf16[2,1024,1152]{2,1,0:T(8,128)(2,1)S(1)}, bf16[2,1024,1152]{2,1,0:T(8,128)(2,1)}, u32[]{:S(2)}) copy-start(bf16[2,1024,1152]{2,1,0:T(8,128)(2,1)} %all-gather.5.cloned.1.call-done) | copy-start | bytes 14155780
  230.3 5.4 %copy-start.4 = (s32[1,1024,1024]{2,1,0:T(8,128)S(1)}, s32[1,1024,1024]{2,1,0:T(8,128)}, u32[]{:S(2)}) copy-start(s32[1,1024,1024]{2,1,0:T(8,128)} %param.10) | copy-start | bytes 12582916
  235.7 7.1 %copy-start.5 = (bf16[1,1024,1152]{2,1,0:T(8,128)(2,1)S(1)}, bf16[1,1024,1152]{2,1,0:T(8,128)(2,1)}, u32[]{:S(2)}) copy-start(bf16[1,1024,1152]{2,1,0:T(8,128)(2,1)} %all-gather.3.cloned.1.call-done) | copy-start | bytes 7077892
  248.5 6.0 %copy-start.7 = (bf16[1024,1024]{1,0:T(8,128)(2,1)S(1)}, bf16[1024,1024]{1,0:T(8,128)(2,1)}, u32[]{:S(2)}) copy-start(bf16[1024,1024]{1,0:T(8,128)(2,1)} %copy-done.6) | copy-start | bytes 6291460
  254.6 8.3 %copy-start.1 = (bf16[1,1152,1024]{2,1,0:T(8,128)(2,1)S(1)}, bf16[1,1152,1024]{2,1,0:T(8,128)(2,1)}, u32[]{:S(2)}) copy-start(bf16[1,1152,1024]{2,1,0:T(8,128)(2,1)} %param.8) | copy-start | bytes 7077892
Sparse Core Ops, SparseCore 0:
  9.6 26.7 all-gather.2
  54.6 76.4 reduce-scatter.1
  133.5 55.8 all-reduce.1
  191.8 38.4 all-gather.4
where the time goes:
time: 270 us; the launch traced here: 269 us
  waiting for transfers between devices  201 us (74%)
  matrix products  38.7 us (14%)
  between operations  13.9 us (5%)
  other arithmetic  12.2 us (5%)
  local copies, waits for them, and re-layouts  3.18 us (1%)
    reduce_scatter x1, waiting for transfers between devices, shards(): lax.psum_scatter(partials * live_mask[:, None, None], ('feat', 'tok'), sc...  76.6 us
    psum x1, waiting for transfers between devices, shards(): summed = lax.psum(row_sums, 'layer')  58.1 us
    all_gather x1, waiting for transfers between devices, shards(): lax.all_gather((summed * inverse).astype(jnp.bfloat16), ('feat', 'tok'),...  38 us
    all_gather x1, waiting for transfers between devices, shards(): gathered = lax.all_gather(sublevel_entries, 'tok', axis=1, tiled=True)[0]  27.7 us
    dot_general x2, matrix products, shards(): jnp.einsum('td,fd->tf', scaled[desired_reconstruction], writeout_matrix[0...  12.5 us
    dot_general x2, matrix products, shards(): jnp.einsum('tf,td->fd', sparse_code_entries, scaled[desired_reconstructio...  11.7 us
    dot_general x2, matrix products, shards(): jnp.dot(sparse_code_entries, writeout_matrix[0, desired_reconstruction],...  5.74 us
    dot_general x1, matrix products, shards(): jnp.dot(gathered, readin_matrix[0], preferred_element_type=jnp.float32)  5.56 us
  transfers between devices with their start and end apart: 4, of which 4 were waited for; matrix products, arithmetic and copies ran while one was open for 0% of the time, Pallas kernels for 0%

commit v1 on v0

v1 whole, which is shorter than its diff:
```python
import math

import jax
import jax.numpy as jnp
from jax import lax
from jax.sharding import PartitionSpec as P

BF = jnp.bfloat16
F32 = jnp.float32


def plain_shards(entries, readin, offset, cutoff, writeout, hidden, depth):
    layer = lax.axis_index("layer")
    owner = jnp.logical_and(layer == 0, lax.axis_index("feat") == 0).astype(F32)
    gathered = lax.all_gather(entries, "tok", axis=1, tiled=True)[0]
    inverse = 1.0 / math.sqrt(gathered.shape[0])
    gate = cutoff[0].astype(F32)
    pre = jnp.dot(gathered, readin[0], preferred_element_type=F32) + offset[0][None, :]
    act = (pre * gate).astype(BF)
    live = (layer <= depth).astype(F32)
    targets = writeout.shape[1]
    partials = jnp.stack(
        [jnp.dot(act, writeout[0, t], preferred_element_type=F32) for t in range(targets)]
    )
    rows = hidden.shape[1]
    start = lax.axis_index("tok") * rows
    current = lax.dynamic_slice_in_dim(partials, start, rows, 1)
    partials = lax.dynamic_update_slice_in_dim(
        partials, current - owner * hidden.astype(F32), start, 1
    )
    summed = lax.psum_scatter(
        partials * live[:, None, None], ("feat", "tok"), scatter_dimension=1, tiled=True
    )
    summed = lax.psum(summed, "layer")
    scaled = lax.all_gather((summed * inverse).astype(BF), ("feat", "tok"), axis=1, tiled=True)
    dec = [
        (jnp.einsum("tf,td->fd", act, scaled[t], preferred_element_type=F32) * live[t]).astype(BF)
        for t in range(targets)
    ]
    sens = sum(
        live[t] * jnp.einsum("td,fd->tf", scaled[t], writeout[0, t], preferred_element_type=F32)
        for t in range(targets)
    )
    pre_grad = sens * gate
    enc = jnp.einsum("td,tf->df", gathered, pre_grad.astype(BF), preferred_element_type=F32)
    return enc.astype(BF)[None], jnp.stack(dec)[None], jnp.sum(pre_grad, axis=0)[None]


def column_chunks(width, count):
    tile = 128 if width % 128 == 0 else 1
    tiles = width // tile
    edges = [tile * ((tiles * k + count - 1) // count) for k in range(count + 1)]
    return [(a, b) for a, b in zip(edges[:-1], edges[1:]) if b > a]


def pick(flag, a, b):
    return jnp.where(flag, a, b)


def paired_shards(sizes, entries, readin, offset, cutoff, writeout, hidden, depth):
    layers, feats, toks = sizes
    layer, feat, tok = (lax.axis_index(a) for a in ("layer", "feat", "tok"))
    side, core = tok // 2, tok % 2

    def to_core(a):
        return lax.ppermute(a, "tok", [(t, t ^ 1) for t in range(toks)])

    def to_side(a):
        return lax.ppermute(a, "tok", [(t, t ^ 2) for t in range(toks)])

    def mixed(first):
        pairs = []
        for f in range(feats):
            for t in range(toks):
                over_side = (t % 2 == 0) == first
                goal = (f, t ^ 2) if over_side else (f ^ 1, t)
                pairs.append((f * toks + t, goal[0] * toks + goal[1]))
        return lambda a: lax.ppermute(a, ("feat", "tok"), pairs)

    to_first, to_second = mixed(True), mixed(False)
    binary = layers & (layers - 1) == 0

    def layer_goal(l, s):
        return l ^ s if binary else (l + s) % layers

    def layer_source(l, s):
        return l ^ s if binary else (l - s) % layers

    def to_layer(a, s):
        return lax.ppermute(a, "layer", [(l, layer_goal(l, s)) for l in range(layers)])

    own = entries[0]
    rows, width = own.shape
    total = rows * toks
    half = total // 2
    inverse = 1.0 / math.sqrt(total)
    live = (layer <= depth).astype(F32)
    weights = writeout[0]

    far = to_side(own)
    near = to_core(own)
    far_near = to_core(far)
    zero_core = core == 0
    tokens = jnp.concatenate(
        [
            pick(zero_core, own, near),
            pick(zero_core, near, own),
            pick(zero_core, far, far_near),
            pick(zero_core, far_near, far),
        ]
    )
    swapped = side == 1
    gate = cutoff[0]
    gate = jnp.concatenate(
        [
            lax.dynamic_slice_in_dim(gate, side * half, half, 0),
            lax.dynamic_slice_in_dim(gate, (1 - side) * half, half, 0),
        ]
    ).astype(F32)
    pre = jnp.dot(tokens, readin[0], preferred_element_type=F32) + offset[0][None, :]
    act = (pre * gate).astype(BF)

    flag = jnp.logical_and(layer == 0, feat == 0).astype(F32)
    mine_hidden = hidden.astype(F32) * flag

    def partial(target, lo, hi):
        w = lax.dynamic_index_in_dim(weights, target, 0, keepdims=False)[:, lo:hi]
        out = jnp.dot(act, w, preferred_element_type=F32).reshape(4, rows, hi - lo)
        sub = lax.dynamic_index_in_dim(mine_hidden, target, 0, keepdims=False)[:, lo:hi]
        place = (jnp.arange(4) == core).astype(F32)[:, None, None]
        return (out - place * sub[None]) * live[target]

    y1 = feat == 1

    def chunk(lo, hi):
        away = partial(1 - core, lo, hi).astype(BF)
        kept = partial(core, lo, hi)
        summed = kept + to_core(away).astype(F32)
        b0, b1, b2, b3 = (summed[i] for i in range(4))
        send = jnp.stack(
            [
                pick(zero_core, b0, pick(y1, b0, b1)),
                pick(zero_core, b1, pick(y1, b2, b3)),
            ]
        ).astype(BF)
        keep = jnp.stack(
            [
                pick(zero_core, b2, pick(y1, b1, b0)),
                pick(zero_core, b3, pick(y1, b3, b2)),
            ]
        )
        pair = keep + to_first(send).astype(F32)
        second = jnp.logical_or(jnp.logical_not(zero_core), y1)
        send = pick(second, pair[0], pair[1]).astype(BF)
        keep = pick(second, pair[1], pair[0])
        block = keep + to_second(send).astype(F32)
        piece = rows // layers
        low = block.astype(BF)
        mine = lax.dynamic_slice_in_dim(block, layer * piece, piece, 0)
        for s in range(1, layers):
            out = lax.dynamic_slice_in_dim(low, layer_goal(layer, s) * piece, piece, 0)
            mine = mine + to_layer(out, s).astype(F32)
        scaled = (mine * inverse).astype(BF)
        done = jnp.zeros((rows, hi - lo), BF)
        done = lax.dynamic_update_slice_in_dim(done, scaled, layer * piece, 0)
        for s in range(1, layers):
            done = lax.dynamic_update_slice_in_dim(
                done, to_layer(scaled, s), layer_source(layer, s) * piece, 0
            )
        got = to_second(done)
        m0, m1 = pick(second, got, done), pick(second, done, got)
        got = to_first(jnp.stack([m0, m1]))
        r0, r1 = got[0], got[1]
        full = jnp.stack(
            [
                pick(zero_core, r0, pick(y1, r0, m0)),
                pick(zero_core, r1, pick(y1, m0, r0)),
                pick(zero_core, m0, pick(y1, r1, m1)),
                pick(zero_core, m1, pick(y1, m1, r1)),
            ]
        ).reshape(total, hi - lo)
        other = to_core(full)
        return pick(zero_core, full, other), pick(zero_core, other, full)

    act_turned = act.T
    tokens_turned = tokens.T
    sens = jnp.zeros(act.shape, F32)
    dec = [[], []]
    for lo, hi in column_chunks(width, CHUNKS):
        for t, scaled in enumerate(chunk(lo, hi)):
            dec[t].append(
                (jnp.dot(act_turned, scaled, preferred_element_type=F32) * live[t]).astype(BF)
            )
            sens = sens + live[t] * jnp.einsum(
                "td,fd->tf", scaled, weights[t, :, lo:hi], preferred_element_type=F32
            )
    pre_grad = sens * gate
    bias = jnp.sum(pre_grad, axis=0)
    enc = jnp.dot(tokens_turned, pre_grad.astype(BF), preferred_element_type=F32).astype(BF)
    dec = jnp.stack([jnp.concatenate(d, axis=1) for d in dec])
    return enc[None], dec[None], bias[None]


CHUNKS = 2


def solution(mesh):
    sizes = tuple(mesh.shape[a] for a in ("layer", "feat", "tok"))

    def shards(*args):
        rows = args[0].shape[1]
        targets = args[4].shape[1]
        if sizes[1] == targets == 2 and sizes[2] == 4 and rows % sizes[0] == 0:
            return paired_shards(sizes, *args)
        return plain_shards(*args)

    return jax.shard_map(
        shards,
        mesh=mesh,
        in_specs=(
            P("layer", "tok", None),
            P("layer", None, ("feat", "tok")),
            P("layer", ("feat", "tok")),
            P("layer", None, ("feat", "tok")),
            P("layer", None, ("feat", "tok"), None),
            P(None, "tok", None),
            P(),
        ),
        out_specs=(
            P("layer", None, ("feat", "tok")),
            P("layer", None, ("feat", "tok"), None),
            P("layer", ("feat", "tok")),
        ),
        check_vma=False,
    )
```

time: 270 us -> 174 us (0.64)
  waiting for transfers between devices: 201 us -> 61.8 us
  starting transfers between devices: 0.34 us -> 32.1 us
  local copies, waits for them, and re-layouts: 3.18 us -> 21 us
  between operations: 13.9 us -> 1.27 us
  other arithmetic: 12.2 us -> 15.5 us
  matrix products: 38.7 us -> 42 us
    reduce_scatter x1 -> x0, waiting for transfers between devices: 76.6 us -> none  [shards(): lax.psum_scatter(partials * live_mask[:, None, None], ('feat', 'tok'), sc...]
    all_gather x2 -> x0, waiting for transfers between devices: 65.7 us -> none  [the longest x1 38 us: shards(): lax.all_gather((summed * inverse).astype(jnp.bfloat16), ('feat', 'tok'),...]
    ppermute x0 -> x27, waiting for transfers between devices: none -> 61.8 us  [the longest x8 38.8 us: mixed(): return lambda a: lax.ppermute(a, ('feat', 'tok'), pairs)]
    psum x1 -> x0, waiting for transfers between devices: 58.1 us -> none  [shards(): summed = lax.psum(row_sums, 'layer')]
    ppermute x0 -> x27, starting transfers between devices: none -> 32.1 us  [the longest x12 17.1 us: to_layer(): lax.ppermute(a, 'layer', [(l, layer_goal(l, s)) for l in range(layers)])]
    unnamed x17 -> x57, local copies, waits for them, and re-layouts: 2.53 us -> 8.44 us
    slice x1 -> x5, local copies, waits for them, and re-layouts: 0.65 us -> 6.28 us  [the longest x4 5.68 us: partial(): lax.dynamic_index_in_dim(mine_hidden, target, 0, keepdims=False)[:, lo:hi]]
    squeeze x0 -> x2, local copies, waits for them, and re-layouts: none -> 3.72 us  [the longest x1 2.55 us: partial(): w = lax.dynamic_index_in_dim(weights, target, 0, keepdims=False)[:, lo:hi]]
  transfers between devices with their start and end apart: 4 -> 27, of which waited for: 4 -> 16; matrix products, arithmetic and copies ran while one was open for 0% -> 19% of each run, Pallas kernels for 0% -> 0%
where the time goes in v1:
time: 174 us
  waiting for transfers between devices  61.8 us (36%)
  matrix products  42 us (24%)
  starting transfers between devices  32.1 us (18%)
  local copies, waits for them, and re-layouts  21 us (12%)
  other arithmetic  15.5 us (9%)
    ppermute x8, waiting for transfers between devices, mixed(): return lambda a: lax.ppermute(a, ('feat', 'tok'), pairs)  38.8 us
    ppermute x12, waiting for transfers between devices, to_layer(): lax.ppermute(a, 'layer', [(l, layer_goal(l, s)) for l in range(layers)])  18.4 us
    ppermute x12, starting transfers between devices, to_layer(): lax.ppermute(a, 'layer', [(l, layer_goal(l, s)) for l in range(layers)])  17.1 us
    dot_general x4, matrix products, paired_shards(): jnp.einsum('td,fd->tf', scaled, weights[t, :, lo:hi], preferred_element_t...  15.8 us
    ppermute x8, starting transfers between devices, mixed(): return lambda a: lax.ppermute(a, ('feat', 'tok'), pairs)  11.3 us
    dot_general x4, matrix products, paired_shards(): jnp.dot(act_turned, scaled, preferred_element_type=F32) * live[t]  8.55 us
    unnamed x57, local copies, waits for them, and re-layouts  8.44 us
    dot_general x4, matrix products, partial(): out = jnp.dot(act, w, preferred_element_type=F32).reshape(4, rows, hi - lo)  6.09 us
  transfers between devices with their start and end apart: 27, of which 16 were waited for; matrix products, arithmetic and copies ran while one was open for 19% of the time, Pallas kernels for 0%

profile of v1, /device:TPU:0, one launch (start us, length us, event | category | flops | bytes accessed | tf_op | source)
XLA Modules:
  0.0 173.8 jit_solution(4391910540177316479)
XLA Ops:
  0.6 3.0 %collective-permute-start.1 = (bf16[256,1152]{1,0:T(8,128)(2,1)}, bf16[256,1152]{1,0:T(8,128)(2,1)}, u32[]{:S(2)}, u32[]{:S(2)}) collective-permute-start(bf16[256,1152]{1,0:T(8,128)(2,1)} %bitcast.148), channel_id=1, source_target_pairs={{0,2},{1,3},{2,0},{3,1},{4,6},{5,7},{6,4},{7,5},{8,10},{9,11},{10,... | collective-permute-start | bytes 1769480 | tf_op jit(solution)/shard_map/ppermute | solution.py:69
  7.1 2.4 %dynamic-slice_bitcast_fusion.3 = (s32[512,1024]{1,0:T(8,128)}, s32[512,1024]{1,0:T(8,128)}) fusion(s32[1,1024,1024]{2,1,0:T(8,128)S(1)} %copy-done.7, s32[]{:T(128)S(6)} %select_n.331, s32[]{:T(128)S(6)} %select_n.332), kind=kLoop, calls=%fused_computation.24 | loop fusion | bytes 8388616 | tf_op jit(solution)/shard_map/dynamic_slice | solution.py:116
  10.1 2.5 %dynamic-slice_bitcast_fusion.1 = (bf16[1024,1152]{1,0:T(8,128)(2,1)}, bf16[1024,1152]{1,0:T(8,128)(2,1)}) fusion(bf16[1,2,1024,1152]{3,2,1,0:T(8,128)(2,1)S(1)} %bitcast.130, s32[]{:T(128)S(6)} %select_n.333, s32[]{:T(128)S(6)} %select_n.334), kind=kLoop, calls=%fused_computation.17 | loop fusion | bytes 9437192 | tf_op jit(solution)/shard_map/jit(dynamic_index_in_dim)/squeeze | solution.py:127
  12.6 4.7 %collective-permute-done.1 = bf16[256,1152]{1,0:T(8,128)(2,1)} collective-permute-done((bf16[256,1152]{1,0:T(8,128)(2,1)}, bf16[256,1152]{1,0:T(8,128)(2,1)}, u32[]{:S(2)}, u32[]{:S(2)}) %collective-permute-start.1) | collective-permute-done | bytes 589856 | tf_op jit(solution)/shard_map/ppermute | solution.py:69
  19.2 2.0 %slice.131 = f32[256,640]{1,0:T(8,128)} slice(f32[256,1152]{1,0:T(8,128)} %get-tuple-element.22), slice={[0:256], [0:640]} | slice | bytes 1310720 | tf_op jit(solution)/shard_map/slice | solution.py:129
  26.3 5.6 %multiply_convert_fusion = bf16[1024,1024]{1,0:T(8,128)(2,1)S(1)} fusion(s32[512,1024]{1,0:T(8,128)S(1)} %copy-done.5, s32[512,1024]{1,0:T(8,128)S(1)} %copy-done.3, f32[1024]{0:T(1024)S(1)} %bitcast.151, bf16[1,1152,1024]{2,1,0:T(8,128)(2,1)S(1)} %copy-done, bf16[256,1152]{1,0:T(8,128)(2,1)S(1)} %get-tuple-element.31, ...), kind=kOutput, calls=%fused_computation.3 | convolution fusion | flops 2430599168 | bytes 11014144 | tf_op jit(solution)/shard_map/dot_general | solution.py:120
  45.7 6.0 %collective-permute-done.16 = bf16[2,256,512]{2,1,0:T(8,128)(2,1)S(1)} collective-permute-done((bf16[2,256,512]{2,1,0:T(8,128)(2,1)S(1)}, bf16[2,256,512]{2,1,0:T(8,128)(2,1)S(1)}, u32[]{:S(2)}, u32[]{:S(2)}) %collective-permute-start.16) | collective-permute-done | bytes 524320 | tf_op jit(solution)/shard_map/ppermute | solution.py:78
  55.5 5.4 %collective-permute-done.17 = bf16[256,512]{1,0:T(8,128)(2,1)S(1)} collective-permute-done((bf16[256,512]{1,0:T(8,128)(2,1)S(1)}, bf16[256,512]{1,0:T(8,128)(2,1)S(1)}, u32[]{:S(2)}, u32[]{:S(2)}) %collective-permute-start.17) | collective-permute-done | bytes 262176 | tf_op jit(solution)/shard_map/ppermute | solution.py:78
  61.1 2.0 %collective-permute-start.18 = (bf16[64,512]{1,0:T(8,128)(2,1)S(1)}, bf16[64,512]{1,0:T(8,128)(2,1)S(1)}, u32[]{:S(2)}, u32[]{:S(2)}) collective-permute-start(bf16[64,512]{1,0:T(8,128)(2,1)S(1)} %get-tuple-element.47), channel_id=1, source_target_pairs={{0,8},{8,0},{16,24},{24,16},{1,9},{9,1},{17,25},{25,17},{2,10},{10... | collective-permute-start | bytes 196616 | tf_op jit(solution)/shard_map/ppermute | solution.py:90
  63.1 2.5 %collective-permute-start.20 = (bf16[64,512]{1,0:T(8,128)(2,1)S(1)}, bf16[64,512]{1,0:T(8,128)(2,1)S(1)}, u32[]{:S(2)}, u32[]{:S(2)}) collective-permute-start(bf16[64,512]{1,0:T(8,128)(2,1)S(1)} %get-tuple-element.48), channel_id=1, source_target_pairs={{0,24},{8,16},{16,8},{24,0},{1,25},{9,17},{17,9},{25,1},{2,26},{10... | collective-permute-start | bytes 196616 | tf_op jit(solution)/shard_map/ppermute | solution.py:90
  65.9 3.6 %collective-permute-done.20 = bf16[64,512]{1,0:T(8,128)(2,1)S(1)} collective-permute-done((bf16[64,512]{1,0:T(8,128)(2,1)S(1)}, bf16[64,512]{1,0:T(8,128)(2,1)S(1)}, u32[]{:S(2)}, u32[]{:S(2)}) %collective-permute-start.20) | collective-permute-done | bytes 65568 | tf_op jit(solution)/shard_map/ppermute | solution.py:90
  69.5 2.7 %collective-permute-done.19 = bf16[64,512]{1,0:T(8,128)(2,1)S(1)} collective-permute-done((bf16[64,512]{1,0:T(8,128)(2,1)S(1)}, bf16[64,512]{1,0:T(8,128)(2,1)S(1)}, u32[]{:S(2)}, u32[]{:S(2)}) %collective-permute-start.19) | collective-permute-done | bytes 65568 | tf_op jit(solution)/shard_map/ppermute | solution.py:90
  72.4 3.4 %collective-permute-start.21 = (bf16[64,512]{1,0:T(8,128)(2,1)S(1)}, bf16[64,512]{1,0:T(8,128)(2,1)S(1)}, u32[]{:S(2)}, u32[]{:S(2)}) collective-permute-start(bf16[64,512]{1,0:T(8,128)(2,1)S(1)} %get-tuple-element.11), channel_id=1, source_target_pairs={{0,8},{8,0},{16,24},{24,16},{1,9},{9,1},{17,25},{25,17},{2,10},{10... | collective-permute-start | bytes 196616 | tf_op jit(solution)/shard_map/ppermute | solution.py:90
  78.7 3.2 %collective-permute-done.23 = bf16[64,512]{1,0:T(8,128)(2,1)S(1)} collective-permute-done((bf16[64,512]{1,0:T(8,128)(2,1)S(1)}, bf16[64,512]{1,0:T(8,128)(2,1)S(1)}, u32[]{:S(2)}, u32[]{:S(2)}) %collective-permute-start.23) | collective-permute-done | bytes 65568 | tf_op jit(solution)/shard_map/ppermute | solution.py:90
  84.1 4.9 %collective-permute-done.24 = bf16[256,512]{1,0:T(8,128)(2,1)S(1)} collective-permute-done((bf16[256,512]{1,0:T(8,128)(2,1)S(1)}, bf16[256,512]{1,0:T(8,128)(2,1)S(1)}, u32[]{:S(2)}, u32[]{:S(2)}) %collective-permute-start.24) | collective-permute-done | bytes 262176 | tf_op jit(solution)/shard_map/ppermute | solution.py:78
  89.1 7.0 %collective-permute-done.5 = bf16[256,640]{1,0:T(8,128)(2,1)S(1)} collective-permute-done((bf16[256,640]{1,0:T(8,128)(2,1)S(1)}, bf16[256,640]{1,0:T(8,128)(2,1)S(1)}, u32[]{:S(2)}, u32[]{:S(2)}) %collective-permute-start.5) | collective-permute-done | bytes 327712 | tf_op jit(solution)/shard_map/ppermute | solution.py:78
  96.4 3.4 %collective-permute-start.7 = (bf16[64,640]{1,0:T(8,128)(2,1)S(1)}, bf16[64,640]{1,0:T(8,128)(2,1)S(1)}, u32[]{:S(2)}, u32[]{:S(2)}) collective-permute-start(bf16[64,640]{1,0:T(8,128)(2,1)S(1)} %get-tuple-element.46), channel_id=1, source_target_pairs={{0,16},{8,24},{16,0},{24,8},{1,17},{9,25},{17,1},{25,9},{2,18},{10... | collective-permute-start | bytes 245768 | tf_op jit(solution)/shard_map/ppermute | solution.py:90
  102.7 2.1 %collective-permute-done.7 = bf16[64,640]{1,0:T(8,128)(2,1)S(1)} collective-permute-done((bf16[64,640]{1,0:T(8,128)(2,1)S(1)}, bf16[64,640]{1,0:T(8,128)(2,1)S(1)}, u32[]{:S(2)}, u32[]{:S(2)}) %collective-permute-start.7) | collective-permute-done | bytes 81952 | tf_op jit(solution)/shard_map/ppermute | solution.py:90
  105.0 2.1 %collective-permute-start.10 = (bf16[64,640]{1,0:T(8,128)(2,1)S(1)}, bf16[64,640]{1,0:T(8,128)(2,1)S(1)}, u32[]{:S(2)}, u32[]{:S(2)}) collective-permute-start(bf16[64,640]{1,0:T(8,128)(2,1)S(1)} %get-tuple-element.7), channel_id=1, source_target_pairs={{0,16},{8,24},{16,0},{24,8},{1,17},{9,25},{17,1},{25,9},{2,18},{10... | collective-permute-start | bytes 245768 | tf_op jit(solution)/shard_map/ppermute | solution.py:90
  107.1 2.2 %collective-permute-start.11 = (bf16[64,640]{1,0:T(8,128)(2,1)S(1)}, bf16[64,640]{1,0:T(8,128)(2,1)S(1)}, u32[]{:S(2)}, u32[]{:S(2)}) collective-permute-start(bf16[64,640]{1,0:T(8,128)(2,1)S(1)} %get-tuple-element.7), channel_id=1, source_target_pairs={{0,24},{8,16},{16,8},{24,0},{1,25},{9,17},{17,9},{25,1},{2,26},{10... | collective-permute-start | bytes 245768 | tf_op jit(solution)/shard_map/ppermute | solution.py:90
  110.4 3.0 %collective-permute-done.11 = bf16[64,640]{1,0:T(8,128)(2,1)S(1)} collective-permute-done((bf16[64,640]{1,0:T(8,128)(2,1)S(1)}, bf16[64,640]{1,0:T(8,128)(2,1)S(1)}, u32[]{:S(2)}, u32[]{:S(2)}) %collective-permute-start.11) | collective-permute-done | bytes 81952 | tf_op jit(solution)/shard_map/ppermute | solution.py:90
  113.6 7.0 %collective-permute-done.12 = bf16[256,640]{1,0:T(8,128)(2,1)S(1)} collective-permute-done((bf16[256,640]{1,0:T(8,128)(2,1)S(1)}, bf16[256,640]{1,0:T(8,128)(2,1)S(1)}, u32[]{:S(2)}, u32[]{:S(2)}) %collective-permute-start.12) | collective-permute-done | bytes 327712 | tf_op jit(solution)/shard_map/ppermute | solution.py:78
  122.8 8.5 %collective-permute-done.13 = bf16[2,256,640]{2,1,0:T(8,128)(2,1)S(1)} collective-permute-done((bf16[2,256,640]{2,1,0:T(8,128)(2,1)S(1)}, bf16[2,256,640]{2,1,0:T(8,128)(2,1)S(1)}, u32[]{:S(2)}, u32[]{:S(2)}) %collective-permute-start.13) | collective-permute-done | bytes 655392 | tf_op jit(solution)/shard_map/ppermute | solution.py:78
  131.8 4.9 %fusion.12 = f32[1024,1024]{1,0:T(8,128)} fusion(bf16[2,1024,1152]{2,1,0:T(8,128)(2,1)} %bitcast.127, bf16[1024,512]{1,0:T(8,128)(2,1)S(1)} %bitcast.123, bf16[1024,512]{1,0:T(8,128)(2,1)S(1)} %collective-permute-done.26, pred[]{:T(512)S(6)} %eq.30), kind=kOutput, calls=%fused_computation.41 | convolution fusion | flops 1074266112 | bytes 7340033 | tf_op jit(solution)/shard_map/td,fd->tf/dot_general | solution.py:194
  136.7 2.2 %multiply_convert_fusion.4 = bf16[1024,512]{0,1:T(8,128)(2,1)S(1)} fusion(bf16[1024,1024]{1,0:T(8,128)(2,1)S(1)} %multiply_convert_fusion, f32[]{:T(128)} %bitcast.27, bf16[1024,512]{1,0:T(8,128)(2,1)S(1)} %collective-permute-done.26, bf16[1024,512]{1,0:T(8,128)(2,1)S(1)} %bitcast.124, pred[]{:T(512)S(6)} %eq.30), kind=kOutput, calls=%fused_computation.18 | convolution fusion | flops 1075314688 | bytes 5242885 | tf_op jit(solution)/shard_map/dot_general | solution.py:192
  140.9 2.2 %multiply_convert_fusion.1 = bf16[1024,640]{0,1:T(8,128)(2,1)S(1)} fusion(bf16[1024,1024]{1,0:T(8,128)(2,1)S(1)} %multiply_convert_fusion, f32[]{:T(128)} %bitcast.27, bf16[1024,640]{1,0:T(8,128)(2,1)S(1)} %collective-permute-done.14, bf16[1024,640]{1,0:T(8,128)(2,1)S(1)} %bitcast.144, pred[]{:T(512)S(6)} %eq.30), kind=kOutput, calls=%fused_computation.6 | convolution fusion | flops 1344143360 | bytes 6029317 | tf_op jit(solution)/shard_map/dot_general | solution.py:192
  143.1 2.2 %multiply_convert_fusion.2 = bf16[1024,640]{0,1:T(8,128)(2,1)S(1)} fusion(bf16[1024,1024]{1,0:T(8,128)(2,1)S(1)} %multiply_convert_fusion, f32[]{:T(128)} %bitcast.1, bf16[1024,640]{1,0:T(8,128)(2,1)S(1)} %bitcast.145, bf16[1024,640]{1,0:T(8,128)(2,1)S(1)} %collective-permute-done.14, pred[]{:T(512)S(6)} %eq.30), kind=kOutput, calls=%fused_computation.7 | convolution fusion | flops 1344143360 | bytes 6029317 | tf_op jit(solution)/shard_map/dot_general | solution.py:192
  145.9 2.6 %maximum_bitcast_fusion = bf16[1,2,1024,1152]{2,3,1,0:T(8,128)(2,1)} fusion(bf16[1,1024,1152]{1,2,0:T(8,128)(2,1)S(1)} %get-tuple-element.57, bf16[1,1024,1152]{1,2,0:T(8,128)(2,1)S(1)} %get-tuple-element.56), kind=kLoop, calls=%fused_computation | loop fusion | flops 2359296 | bytes 9437184 | tf_op jit(solution)/shard_map/broadcast_in_dim | solution.py:201
  148.5 6.7 %copy.10 = bf16[1,2,1024,1152]{3,2,1,0:T(8,128)(2,1)} copy(bf16[1,2,1024,1152]{2,3,1,0:T(8,128)(2,1)} %maximum_bitcast_fusion) | data formatting | bytes 9437184
  155.2 3.7 %fusion.6 = f32[1024,1024]{1,0:T(8,128)S(1)} fusion(bf16[2,1024,1152]{2,1,0:T(8,128)(2,1)} %bitcast.128, bf16[1024,640]{1,0:T(8,128)(2,1)} %copy-done.21, bf16[1024,640]{1,0:T(8,128)(2,1)} %bitcast.146, pred[]{:T(512)S(6)} %eq.30), kind=kOutput, calls=%fused_computation.26 | convolution fusion | flops 1342832640 | bytes 8126465 | tf_op jit(solution)/shard_map/td,fd->tf/dot_general | solution.py:194
  162.4 5.3 %fusion.30 = (f32[1024]{0:T(1024)}, bf16[1024,1024]{1,0:T(8,128)(2,1)}) fusion(s32[512,1024]{1,0:T(8,128)S(1)} %copy-done.6, s32[512,1024]{1,0:T(8,128)S(1)} %copy-done.4, bf16[2,1024,1152]{2,1,0:T(8,128)(2,1)S(1)} %bitcast.134, bf16[1024,512]{1,0:T(8,128)(2,1)S(1)} %collective-permute-done.26, bf16[1024,512]{1,0:T(8,128)(2,1)S(1)} %bitcast.126, ...), kind=kOutput, calls=%fused_computation.117 | convolution fusion | flops 1086848000 | bytes 22024200 | tf_op jit(solution)/shard_map/td,fd->tf/dot_general | solution.py:194
  167.8 6.0 %fusion = bf16[1,1152,1024]{2,1,0:T(8,128)(2,1)} fusion(bf16[1024,1024]{1,0:T(8,128)(2,1)} %get-tuple-element.55, bf16[256,1152]{1,0:T(8,128)(2,1)} %copy-done.20, bf16[256,1152]{1,0:T(8,128)(2,1)S(1)} %copy-done.19, bf16[256,1152]{1,0:T(8,128)(2,1)S(1)} %copy-done.17, bf16[256,1152]{1,0:T(8,128)(2,1)S(1)} %get-tuple-element.28), kind=kOutput, calls=%fused_computation.5 | convolution fusion | flops 2426535936 | bytes 6815744 | tf_op jit(solution)/shard_map/dot_general | solution.py:199
  (146 shorter events, 47.4 us)
Async XLA Ops:
  0.6 25.6 %copy-start = (bf16[1,1152,1024]{2,1,0:T(8,128)(2,1)S(1)}, bf16[1,1152,1024]{2,1,0:T(8,128)(2,1)}, u32[]{:S(2)}) copy-start(bf16[1,1152,1024]{2,1,0:T(8,128)(2,1)} %param.8) | copy-start | bytes 7077892
  0.6 16.7 %collective-permute-start.1 = (bf16[256,1152]{1,0:T(8,128)(2,1)}, bf16[256,1152]{1,0:T(8,128)(2,1)}, u32[]{:S(2)}, u32[]{:S(2)}) collective-permute-start(bf16[256,1152]{1,0:T(8,128)(2,1)} %bitcast.148), channel_id=1, source_target_pairs={{0,2},{1,3},{2,0},{3,1},{4,6},{5,7},{6,4},{7,5},{8,10},{9,11},{10,... | collective-permute-start | bytes 1769480 | tf_op jit(solution)/shard_map/ppermute | solution.py:69
  3.7 19.3 %collective-permute-start = (bf16[256,1152]{1,0:T(8,128)(2,1)}, bf16[256,1152]{1,0:T(8,128)(2,1)}, u32[]{:S(2)}, u32[]{:S(2)}) collective-permute-start(bf16[256,1152]{1,0:T(8,128)(2,1)} %bitcast.149), channel_id=1, source_target_pairs={{0,1},{1,0},{2,3},{3,2},{4,5},{5,4},{6,7},{7,6},{8,9},{9,8},{10,11... | collective-permute-start | bytes 1769480 | tf_op jit(solution)/shard_map/ppermute | solution.py:66
  17.3 7.2 %collective-permute-start.2 = (bf16[256,1152]{1,0:T(8,128)(2,1)}, bf16[256,1152]{1,0:T(8,128)(2,1)}, u32[]{:S(2)}, u32[]{:S(2)}) collective-permute-start(bf16[256,1152]{1,0:T(8,128)(2,1)} %collective-permute-done.1), channel_id=1, source_target_pairs={{0,1},{1,0},{2,3},{3,2},{4,5},{5,4},{6,7},{7,6},{8,9},{9,8},{10,11... | collective-permute-start | bytes 1769480 | tf_op jit(solution)/shard_map/ppermute | solution.py:66
  24.5 7.4 %copy-start.16 = (bf16[256,1152]{1,0:T(8,128)(2,1)}, bf16[256,1152]{1,0:T(8,128)(2,1)S(1)}, u32[]{:S(2)}) copy-start(bf16[256,1152]{1,0:T(8,128)(2,1)S(1)} %get-tuple-element.29) | copy-start | bytes 1769476
  36.1 5.0 %collective-permute-start.15 = (bf16[4,256,512]{2,1,0:T(8,128)(2,1)S(1)}, bf16[4,256,512]{2,1,0:T(8,128)(2,1)S(1)}, u32[]{:S(2)}, u32[]{:S(2)}) collective-permute-start(bf16[4,256,512]{2,1,0:T(8,128)(2,1)S(1)} %multiply_convert_fusion.6), channel_id=1, source_target_pairs={{0,1},{1,0},{2,3},{3,2},{4,5},{5,4},{6,7},{7,6},{8,9},{9,8},{10,11... | collective-permute-start | bytes 3145736 | tf_op jit(solution)/shard_map/ppermute | solution.py:66
  37.9 6.6 %collective-permute-start.3 = (bf16[4,256,640]{2,1,0:T(8,128)(2,1)S(1)}, bf16[4,256,640]{2,1,0:T(8,128)(2,1)S(1)}, u32[]{:S(2)}, u32[]{:S(2)}) collective-permute-start(bf16[4,256,640]{2,1,0:T(8,128)(2,1)S(1)} %multiply_convert_fusion.3), channel_id=1, source_target_pairs={{0,1},{1,0},{2,3},{3,2},{4,5},{5,4},{6,7},{7,6},{8,9},{9,8},{10,11... | collective-permute-start | bytes 3932168 | tf_op jit(solution)/shard_map/ppermute | solution.py:66
  42.5 9.2 %collective-permute-start.16 = (bf16[2,256,512]{2,1,0:T(8,128)(2,1)S(1)}, bf16[2,256,512]{2,1,0:T(8,128)(2,1)S(1)}, u32[]{:S(2)}, u32[]{:S(2)}) collective-permute-start(bf16[2,256,512]{2,1,0:T(8,128)(2,1)S(1)} %pad_maximum_fusion.5), channel_id=1, source_target_pairs={{0,2},{1,5},{2,0},{3,7},{4,6},{5,1},{6,4},{7,3},{8,10},{9,13},{10,... | collective-permute-start | bytes 1572872 | tf_op jit(solution)/shard_map/ppermute | solution.py:78
  51.9 9.0 %collective-permute-start.17 = (bf16[256,512]{1,0:T(8,128)(2,1)S(1)}, bf16[256,512]{1,0:T(8,128)(2,1)S(1)}, u32[]{:S(2)}, u32[]{:S(2)}) collective-permute-start(bf16[256,512]{1,0:T(8,128)(2,1)S(1)} %fusion.24), channel_id=1, source_target_pairs={{0,4},{1,3},{2,6},{3,1},{4,0},{5,7},{6,2},{7,5},{8,12},{9,11},{10,... | collective-permute-start | bytes 786440 | tf_op jit(solution)/shard_map/ppermute | solution.py:78
  54.0 22.7 %collective-permute-start.4 = (bf16[2,256,640]{2,1,0:T(8,128)(2,1)S(1)}, bf16[2,256,640]{2,1,0:T(8,128)(2,1)S(1)}, u32[]{:S(2)}, u32[]{:S(2)}) collective-permute-start(bf16[2,256,640]{2,1,0:T(8,128)(2,1)S(1)} %pad_maximum_fusion.3), channel_id=1, source_target_pairs={{0,2},{1,5},{2,0},{3,7},{4,6},{5,1},{6,4},{7,3},{8,10},{9,13},{10,... | collective-permute-start | bytes 1966088 | tf_op jit(solution)/shard_map/ppermute | solution.py:78
  61.1 4.8 %collective-permute-start.18 = (bf16[64,512]{1,0:T(8,128)(2,1)S(1)}, bf16[64,512]{1,0:T(8,128)(2,1)S(1)}, u32[]{:S(2)}, u32[]{:S(2)}) collective-permute-start(bf16[64,512]{1,0:T(8,128)(2,1)S(1)} %get-tuple-element.47), channel_id=1, source_target_pairs={{0,8},{8,0},{16,24},{24,16},{1,9},{9,1},{17,25},{25,17},{2,10},{10... | collective-permute-start | bytes 196616 | tf_op jit(solution)/shard_map/ppermute | solution.py:90
  63.1 6.4 %collective-permute-start.20 = (bf16[64,512]{1,0:T(8,128)(2,1)S(1)}, bf16[64,512]{1,0:T(8,128)(2,1)S(1)}, u32[]{:S(2)}, u32[]{:S(2)}) collective-permute-start(bf16[64,512]{1,0:T(8,128)(2,1)S(1)} %get-tuple-element.48), channel_id=1, source_target_pairs={{0,24},{8,16},{16,8},{24,0},{1,25},{9,17},{17,9},{25,1},{2,26},{10... | collective-permute-start | bytes 196616 | tf_op jit(solution)/shard_map/ppermute | solution.py:90
  65.6 6.6 %collective-permute-start.19 = (bf16[64,512]{1,0:T(8,128)(2,1)S(1)}, bf16[64,512]{1,0:T(8,128)(2,1)S(1)}, u32[]{:S(2)}, u32[]{:S(2)}) collective-permute-start(bf16[64,512]{1,0:T(8,128)(2,1)S(1)} %get-tuple-element.49), channel_id=1, source_target_pairs={{0,16},{8,24},{16,0},{24,8},{1,17},{9,25},{17,1},{25,9},{2,18},{10... | collective-permute-start | bytes 196616 | tf_op jit(solution)/shard_map/ppermute | solution.py:90
  72.3 6.4 %collective-permute-start.22 = (bf16[64,512]{1,0:T(8,128)(2,1)S(1)}, bf16[64,512]{1,0:T(8,128)(2,1)S(1)}, u32[]{:S(2)}, u32[]{:S(2)}) collective-permute-start(bf16[64,512]{1,0:T(8,128)(2,1)S(1)} %get-tuple-element.11), channel_id=1, source_target_pairs={{0,16},{8,24},{16,0},{24,8},{1,17},{9,25},{17,1},{25,9},{2,18},{10... | collective-permute-start | bytes 196616 | tf_op jit(solution)/shard_map/ppermute | solution.py:90
  72.4 6.2 %collective-permute-start.21 = (bf16[64,512]{1,0:T(8,128)(2,1)S(1)}, bf16[64,512]{1,0:T(8,128)(2,1)S(1)}, u32[]{:S(2)}, u32[]{:S(2)}) collective-permute-start(bf16[64,512]{1,0:T(8,128)(2,1)S(1)} %get-tuple-element.11), channel_id=1, source_target_pairs={{0,8},{8,0},{16,24},{24,16},{1,9},{9,1},{17,25},{25,17},{2,10},{10... | collective-permute-start | bytes 196616 | tf_op jit(solution)/shard_map/ppermute | solution.py:90
  75.8 6.1 %collective-permute-start.23 = (bf16[64,512]{1,0:T(8,128)(2,1)S(1)}, bf16[64,512]{1,0:T(8,128)(2,1)S(1)}, u32[]{:S(2)}, u32[]{:S(2)}) collective-permute-start(bf16[64,512]{1,0:T(8,128)(2,1)S(1)} %get-tuple-element.11), channel_id=1, source_target_pairs={{0,24},{8,16},{16,8},{24,0},{1,25},{9,17},{17,9},{25,1},{2,26},{10... | collective-permute-start | bytes 196616 | tf_op jit(solution)/shard_map/ppermute | solution.py:90
  81.9 7.1 %collective-permute-start.24 = (bf16[256,512]{1,0:T(8,128)(2,1)S(1)}, bf16[256,512]{1,0:T(8,128)(2,1)S(1)}, u32[]{:S(2)}, u32[]{:S(2)}) collective-permute-start(bf16[256,512]{1,0:T(8,128)(2,1)S(1)} %constant_dynamic-update-slice_fusion), channel_id=1, source_target_pairs={{0,4},{1,3},{2,6},{3,1},{4,0},{5,7},{6,2},{7,5},{8,12},{9,11},{10,... | collective-permute-start | bytes 786440 | tf_op jit(solution)/shard_map/ppermute | solution.py:78
  82.9 13.2 %collective-permute-start.5 = (bf16[256,640]{1,0:T(8,128)(2,1)S(1)}, bf16[256,640]{1,0:T(8,128)(2,1)S(1)}, u32[]{:S(2)}, u32[]{:S(2)}) collective-permute-start(bf16[256,640]{1,0:T(8,128)(2,1)S(1)} %fusion.21), channel_id=1, source_target_pairs={{0,4},{1,3},{2,6},{3,1},{4,0},{5,7},{6,2},{7,5},{8,12},{9,11},{10,... | collective-permute-start | bytes 983048 | tf_op jit(solution)/shard_map/ppermute | solution.py:78
  96.2 5.5 %collective-permute-start.6 = (bf16[64,640]{1,0:T(8,128)(2,1)S(1)}, bf16[64,640]{1,0:T(8,128)(2,1)S(1)}, u32[]{:S(2)}, u32[]{:S(2)}) collective-permute-start(bf16[64,640]{1,0:T(8,128)(2,1)S(1)} %get-tuple-element.44), channel_id=1, source_target_pairs={{0,8},{8,0},{16,24},{24,16},{1,9},{9,1},{17,25},{25,17},{2,10},{10... | collective-permute-start | bytes 245768 | tf_op jit(solution)/shard_map/ppermute | solution.py:90
  96.3 6.4 %collective-permute-start.8 = (bf16[64,640]{1,0:T(8,128)(2,1)S(1)}, bf16[64,640]{1,0:T(8,128)(2,1)S(1)}, u32[]{:S(2)}, u32[]{:S(2)}) collective-permute-start(bf16[64,640]{1,0:T(8,128)(2,1)S(1)} %get-tuple-element.45), channel_id=1, source_target_pairs={{0,24},{8,16},{16,8},{24,0},{1,25},{9,17},{17,9},{25,1},{2,26},{10... | collective-permute-start | bytes 245768 | tf_op jit(solution)/shard_map/ppermute | solution.py:90
  96.4 8.4 %collective-permute-start.7 = (bf16[64,640]{1,0:T(8,128)(2,1)S(1)}, bf16[64,640]{1,0:T(8,128)(2,1)S(1)}, u32[]{:S(2)}, u32[]{:S(2)}) collective-permute-start(bf16[64,640]{1,0:T(8,128)(2,1)S(1)} %get-tuple-element.46), channel_id=1, source_target_pairs={{0,16},{8,24},{16,0},{24,8},{1,17},{9,25},{17,1},{25,9},{2,18},{10... | collective-permute-start | bytes 245768 | tf_op jit(solution)/shard_map/ppermute | solution.py:90
  99.8 13.6 %collective-permute-start.25 = (bf16[2,256,512]{2,1,0:T(8,128)(2,1)S(1)}, bf16[2,256,512]{2,1,0:T(8,128)(2,1)S(1)}, u32[]{:S(2)}, u32[]{:S(2)}) collective-permute-start(bf16[2,256,512]{2,1,0:T(8,128)(2,1)S(1)} %pad_maximum_fusion.6), channel_id=1, source_target_pairs={{0,2},{1,5},{2,0},{3,7},{4,6},{5,1},{6,4},{7,3},{8,10},{9,13},{10,... | collective-permute-start | bytes 1572872 | tf_op jit(solution)/shard_map/ppermute | solution.py:78
  104.9 4.5 %collective-permute-start.9 = (bf16[64,640]{1,0:T(8,128)(2,1)S(1)}, bf16[64,640]{1,0:T(8,128)(2,1)S(1)}, u32[]{:S(2)}, u32[]{:S(2)}) collective-permute-start(bf16[64,640]{1,0:T(8,128)(2,1)S(1)} %get-tuple-element.7), channel_id=1, source_target_pairs={{0,8},{8,0},{16,24},{24,16},{1,9},{9,1},{17,25},{25,17},{2,10},{10... | collective-permute-start | bytes 245768 | tf_op jit(solution)/shard_map/ppermute | solution.py:90
  105.0 5.4 %collective-permute-start.10 = (bf16[64,640]{1,0:T(8,128)(2,1)S(1)}, bf16[64,640]{1,0:T(8,128)(2,1)S(1)}, u32[]{:S(2)}, u32[]{:S(2)}) collective-permute-start(bf16[64,640]{1,0:T(8,128)(2,1)S(1)} %get-tuple-element.7), channel_id=1, source_target_pairs={{0,16},{8,24},{16,0},{24,8},{1,17},{9,25},{17,1},{25,9},{2,18},{10... | collective-permute-start | bytes 245768 | tf_op jit(solution)/shard_map/ppermute | solution.py:90
  107.1 6.2 %collective-permute-start.11 = (bf16[64,640]{1,0:T(8,128)(2,1)S(1)}, bf16[64,640]{1,0:T(8,128)(2,1)S(1)}, u32[]{:S(2)}, u32[]{:S(2)}) collective-permute-start(bf16[64,640]{1,0:T(8,128)(2,1)S(1)} %get-tuple-element.7), channel_id=1, source_target_pairs={{0,24},{8,16},{16,8},{24,0},{1,25},{9,17},{17,9},{25,1},{2,26},{10... | collective-permute-start | bytes 245768 | tf_op jit(solution)/shard_map/ppermute | solution.py:90
  113.4 7.1 %collective-permute-start.12 = (bf16[256,640]{1,0:T(8,128)(2,1)S(1)}, bf16[256,640]{1,0:T(8,128)(2,1)S(1)}, u32[]{:S(2)}, u32[]{:S(2)}) collective-permute-start(bf16[256,640]{1,0:T(8,128)(2,1)S(1)} %constant_dynamic-update-slice_fusion.4), channel_id=1, source_target_pairs={{0,4},{1,3},{2,6},{3,1},{4,0},{5,7},{6,2},{7,5},{8,12},{9,11},{10,... | collective-permute-start | bytes 983048 | tf_op jit(solution)/shard_map/ppermute | solution.py:78
  120.7 10.7 %collective-permute-start.13 = (bf16[2,256,640]{2,1,0:T(8,128)(2,1)S(1)}, bf16[2,256,640]{2,1,0:T(8,128)(2,1)S(1)}, u32[]{:S(2)}, u32[]{:S(2)}) collective-permute-start(bf16[2,256,640]{2,1,0:T(8,128)(2,1)S(1)} %pad_maximum_fusion.4), channel_id=1, source_target_pairs={{0,2},{1,5},{2,0},{3,7},{4,6},{5,1},{6,4},{7,3},{8,10},{9,13},{10,... | collective-permute-start | bytes 1966088 | tf_op jit(solution)/shard_map/ppermute | solution.py:78
  122.7 9.1 %collective-permute-start.26 = (bf16[1024,512]{1,0:T(8,128)(2,1)S(1)}, bf16[1024,512]{1,0:T(8,128)(2,1)S(1)}, u32[]{:S(2)}, u32[]{:S(2)}) collective-permute-start(bf16[1024,512]{1,0:T(8,128)(2,1)S(1)} %bitcast.122), channel_id=1, source_target_pairs={{0,1},{1,0},{2,3},{3,2},{4,5},{5,4},{6,7},{7,6},{8,9},{9,8},{10,11... | collective-permute-start | bytes 3145736 | tf_op jit(solution)/shard_map/ppermute | solution.py:66
  131.7 11.4 %copy-start.14 = (bf16[4,256,640]{2,1,0:T(8,128)(2,1)}, bf16[4,256,640]{2,1,0:T(8,128)(2,1)S(1)}, u32[]{:S(2)}) copy-start(bf16[4,256,640]{2,1,0:T(8,128)(2,1)S(1)} %pad_maximum_fusion.1) | copy-start | bytes 3932164
  131.7 9.1 %collective-permute-start.14 = (bf16[1024,640]{1,0:T(8,128)(2,1)S(1)}, bf16[1024,640]{1,0:T(8,128)(2,1)S(1)}, u32[]{:S(2)}, u32[]{:S(2)}) collective-permute-start(bf16[1024,640]{1,0:T(8,128)(2,1)S(1)} %bitcast.143), channel_id=1, source_target_pairs={{0,1},{1,0},{2,3},{3,2},{4,5},{5,4},{6,7},{7,6},{8,9},{9,8},{10,11... | collective-permute-start | bytes 3932168 | tf_op jit(solution)/shard_map/ppermute | solution.py:66
  148.5 10.4 %slice-start.2 = ((s8[4718592]{0:T(1024)(128)(4,1)}), s8[524288]{0:T(1024)(128)(4,1)S(1)}, s32[]{:S(2)}) async-start(s8[4718592]{0:T(1024)(128)(4,1)} %bitcast.131), calls=%async_computation.2 | async-start | bytes 1048576
  167.8 6.0 %copy-start.1 = (bf16[1,1152,1024]{2,1,0:T(8,128)(2,1)S(1)}, bf16[1,1152,1024]{2,1,0:T(8,128)(2,1)}, u32[]{:S(2)}) copy-start(bf16[1,1152,1024]{2,1,0:T(8,128)(2,1)} %param.8) | copy-start | bytes 7077892
  (23 other events, 78.2 us)

commit v2 on v1

v2 whole, which is shorter than its diff:
```python
import math

import jax
import jax.numpy as jnp
from jax import lax
from jax.experimental import pallas as pl
from jax.experimental.pallas import tpu as pltpu
from jax.sharding import PartitionSpec as P

BF = jnp.bfloat16
F32 = jnp.float32


def plain_shards(entries, readin, offset, cutoff, writeout, hidden, depth):
    layer = lax.axis_index("layer")
    owner = jnp.logical_and(layer == 0, lax.axis_index("feat") == 0).astype(F32)
    gathered = lax.all_gather(entries, "tok", axis=1, tiled=True)[0]
    inverse = 1.0 / math.sqrt(gathered.shape[0])
    gate = cutoff[0].astype(F32)
    pre = jnp.dot(gathered, readin[0], preferred_element_type=F32) + offset[0][None, :]
    act = (pre * gate).astype(BF)
    live = (layer <= depth).astype(F32)
    targets = writeout.shape[1]
    partials = jnp.stack(
        [jnp.dot(act, writeout[0, t], preferred_element_type=F32) for t in range(targets)]
    )
    rows = hidden.shape[1]
    start = lax.axis_index("tok") * rows
    current = lax.dynamic_slice_in_dim(partials, start, rows, 1)
    partials = lax.dynamic_update_slice_in_dim(
        partials, current - owner * hidden.astype(F32), start, 1
    )
    summed = lax.psum_scatter(
        partials * live[:, None, None], ("feat", "tok"), scatter_dimension=1, tiled=True
    )
    summed = lax.psum(summed, "layer")
    scaled = lax.all_gather((summed * inverse).astype(BF), ("feat", "tok"), axis=1, tiled=True)
    dec = [
        (jnp.einsum("tf,td->fd", act, scaled[t], preferred_element_type=F32) * live[t]).astype(BF)
        for t in range(targets)
    ]
    sens = sum(
        live[t] * jnp.einsum("td,fd->tf", scaled[t], writeout[0, t], preferred_element_type=F32)
        for t in range(targets)
    )
    pre_grad = sens * gate
    enc = jnp.einsum("td,tf->df", gathered, pre_grad.astype(BF), preferred_element_type=F32)
    return enc.astype(BF)[None], jnp.stack(dec)[None], jnp.sum(pre_grad, axis=0)[None]


def column_chunks(width):
    for parts in (3, 2):
        if width % (128 * parts) == 0:
            unit = width // parts
            return [(0, width - unit), (width - unit, width)]
    return [(0, width)]


VMEM_MIB = 16
FEATURE_BLOCK = 256
ROWS_UNIT = 128
SIDE, CORE, FEAT, LAYER = range(4)
HELD = pl.BlockSpec(memory_space=pltpu.VMEM)
ANYWHERE = pl.BlockSpec(memory_space=pl.ANY)


def held(shape, dtype):
    return pltpu.VMEM(shape, dtype)


def array(shape, dtype):
    return jax.ShapeDtypeStruct(shape, dtype)


def block_of(features):
    return FEATURE_BLOCK if features % FEATURE_BLOCK == 0 else features


def span(number, size):
    return pl.ds(pl.multiple_of(number * size, size), size)


class Order:
    def __init__(self, scalars):
        self.scalars = scalars
        self.last = None

    def __call__(
        self, kernel, operands, outs, specs=None, out_specs=None, grid=(1,), scratch=(), aliases=()
    ):
        count = len(operands)
        operands = list(operands)
        specs = list(specs or [HELD] * count)
        waits = [] if self.last is None else [self.last]

        def body(*refs):
            at = len(self.scalars) + count
            kernel(*refs[:at], *refs[at + len(waits) :])

        results = pl.pallas_call(
            body,
            grid_spec=pltpu.PrefetchScalarGridSpec(
                num_scalar_prefetch=len(self.scalars),
                grid=grid,
                in_specs=specs + [ANYWHERE] * len(waits),
                out_specs=list(out_specs or [HELD] * len(outs)),
                scratch_shapes=list(scratch),
            ),
            out_shape=list(outs),
            input_output_aliases={len(self.scalars) + i: o for i, o in aliases},
            compiler_params=pltpu.CompilerParams(vmem_limit_bytes=VMEM_MIB * 1024 * 1024),
            cost_estimate=pl.CostEstimate(flops=1000, bytes_accessed=1000, transcendentals=0),
        )(*self.scalars, *operands, *waits)
        self.last = results[0]
        return results

    def pass_on(self, value):
        def kernel(*refs):
            pass

        last = self.last
        out = self(kernel, [value], [array(value.shape, value.dtype)], [ANYWHERE], [ANYWHERE],
                   aliases=[(0, 0)])[0]
        self.last = last
        return out


def load(order, *operands):
    parts = []
    for k, o in enumerate(operands):
        axis = max(range(o.ndim - 1), key=lambda i: o.shape[i])
        cuts = 4 if o.shape[axis] % 64 == 0 else 1
        size = o.shape[axis] // cuts
        for c in range(cuts):
            parts.append((k, (slice(None),) * axis + (pl.ds(c * size, size),)))

    def kernel(w, d, *refs):
        *refs, sems = refs
        n = len(operands)
        copies = [
            pltpu.make_async_copy(refs[k].at[at], refs[n + k].at[at], sems.at[i])
            for i, (k, at) in enumerate(parts)
        ]
        for copy in copies:
            copy.start()
        for copy in copies:
            copy.wait()

    return order(
        kernel,
        [pltpu.with_memory_space_constraint(o, pltpu.HBM) for o in operands],
        [held(o.shape, o.dtype) for o in operands],
        specs=[pl.BlockSpec(memory_space=pltpu.HBM)] * len(operands),
        scratch=[pltpu.SemaphoreType.DMA((len(parts),))],
    )


def encode(order, near, parts, readin, offset, cutoff):
    rows, width = parts[0].shape
    count = 2 * rows
    features = readin.shape[-1]
    block = block_of(features)

    def kernel(
        w, d, own_ref, other_ref, readin_ref, offset_ref, cutoff_ref, act_ref, turned_ref, tokens_ref
    ):
        i = pl.program_id(0)
        cols = span(i, block)
        first = w[SIDE] if near else 1 - w[SIDE]
        for ref, number in ((own_ref, w[CORE]), (other_ref, 1 - w[CORE])):
            at = span(number, rows)
            pre = jnp.dot(ref[...], readin_ref[0, :, cols], preferred_element_type=F32)
            gate = cutoff_ref[0, span(2 * first + number, rows), cols].astype(F32)
            act = ((pre + offset_ref[:, cols]) * gate).astype(BF)
            act_ref[at, cols] = act
            turned_ref[cols, at] = act.T

            @pl.when(i == 0)
            def _():
                tokens_ref[:, at] = ref[...].T

    return order(
        kernel,
        [*parts, readin, offset, cutoff],
        [held((count, features), BF), held((features, count), BF), held((width, count), BF)],
        grid=(features // block,),
    )


def decode(order, away, act, writeout, hidden, lo, hi, unit):
    count, features = act.shape
    dtype = BF if away else F32

    def kernel(w, d, act_ref, weight_ref, *rest):
        out_ref = rest[-1]
        target = 1 - w[CORE] if away else w[CORE]
        live = jnp.where(w[LAYER] <= d[target], 1.0, 0.0)
        owner = jnp.logical_and(w[LAYER] == 0, w[FEAT] == 0)
        for j in range(lo, hi, unit):
            cols, to = slice(j, j + unit), slice(j - lo, j - lo + unit)
            out = jnp.dot(act_ref[...], weight_ref[0, target, :, cols], preferred_element_type=F32)
            if hidden is None:
                out_ref[:, to] = (out * live).astype(dtype)
                continue
            less = rest[0][target, :, cols].astype(F32)
            rows = less.shape[0]
            for b in range(count // rows):
                mine = jnp.where(jnp.logical_and(owner, w[CORE] == b), 1.0, 0.0)
                part = out[b * rows : (b + 1) * rows] - mine * less
                out_ref[b * rows : (b + 1) * rows, to] = (part * live).astype(dtype)

    operands = [act, writeout] + ([] if hidden is None else [hidden])
    return order(kernel, operands, [held((count, hi - lo), dtype)])[0]


def gradients(order, scaled, turned, writeout, lo, hi, sens=None, dec=None, last=None):
    targets, features, width = writeout.shape[1:]
    total, columns = scaled[0].shape
    count = turned[0].shape[1]
    block = block_of(features)
    at = lo // columns

    def kernel(w, d, *refs):
        refs = list(refs)
        s_refs = [refs.pop(0) for _ in range(targets)]
        near_ref, far_ref, weight_ref = refs.pop(0), refs.pop(0), refs.pop(0)
        sens_in = refs.pop(0) if sens is not None else None
        if last is not None:
            cutoff_ref, token_refs = refs.pop(0), [refs.pop(0), refs.pop(0)]
        if dec is not None:
            refs.pop(0)
        dec_ref = refs.pop(0)
        cols = span(pl.program_id(0), block)
        numbers = [w[CORE], 1 - w[CORE]]
        live = [jnp.where(w[LAYER] <= d[n], 1.0, 0.0) for n in numbers]
        grads = [None, None]
        for half in range(2):
            rows = slice(half * count, (half + 1) * count)
            grad = 0.0 if sens_in is None else sens_in[rows, cols]
            for t in range(targets):
                grad = grad + live[t] * lax.dot_general(
                    s_refs[t][rows, :],
                    weight_ref[0, numbers[t], cols, lo:hi],
                    (((1,), (1,)), ((), ())),
                    preferred_element_type=F32,
                )
            grads[half] = grad
        if last is None:
            for half in range(2):
                refs[0][half * count : (half + 1) * count, cols] = grads[half]
        else:
            enc_ref, bias_ref = refs
            sides = [w[SIDE], 1 - w[SIDE]]
            grads = [
                g * cutoff_ref[0, span(s, count), cols].astype(F32) for g, s in zip(grads, sides)
            ]
            bias_ref[...] = sum(jnp.sum(g, axis=0, keepdims=True) for g in grads)
            enc_ref[0] = sum(
                jnp.dot(ref[...], g.astype(BF), preferred_element_type=F32)
                for ref, g in zip(token_refs, grads)
            ).astype(BF)
        for t in range(targets):
            out = jnp.dot(near_ref[cols, :], s_refs[t][:count, :], preferred_element_type=F32)
            out += jnp.dot(far_ref[cols, :], s_refs[t][count:, :], preferred_element_type=F32)
            dec_ref[0, numbers[t]] = (out * live[t]).astype(BF)

    operands = [*scaled, *turned, writeout]
    if sens is not None:
        operands.append(sens)
    if last is not None:
        operands += [last[0], *last[1]]
    specs = [HELD] * len(operands)
    aliases = []
    if dec is not None:
        aliases = [(len(operands), 0)]
        operands.append(dec)
        specs.append(ANYWHERE)
    out_specs = [pl.BlockSpec((1, targets, block, columns), lambda i, w, d: (0, 0, i, at))]
    outs = [array(writeout.shape, BF)]
    if last is not None:
        out_specs.append(pl.BlockSpec((1, width, block), lambda i, w, d: (0, 0, i)))
        out_specs.append(pl.BlockSpec((1, block), lambda i, w, d: (0, i)))
        outs += [array((1, width, features), BF), array((1, features), F32)]
    else:
        out_specs.append(HELD)
        outs.append(held((total, features), F32))
    results = order(
        kernel, operands, outs, specs, out_specs, grid=(features // block,), aliases=aliases
    )
    if last is None:
        order.last = results[1]
    return results


def paired_shards(sizes, entries, readin, offset, cutoff, writeout, hidden, depth):
    layers, feats, toks = sizes
    layer, feat, tok = (lax.axis_index(a) for a in ("layer", "feat", "tok"))
    where = jnp.stack([tok // 2, tok % 2, feat, layer]).astype(jnp.int32)
    order = Order((where, depth))

    def to_core(a):
        return lax.ppermute(a, "tok", [(t, t ^ 1) for t in range(toks)])

    def to_side(a):
        return lax.ppermute(a, "tok", [(t, t ^ 2) for t in range(toks)])

    def mixed(first):
        pairs = []
        for f in range(feats):
            for t in range(toks):
                over_side = (t % 2 == 0) == first
                goal = (f, t ^ 2) if over_side else (f ^ 1, t)
                pairs.append((f * toks + t, goal[0] * toks + goal[1]))
        return lambda a: lax.ppermute(a, ("feat", "tok"), pairs)

    to_first, to_second = mixed(True), mixed(False)
    binary = layers & (layers - 1) == 0

    def layer_goal(l, s):
        return l ^ s if binary else lax.rem(l + s, layers)

    def layer_source(l, s):
        return l ^ s if binary else lax.rem(l - s + layers, layers)

    def to_layer(a, s):
        return lax.ppermute(
            a, "layer", [(l, l ^ s if binary else (l + s) % layers) for l in range(layers)]
        )

    own = entries[0]
    rows, width = own.shape
    total = rows * toks
    inverse = 1.0 / math.sqrt(total)
    piece = rows // layers
    chunks = column_chunks(width)
    unit = chunks[-1][1] - chunks[-1][0]

    far = to_side(own)
    near = to_core(own)
    readin, cutoff, writeout, hidden = load(order, readin, cutoff, writeout, hidden)
    act, turned, tokens = encode(order, True, (own, near), readin, offset, cutoff)

    def partials(act, hidden, lo, hi):
        away = decode(order, True, act, writeout, hidden, lo, hi, unit)
        got = to_core(away)
        return decode(order, False, act, writeout, hidden, lo, hi, unit), got

    here = partials(act, hidden, 0, width)

    def first_kernel(w, d, kept, got, out):
        at = span(1 - w[FEAT], rows)
        out[...] = (kept[at, :] + got[at, :].astype(F32)).astype(BF)

    send = order(first_kernel, here, [held((rows, width), BF)])[0]
    got_first = to_first(send)

    far = order.pass_on(far)
    far_near = to_core(far)
    act, turned_far, tokens_far = encode(order, False, (far, far_near), readin, offset, cutoff)

    def reduce_sides(lo, hi):
        size = hi - lo
        there = partials(act, None, lo, hi)

        def second_kernel(w, d, hk, hg, tk, tg, first, out_first, out_second):
            at, other = span(w[FEAT], rows), span(1 - w[FEAT], rows)
            here_y = hk[at, lo:hi] + hg[at, lo:hi].astype(F32)
            there_other = tk[other, :] + tg[other, :].astype(F32)
            zero = w[CORE] == 0
            out_first[...] = jnp.where(zero, here_y, there_other).astype(BF)
            rest = jnp.where(zero, there_other, here_y) + first[:, lo:hi].astype(F32)
            out_second[...] = rest.astype(BF)

        sends = order(second_kernel, (*here, *there, got_first), [held((rows, size), BF)] * 2)
        return there, to_first(sends[0]), to_second(sends[1])

    def send_pieces(there, got, got_second):
        size = got.shape[1]

        def kernel(w, d, tk, tg, first, second, mine, *outs):
            *outs, kept = outs
            at = span(w[FEAT], rows)
            kept[...] = (
                tk[at, :]
                + tg[at, :].astype(F32)
                + first[...].astype(F32)
                + second[...].astype(F32)
            )
            mine[...] = kept[span(w[LAYER], piece), :]
            for s, out in enumerate(outs, 1):
                out[...] = kept[span(layer_goal(w[LAYER], s), piece), :].astype(BF)

        outs = [held((piece, size), F32)] + [held((piece, size), BF)] * (layers - 1)
        mine, *outs = order(
            kernel, (*there, got, got_second), outs, scratch=[pltpu.VMEM((rows, size), F32)]
        )
        return mine, [to_layer(out, s) for s, out in enumerate(outs, 1)]

    def scale_piece(mine, pieces):
        def kernel(w, d, mine_ref, *refs):
            *refs, out = refs
            value = mine_ref[...]
            for ref in refs:
                value = value + ref[...].astype(F32)
            out[...] = (value * inverse).astype(BF)

        scaled = order(kernel, (mine, *pieces), [held(mine.shape, BF)])[0]
        return scaled, [to_layer(scaled, s) for s in range(1, layers)]

    def join_pieces(scaled, pieces):
        def kernel(w, d, *refs):
            *refs, out = refs
            out[span(w[LAYER], piece), :] = refs[0][...]
            for s, ref in enumerate(refs[1:], 1):
                out[span(layer_source(w[LAYER], s), piece), :] = ref[...]

        done = order(kernel, (scaled, *pieces), [held((rows, scaled.shape[1]), BF)])[0]
        return done, to_second(done)

    def join_pair(done, got):
        def kernel(w, d, done_ref, got_ref, out):
            number = jnp.where(w[CORE] == 0, w[FEAT], 1)
            out[span(number, rows), :] = done_ref[...]
            out[span(1 - number, rows), :] = got_ref[...]

        pair = order(kernel, (done, got), [held((2 * rows, done.shape[1]), BF)])[0]
        return pair, to_first(pair)

    def join_all(pair, got):
        def kernel(w, d, pair_ref, got_ref, out):
            zero = w[CORE] == 0
            y = w[FEAT]
            for ref, numbers in (
                (pair_ref, (jnp.where(zero, 2, y), jnp.where(zero, 3, 2 + y))),
                (got_ref, (jnp.where(zero, 0, 1 - y), jnp.where(zero, 1, 3 - y))),
            ):
                for b, number in enumerate(numbers):
                    out[span(number, rows), :] = ref[b * rows : (b + 1) * rows, :]

        full = order(kernel, (pair, got), [held((total, pair.shape[1]), BF)])[0]
        return full, to_core(full)

    stages = [reduce_sides(lo, hi) for lo, hi in chunks]
    stages = [send_pieces(*stage) for stage in stages]
    stages = [scale_piece(*stage) for stage in stages]
    stages = [join_pair(*join_pieces(*stage)) for stage in stages]
    sens = dec = None
    for k, (lo, hi) in enumerate(chunks):
        last = (cutoff, (tokens, tokens_far)) if k == len(chunks) - 1 else None
        scaled = join_all(*stages[k])
        dec, *rest = gradients(
            order, scaled, (turned, turned_far), writeout, lo, hi, sens, dec, last
        )
        sens = rest[0]
    return rest[0], dec, rest[1]


def solution(mesh):
    sizes = tuple(mesh.shape[a] for a in ("layer", "feat", "tok"))

    def shards(*args):
        rows = args[0].shape[1]
        targets = args[4].shape[1]
        paired = sizes[1] == targets == 2 and sizes[2] == 4
        if paired and rows % ROWS_UNIT == 0 and rows % (16 * sizes[0]) == 0:
            return paired_shards(sizes, *args)
        return plain_shards(*args)

    return jax.shard_map(
        shards,
        mesh=mesh,
        in_specs=(
            P("layer", "tok", None),
            P("layer", None, ("feat", "tok")),
            P("layer", ("feat", "tok")),
            P("layer", None, ("feat", "tok")),
            P("layer", None, ("feat", "tok"), None),
            P(None, "tok", None),
            P(),
        ),
        out_specs=(
            P("layer", None, ("feat", "tok")),
            P("layer", None, ("feat", "tok"), None),
            P("layer", ("feat", "tok")),
        ),
        check_vma=False,
    )
```

time: 174 us -> 145 us (0.83)
  Pallas kernels: 0 us -> 55.1 us
  matrix products: 42 us -> 0 us
  local copies, waits for them, and re-layouts: 21 us -> 0.66 us
  other arithmetic: 15.5 us -> 0.08 us
  waiting for transfers between devices: 61.8 us -> 55.2 us
    pallas_call x0 -> x25, Pallas kernels: none -> 55.1 us  [__call__(): pl.pallas_call(body, grid_spec=pltpu.PrefetchScalarGridSpec(num_scalar_pr...]
    dot_general x14 -> x0, matrix products: 42 us -> none  [the longest x4 15.8 us: paired_shards(): jnp.einsum('td,fd->tf', scaled, weights[t, :, lo:hi], preferred_element_t...]
    ppermute x8 -> x9, waiting for transfers between devices: 38.8 us -> 23.5 us  [mixed(): return lambda a: lax.ppermute(a, ('feat', 'tok'), pairs)]
    unnamed x57 -> x6, local copies, waits for them, and re-layouts: 8.44 us -> 0.66 us
    slice x5 -> x0, local copies, waits for them, and re-layouts: 6.28 us -> none  [the longest x4 5.68 us: partial(): lax.dynamic_index_in_dim(mine_hidden, target, 0, keepdims=False)[:, lo:hi]]
    ppermute x1, waiting for transfers between devices: 4.66 us -> 10.5 us  [to_side(): return lax.ppermute(a, 'tok', [(t, t ^ 2) for t in range(toks)])]
    ppermute x6 -> x7, waiting for transfers between devices: 0.02 us -> 5.81 us  [to_core(): return lax.ppermute(a, 'tok', [(t, t ^ 1) for t in range(toks)])]
    squeeze x2 -> x0, local copies, waits for them, and re-layouts: 3.72 us -> none  [the longest x1 2.55 us: partial(): w = lax.dynamic_index_in_dim(weights, target, 0, keepdims=False)[:, lo:hi]]
  transfers between devices with their start and end apart: 27 -> 29, of which waited for: 16 -> 13; matrix products, arithmetic and copies ran while one was open for 19% -> 0% of each run, Pallas kernels for 0% -> 17%
where the time goes in v2:
time: 145 us
  waiting for transfers between devices  55.2 us (38%)
  Pallas kernels  55.1 us (38%)
  starting transfers between devices  33.2 us (23%)
    pallas_call x25, Pallas kernels, __call__(): pl.pallas_call(body, grid_spec=pltpu.PrefetchScalarGridSpec(num_scalar_pr...  55.1 us
    ppermute x9, waiting for transfers between devices, mixed(): return lambda a: lax.ppermute(a, ('feat', 'tok'), pairs)  23.5 us
    ppermute x12, starting transfers between devices, to_layer(): lax.ppermute(a, 'layer', [(l, l ^ s if binary else (l + s) % layers) for...  17.4 us
    ppermute x12, waiting for transfers between devices, to_layer(): lax.ppermute(a, 'layer', [(l, l ^ s if binary else (l + s) % layers) for...  15.4 us
    ppermute x9, starting transfers between devices, mixed(): return lambda a: lax.ppermute(a, ('feat', 'tok'), pairs)  11.4 us
    ppermute x1, waiting for transfers between devices, to_side(): return lax.ppermute(a, 'tok', [(t, t ^ 2) for t in range(toks)])  10.5 us
    ppermute x7, waiting for transfers between devices, to_core(): return lax.ppermute(a, 'tok', [(t, t ^ 1) for t in range(toks)])  5.81 us
    ppermute x1, starting transfers between devices, to_side(): return lax.ppermute(a, 'tok', [(t, t ^ 2) for t in range(toks)])  2.94 us
  transfers between devices with their start and end apart: 29, of which 13 were waited for; matrix products, arithmetic and copies ran while one was open for 0% of the time, Pallas kernels for 17%

profile of v2, /device:TPU:0, one launch (start us, length us, event | category | flops | bytes accessed | tf_op | source)
XLA Modules:
  0.0 145.2 jit_solution(10792151538930239835)
XLA Ops:
  1.9 5.3 %shard_map.94 = (bf16[1,1152,1024]{2,1,0:T(8,128)(2,1)S(1)}, s32[1,1024,1024]{2,1,0:T(8,128)S(1)}, bf16[1,2,1024,1152]{3,2,1,0:T(8,128)(2,1)S(1)}, bf16[2,256,1152]{2,1,0:T(8,128)(2,1)S(1)}) custom-call(s32[4]{0:T(128)S(1)} %pad_add_fusion.refs_0_, s32[2]{0:T(128)S(1)} %copy-done.1, bf16[1,1152,1024]{2,1,0:T(8,128)(2,1)} %refs_2_.1, ...), custom_call_target="tpu_custom_call" | custom-call | flops 1000 | bytes 1000 | tf_op jit(solution)/shard_map/pallas_call | solution.py:100
  7.2 5.4 %shard_map.95 = (bf16[512,1024]{1,0:T(8,128)(2,1)S(1)}, bf16[1024,512]{1,0:T(8,128)(2,1)S(1)}, bf16[1152,512]{1,0:T(8,128)(2,1)S(1)}) custom-call(s32[4]{0:T(128)S(1)} %pad_add_fusion.refs_0_, s32[2]{0:T(128)S(1)} %copy-done.1, bf16[256,1152]{1,0:T(8,128)(2,1)S(1)} %bitcast.6, bf16[256,1152]{1,0:T(8,128)(2,1)S(1)} %collective-permute-done.1.refs_3_, ...), custom_call_target="tpu_custom_call" | custom-call | flops 1000 | bytes 1000 | tf_op jit(solution)/shard_map/pallas_call | solution.py:100
  12.6 2.3 %shard_map.96.refs_5_ = bf16[512,1152]{1,0:T(8,128)(2,1)S(1)} custom-call(s32[4]{0:T(128)S(1)} %pad_add_fusion.refs_0_, s32[2]{0:T(128)S(1)} %copy-done.1, bf16[512,1024]{1,0:T(8,128)(2,1)S(1)} %get-tuple-element.32.refs_2_.refs_5_, bf16[1,2,1024,1152]{3,2,1,0:T(8,128)(2,1)S(1)} %get-tuple-element.33.refs_3_.refs_6_, ...), custom_call_target="tpu_custom_call" | custom-call | flops 1000 | bytes 1000 | tf_op jit(solution)/shard_map/pallas_call | solution.py:100
  15.1 2.9 %collective-permute-start = (bf16[256,1152]{1,0:T(8,128)(2,1)S(1)}, bf16[256,1152]{1,0:T(8,128)(2,1)S(1)}, u32[]{:S(2)}, u32[]{:S(2)}) collective-permute-start(bf16[256,1152]{1,0:T(8,128)(2,1)S(1)} %bitcast.7), channel_id=1, source_target_pairs={{0,2},{1,3},{2,0},{3,1},{4,6},{5,7},{6,4},{7,5},{8,10},{9,11},{10,... | collective-permute-start | bytes 1769480 | tf_op jit(solution)/shard_map/ppermute | solution.py:305
  18.0 2.3 %shard_map.97.refs_2_.refs_4_ = f32[512,1152]{1,0:T(8,128)S(1)} custom-call(s32[4]{0:T(128)S(1)} %pad_add_fusion.refs_0_, s32[2]{0:T(128)S(1)} %copy-done.1, bf16[512,1024]{1,0:T(8,128)(2,1)S(1)} %get-tuple-element.32.refs_2_.refs_5_, bf16[1,2,1024,1152]{3,2,1,0:T(8,128)(2,1)S(1)} %get-tuple-element.33.refs_3_.refs_6_, ...), custom_call_target="tpu_custom_call" | custom-call | flops 1000 | bytes 1000 | tf_op jit(solution)/shard_map/pallas_call | solution.py:100
  21.1 10.5 %collective-permute-done.refs_2_ = bf16[256,1152]{1,0:T(8,128)(2,1)S(1)} collective-permute-done((bf16[256,1152]{1,0:T(8,128)(2,1)S(1)}, bf16[256,1152]{1,0:T(8,128)(2,1)S(1)}, u32[]{:S(2)}, u32[]{:S(2)}) %collective-permute-start) | collective-permute-done | bytes 589856 | tf_op jit(solution)/shard_map/ppermute | solution.py:305
  32.2 2.0 %collective-permute-done.3.refs_3_ = bf16[256,1152]{1,0:T(8,128)(2,1)S(1)} collective-permute-done((bf16[256,1152]{1,0:T(8,128)(2,1)S(1)}, bf16[256,1152]{1,0:T(8,128)(2,1)S(1)}, u32[]{:S(2)}, u32[]{:S(2)}) %collective-permute-start.3) | collective-permute-done | bytes 589856 | tf_op jit(solution)/shard_map/ppermute | solution.py:302
  34.2 5.4 %shard_map.100 = (bf16[512,1024]{1,0:T(8,128)(2,1)S(1)}, bf16[1024,512]{1,0:T(8,128)(2,1)S(1)}, bf16[1152,512]{1,0:T(8,128)(2,1)S(1)}) custom-call(s32[4]{0:T(128)S(1)} %pad_add_fusion.refs_0_, s32[2]{0:T(128)S(1)} %copy-done.1, bf16[256,1152]{1,0:T(8,128)(2,1)S(1)} %shard_map.99.refs_2_, bf16[256,1152]{1,0:T(8,128)(2,1)S(1)} %collective-permute-done.3.refs_3_, ...), custom_call_target="tpu_custom_call" | custom-call | flops 1000 | bytes 1000 | tf_op jit(solution)/shard_map/pallas_call | solution.py:100
  39.6 1.8 %shard_map.101.refs_4_ = bf16[512,768]{1,0:T(8,128)(2,1)S(1)} custom-call(s32[4]{0:T(128)S(1)} %pad_add_fusion.refs_0_, s32[2]{0:T(128)S(1)} %copy-done.1, bf16[512,1024]{1,0:T(8,128)(2,1)S(1)} %get-tuple-element.35.refs_2_.refs_4_, bf16[1,2,1024,1152]{3,2,1,0:T(8,128)(2,1)S(1)} %get-tuple-element.33.refs_3_.refs_6_, ...), custom_call_target="tpu_custom_call" | custom-call | flops 1000 | bytes 1000 | tf_op jit(solution)/shard_map/pallas_call | solution.py:100
  41.6 1.7 %collective-permute-start.5 = (bf16[256,1152]{1,0:T(8,128)(2,1)S(1)}, bf16[256,1152]{1,0:T(8,128)(2,1)S(1)}, u32[]{:S(2)}, u32[]{:S(2)}) collective-permute-start(bf16[256,1152]{1,0:T(8,128)(2,1)S(1)} %shard_map.98.refs_3_.refs_7_), channel_id=1, source_target_pairs={{0,2},{1,5},{2,0},{3,7},{4,6},{5,1},{6,4},{7,3},{8,10},{9,13},{10,... | collective-permute-start | bytes 1769480 | tf_op jit(solution)/shard_map/ppermute | solution.py:314
  43.4 1.8 %shard_map.102.refs_4_.refs_7_.refs_2_ = f32[512,768]{1,0:T(8,128)S(1)} custom-call(s32[4]{0:T(128)S(1)} %pad_add_fusion.refs_0_, s32[2]{0:T(128)S(1)} %copy-done.1, bf16[512,1024]{1,0:T(8,128)(2,1)S(1)} %get-tuple-element.35.refs_2_.refs_4_, bf16[1,2,1024,1152]{3,2,1,0:T(8,128)(2,1)S(1)} %get-tuple-element.33.refs_3_.refs_6_, ...), custom_call_target="tpu_custom_call" | custom-call | flops 1000 | bytes 1000 | tf_op jit(solution)/shard_map/pallas_call | solution.py:100
  45.2 6.3 %collective-permute-done.5.refs_6_ = bf16[256,1152]{1,0:T(8,128)(2,1)S(1)} collective-permute-done((bf16[256,1152]{1,0:T(8,128)(2,1)S(1)}, bf16[256,1152]{1,0:T(8,128)(2,1)S(1)}, u32[]{:S(2)}, u32[]{:S(2)}) %collective-permute-start.5) | collective-permute-done | bytes 589856 | tf_op jit(solution)/shard_map/ppermute | solution.py:314
  53.7 1.8 %collective-permute-start.10 = (bf16[256,768]{1,0:T(8,128)(2,1)S(1)}, bf16[256,768]{1,0:T(8,128)(2,1)S(1)}, u32[]{:S(2)}, u32[]{:S(2)}) collective-permute-start(bf16[256,768]{1,0:T(8,128)(2,1)S(1)} %get-tuple-element.39), channel_id=1, source_target_pairs={{0,4},{1,3},{2,6},{3,1},{4,0},{5,7},{6,2},{7,5},{8,12},{9,11},{10,... | collective-permute-start | bytes 1179656 | tf_op jit(solution)/shard_map/ppermute | solution.py:314
  59.8 5.0 %collective-permute-done.10.refs_5_ = bf16[256,768]{1,0:T(8,128)(2,1)S(1)} collective-permute-done((bf16[256,768]{1,0:T(8,128)(2,1)S(1)}, bf16[256,768]{1,0:T(8,128)(2,1)S(1)}, u32[]{:S(2)}, u32[]{:S(2)}) %collective-permute-start.10) | collective-permute-done | bytes 393248 | tf_op jit(solution)/shard_map/ppermute | solution.py:314
  64.8 2.5 %collective-permute-done.9.refs_4_ = bf16[256,768]{1,0:T(8,128)(2,1)S(1)} collective-permute-done((bf16[256,768]{1,0:T(8,128)(2,1)S(1)}, bf16[256,768]{1,0:T(8,128)(2,1)S(1)}, u32[]{:S(2)}, u32[]{:S(2)}) %collective-permute-start.9) | collective-permute-done | bytes 393248 | tf_op jit(solution)/shard_map/ppermute | solution.py:314
  68.2 1.9 %collective-permute-start.14 = (bf16[64,768]{1,0:T(8,128)(2,1)S(1)}, bf16[64,768]{1,0:T(8,128)(2,1)S(1)}, u32[]{:S(2)}, u32[]{:S(2)}) collective-permute-start(bf16[64,768]{1,0:T(8,128)(2,1)S(1)} %get-tuple-element.45), channel_id=1, source_target_pairs={{0,8},{8,0},{16,24},{24,16},{1,9},{9,1},{17,25},{25,17},{2,10},{10... | collective-permute-start | bytes 294920 | tf_op jit(solution)/shard_map/ppermute | solution.py:326
  70.1 2.6 %collective-permute-start.15 = (bf16[64,768]{1,0:T(8,128)(2,1)S(1)}, bf16[64,768]{1,0:T(8,128)(2,1)S(1)}, u32[]{:S(2)}, u32[]{:S(2)}) collective-permute-start(bf16[64,768]{1,0:T(8,128)(2,1)S(1)} %get-tuple-element.46), channel_id=1, source_target_pairs={{0,16},{8,24},{16,0},{24,8},{1,17},{9,25},{17,1},{25,9},{2,18},{10... | collective-permute-start | bytes 294920 | tf_op jit(solution)/shard_map/ppermute | solution.py:326
  74.3 5.5 %collective-permute-done.15.refs_4_ = bf16[64,768]{1,0:T(8,128)(2,1)S(1)} collective-permute-done((bf16[64,768]{1,0:T(8,128)(2,1)S(1)}, bf16[64,768]{1,0:T(8,128)(2,1)S(1)}, u32[]{:S(2)}, u32[]{:S(2)}) %collective-permute-start.15) | collective-permute-done | bytes 98336 | tf_op jit(solution)/shard_map/ppermute | solution.py:326
  80.4 2.6 %collective-permute-start.22 = (bf16[64,768]{1,0:T(8,128)(2,1)S(1)}, bf16[64,768]{1,0:T(8,128)(2,1)S(1)}, u32[]{:S(2)}, u32[]{:S(2)}) collective-permute-start(bf16[64,768]{1,0:T(8,128)(2,1)S(1)} %shard_map.109.refs_6_.refs_2_), channel_id=1, source_target_pairs={{0,24},{8,16},{16,8},{24,0},{1,25},{9,17},{17,9},{25,1},{2,26},{10... | collective-permute-start | bytes 294920 | tf_op jit(solution)/shard_map/ppermute | solution.py:326
  84.9 1.7 %collective-permute-start.12 = (bf16[64,384]{1,0:T(8,128)(2,1)S(1)}, bf16[64,384]{1,0:T(8,128)(2,1)S(1)}, u32[]{:S(2)}, u32[]{:S(2)}) collective-permute-start(bf16[64,384]{1,0:T(8,128)(2,1)S(1)} %get-tuple-element.43), channel_id=1, source_target_pairs={{0,16},{8,24},{16,0},{24,8},{1,17},{9,25},{17,1},{25,9},{2,18},{10... | collective-permute-start | bytes 147464 | tf_op jit(solution)/shard_map/ppermute | solution.py:326
  88.0 6.8 %collective-permute-done.12.refs_4_ = bf16[64,384]{1,0:T(8,128)(2,1)S(1)} collective-permute-done((bf16[64,384]{1,0:T(8,128)(2,1)S(1)}, bf16[64,384]{1,0:T(8,128)(2,1)S(1)}, u32[]{:S(2)}, u32[]{:S(2)}) %collective-permute-start.12) | collective-permute-done | bytes 49184 | tf_op jit(solution)/shard_map/ppermute | solution.py:326
  95.9 2.1 %collective-permute-start.23 = (bf16[256,768]{1,0:T(8,128)(2,1)S(1)}, bf16[256,768]{1,0:T(8,128)(2,1)S(1)}, u32[]{:S(2)}, u32[]{:S(2)}) collective-permute-start(bf16[256,768]{1,0:T(8,128)(2,1)S(1)} %shard_map.111.refs_2_.refs_4_), channel_id=1, source_target_pairs={{0,4},{1,3},{2,6},{3,1},{4,0},{5,7},{6,2},{7,5},{8,12},{9,11},{10,... | collective-permute-start | bytes 1179656 | tf_op jit(solution)/shard_map/ppermute | solution.py:314
  98.0 5.8 %collective-permute-done.23.refs_3_ = bf16[256,768]{1,0:T(8,128)(2,1)S(1)} collective-permute-done((bf16[256,768]{1,0:T(8,128)(2,1)S(1)}, bf16[256,768]{1,0:T(8,128)(2,1)S(1)}, u32[]{:S(2)}, u32[]{:S(2)}) %collective-permute-start.23) | collective-permute-done | bytes 393248 | tf_op jit(solution)/shard_map/ppermute | solution.py:314
  104.5 1.7 %collective-permute-start.19 = (bf16[64,384]{1,0:T(8,128)(2,1)S(1)}, bf16[64,384]{1,0:T(8,128)(2,1)S(1)}, u32[]{:S(2)}, u32[]{:S(2)}) collective-permute-start(bf16[64,384]{1,0:T(8,128)(2,1)S(1)} %shard_map.110.refs_6_.refs_2_), channel_id=1, source_target_pairs={{0,24},{8,16},{16,8},{24,0},{1,25},{9,17},{17,9},{25,1},{2,26},{10... | collective-permute-start | bytes 147464 | tf_op jit(solution)/shard_map/ppermute | solution.py:326
  107.1 1.8 %collective-permute-start.17 = (bf16[64,384]{1,0:T(8,128)(2,1)S(1)}, bf16[64,384]{1,0:T(8,128)(2,1)S(1)}, u32[]{:S(2)}, u32[]{:S(2)}) collective-permute-start(bf16[64,384]{1,0:T(8,128)(2,1)S(1)} %shard_map.110.refs_6_.refs_2_), channel_id=1, source_target_pairs={{0,8},{8,0},{16,24},{24,16},{1,9},{9,1},{17,25},{25,17},{2,10},{10... | collective-permute-start | bytes 147464 | tf_op jit(solution)/shard_map/ppermute | solution.py:326
  108.9 1.9 %collective-permute-done.19.refs_5_ = bf16[64,384]{1,0:T(8,128)(2,1)S(1)} collective-permute-done((bf16[64,384]{1,0:T(8,128)(2,1)S(1)}, bf16[64,384]{1,0:T(8,128)(2,1)S(1)}, u32[]{:S(2)}, u32[]{:S(2)}) %collective-permute-start.19) | collective-permute-done | bytes 49184 | tf_op jit(solution)/shard_map/ppermute | solution.py:326
  112.6 1.8 %collective-permute-start.24 = (bf16[256,384]{1,0:T(8,128)(2,1)S(1)}, bf16[256,384]{1,0:T(8,128)(2,1)S(1)}, u32[]{:S(2)}, u32[]{:S(2)}) collective-permute-start(bf16[256,384]{1,0:T(8,128)(2,1)S(1)} %shard_map.113.refs_2_.refs_4_), channel_id=1, source_target_pairs={{0,4},{1,3},{2,6},{3,1},{4,0},{5,7},{6,2},{7,5},{8,12},{9,11},{10,... | collective-permute-start | bytes 589832 | tf_op jit(solution)/shard_map/ppermute | solution.py:314
  114.3 4.0 %collective-permute-done.24.refs_3_ = bf16[256,384]{1,0:T(8,128)(2,1)S(1)} collective-permute-done((bf16[256,384]{1,0:T(8,128)(2,1)S(1)}, bf16[256,384]{1,0:T(8,128)(2,1)S(1)}, u32[]{:S(2)}, u32[]{:S(2)}) %collective-permute-start.24) | collective-permute-done | bytes 196640 | tf_op jit(solution)/shard_map/ppermute | solution.py:314
  121.4 1.7 %collective-permute-done.27.refs_3_ = bf16[1024,768]{1,0:T(8,128)(2,1)S(1)} collective-permute-done((bf16[1024,768]{1,0:T(8,128)(2,1)S(1)}, bf16[1024,768]{1,0:T(8,128)(2,1)S(1)}, u32[]{:S(2)}, u32[]{:S(2)}) %collective-permute-start.27) | collective-permute-done | bytes 1572896 | tf_op jit(solution)/shard_map/ppermute | solution.py:302
  123.0 8.8 %shard_map.116 = (bf16[1,2,1024,1152]{3,2,1,0:T(8,128)(2,1)}, f32[1024,1024]{1,0:T(8,128)S(1)}) custom-call(s32[4]{0:T(128)S(1)} %pad_add_fusion.refs_0_, s32[2]{0:T(128)S(1)} %copy-done.1, bf16[1024,768]{1,0:T(8,128)(2,1)S(1)} %shard_map.115.refs_2_.refs_7_, bf16[1024,768]{1,0:T(8,128)(2,1)S(1)} %collective-permute-done.27.refs_3_, ...), custom_call_target="tpu_custom_call" | custom-call | flops 1000 | bytes 1000 | tf_op jit(solution)/shard_map/pallas_call | solution.py:100
  132.7 2.1 %collective-permute-done.28.refs_3_ = bf16[1024,384]{1,0:T(8,128)(2,1)S(1)} collective-permute-done((bf16[1024,384]{1,0:T(8,128)(2,1)S(1)}, bf16[1024,384]{1,0:T(8,128)(2,1)S(1)}, u32[]{:S(2)}, u32[]{:S(2)}) %collective-permute-start.28) | collective-permute-done | bytes 786464 | tf_op jit(solution)/shard_map/ppermute | solution.py:302
  134.8 10.3 %shard_map.118 = (bf16[1,2,1024,1152]{3,2,1,0:T(8,128)(2,1)}, bf16[1,1152,1024]{2,1,0:T(8,128)(2,1)}, f32[1,1024]{1,0:T(1,128)}) custom-call(s32[4]{0:T(128)S(1)} %pad_add_fusion.refs_0_, s32[2]{0:T(128)S(1)} %copy-done.1, bf16[1024,384]{1,0:T(8,128)(2,1)S(1)} %shard_map.117.refs_2_.refs_12_, ...), custom_call_target="tpu_custom_call", output_to_operand_aliasing={{0}: (11, {})} | custom-call | flops 1000 | bytes 1000 | tf_op jit(solution)/shard_map/pallas_call | solution.py:100
  (58 shorter events, 24.1 us)
Async XLA Ops:
  0.6 6.6 %collective-permute-start.1 = (bf16[256,1152]{1,0:T(8,128)(2,1)}, bf16[256,1152]{1,0:T(8,128)(2,1)S(1)}, u32[]{:S(2)}, u32[]{:S(2)}) collective-permute-start(bf16[256,1152]{1,0:T(8,128)(2,1)} %bitcast.5), channel_id=1, source_target_pairs={{0,1},{1,0},{2,3},{3,2},{4,5},{5,4},{6,7},{7,6},{8,9},{9,8},{10,11... | collective-permute-start | bytes 1769480 | tf_op jit(solution)/shard_map/ppermute | solution.py:302
  1.2 0.7 copy-start.1
  1.9 5.3 %copy-start = (bf16[1,256,1152]{2,1,0:T(8,128)(2,1)S(1)}, bf16[1,256,1152]{2,1,0:T(8,128)(2,1)}, u32[]{:S(2)}) copy-start(bf16[1,256,1152]{2,1,0:T(8,128)(2,1)} %param.7) | copy-start | bytes 1769476
  1.9 5.3 %copy-start.2 = (f32[1,1024]{1,0:T(1,128)S(1)}, f32[1,1024]{1,0:T(1,128)}, u32[]{:S(2)}) copy-start(f32[1,1024]{1,0:T(1,128)} %refs_5_.5) | copy-start | bytes 12292
  15.0 5.4 %collective-permute-start.2 = (bf16[512,1152]{1,0:T(8,128)(2,1)S(1)}, bf16[512,1152]{1,0:T(8,128)(2,1)S(1)}, u32[]{:S(2)}, u32[]{:S(2)}) collective-permute-start(bf16[512,1152]{1,0:T(8,128)(2,1)S(1)} %shard_map.96.refs_5_), channel_id=1, source_target_pairs={{0,1},{1,0},{2,3},{3,2},{4,5},{5,4},{6,7},{7,6},{8,9},{9,8},{10,11... | collective-permute-start | bytes 3538952 | tf_op jit(solution)/shard_map/ppermute | solution.py:302
  15.1 16.5 %collective-permute-start = (bf16[256,1152]{1,0:T(8,128)(2,1)S(1)}, bf16[256,1152]{1,0:T(8,128)(2,1)S(1)}, u32[]{:S(2)}, u32[]{:S(2)}) collective-permute-start(bf16[256,1152]{1,0:T(8,128)(2,1)S(1)} %bitcast.7), channel_id=1, source_target_pairs={{0,2},{1,3},{2,0},{3,1},{4,6},{5,7},{6,4},{7,5},{8,10},{9,11},{10,... | collective-permute-start | bytes 1769480 | tf_op jit(solution)/shard_map/ppermute | solution.py:305
  32.1 2.1 %collective-permute-start.3 = (bf16[256,1152]{1,0:T(8,128)(2,1)S(1)}, bf16[256,1152]{1,0:T(8,128)(2,1)S(1)}, u32[]{:S(2)}, u32[]{:S(2)}) collective-permute-start(bf16[256,1152]{1,0:T(8,128)(2,1)S(1)} %shard_map.99.refs_2_), channel_id=1, source_target_pairs={{0,1},{1,0},{2,3},{3,2},{4,5},{5,4},{6,7},{7,6},{8,9},{9,8},{10,11... | collective-permute-start | bytes 1769480 | tf_op jit(solution)/shard_map/ppermute | solution.py:302
  41.4 10.1 %collective-permute-start.4 = (bf16[512,768]{1,0:T(8,128)(2,1)S(1)}, bf16[512,768]{1,0:T(8,128)(2,1)S(1)}, u32[]{:S(2)}, u32[]{:S(2)}) collective-permute-start(bf16[512,768]{1,0:T(8,128)(2,1)S(1)} %shard_map.101.refs_4_), channel_id=1, source_target_pairs={{0,1},{1,0},{2,3},{3,2},{4,5},{5,4},{6,7},{7,6},{8,9},{9,8},{10,11... | collective-permute-start | bytes 2359304 | tf_op jit(solution)/shard_map/ppermute | solution.py:302
  41.6 9.9 %collective-permute-start.5 = (bf16[256,1152]{1,0:T(8,128)(2,1)S(1)}, bf16[256,1152]{1,0:T(8,128)(2,1)S(1)}, u32[]{:S(2)}, u32[]{:S(2)}) collective-permute-start(bf16[256,1152]{1,0:T(8,128)(2,1)S(1)} %shard_map.98.refs_3_.refs_7_), channel_id=1, source_target_pairs={{0,2},{1,5},{2,0},{3,7},{4,6},{5,1},{6,4},{7,3},{8,10},{9,13},{10,... | collective-permute-start | bytes 1769480 | tf_op jit(solution)/shard_map/ppermute | solution.py:314
  53.6 4.7 %collective-permute-start.6 = (bf16[512,384]{1,0:T(8,128)(2,1)S(1)}, bf16[512,384]{1,0:T(8,128)(2,1)S(1)}, u32[]{:S(2)}, u32[]{:S(2)}) collective-permute-start(bf16[512,384]{1,0:T(8,128)(2,1)S(1)} %shard_map.104.refs_4_), channel_id=1, source_target_pairs={{0,1},{1,0},{2,3},{3,2},{4,5},{5,4},{6,7},{7,6},{8,9},{9,8},{10,11... | collective-permute-start | bytes 1179656 | tf_op jit(solution)/shard_map/ppermute | solution.py:302
  53.7 11.1 %collective-permute-start.10 = (bf16[256,768]{1,0:T(8,128)(2,1)S(1)}, bf16[256,768]{1,0:T(8,128)(2,1)S(1)}, u32[]{:S(2)}, u32[]{:S(2)}) collective-permute-start(bf16[256,768]{1,0:T(8,128)(2,1)S(1)} %get-tuple-element.39), channel_id=1, source_target_pairs={{0,4},{1,3},{2,6},{3,1},{4,0},{5,7},{6,2},{7,5},{8,12},{9,11},{10,... | collective-permute-start | bytes 1179656 | tf_op jit(solution)/shard_map/ppermute | solution.py:314
  55.5 11.8 %collective-permute-start.9 = (bf16[256,768]{1,0:T(8,128)(2,1)S(1)}, bf16[256,768]{1,0:T(8,128)(2,1)S(1)}, u32[]{:S(2)}, u32[]{:S(2)}) collective-permute-start(bf16[256,768]{1,0:T(8,128)(2,1)S(1)} %get-tuple-element.36.refs_4_), channel_id=1, source_target_pairs={{0,2},{1,5},{2,0},{3,7},{4,6},{5,1},{6,4},{7,3},{8,10},{9,13},{10,... | collective-permute-start | bytes 1179656 | tf_op jit(solution)/shard_map/ppermute | solution.py:314
  59.0 13.7 %collective-permute-start.8 = (bf16[256,384]{1,0:T(8,128)(2,1)S(1)}, bf16[256,384]{1,0:T(8,128)(2,1)S(1)}, u32[]{:S(2)}, u32[]{:S(2)}) collective-permute-start(bf16[256,384]{1,0:T(8,128)(2,1)S(1)} %get-tuple-element.38), channel_id=1, source_target_pairs={{0,4},{1,3},{2,6},{3,1},{4,0},{5,7},{6,2},{7,5},{8,12},{9,11},{10,... | collective-permute-start | bytes 589832 | tf_op jit(solution)/shard_map/ppermute | solution.py:314
  59.6 13.1 %collective-permute-start.7 = (bf16[256,384]{1,0:T(8,128)(2,1)S(1)}, bf16[256,384]{1,0:T(8,128)(2,1)S(1)}, u32[]{:S(2)}, u32[]{:S(2)}) collective-permute-start(bf16[256,384]{1,0:T(8,128)(2,1)S(1)} %get-tuple-element.37.refs_6_), channel_id=1, source_target_pairs={{0,2},{1,5},{2,0},{3,7},{4,6},{5,1},{6,4},{7,3},{8,10},{9,13},{10,... | collective-permute-start | bytes 589832 | tf_op jit(solution)/shard_map/ppermute | solution.py:314
  68.2 6.2 %collective-permute-start.14 = (bf16[64,768]{1,0:T(8,128)(2,1)S(1)}, bf16[64,768]{1,0:T(8,128)(2,1)S(1)}, u32[]{:S(2)}, u32[]{:S(2)}) collective-permute-start(bf16[64,768]{1,0:T(8,128)(2,1)S(1)} %get-tuple-element.45), channel_id=1, source_target_pairs={{0,8},{8,0},{16,24},{24,16},{1,9},{9,1},{17,25},{25,17},{2,10},{10... | collective-permute-start | bytes 294920 | tf_op jit(solution)/shard_map/ppermute | solution.py:326
  70.1 9.8 %collective-permute-start.15 = (bf16[64,768]{1,0:T(8,128)(2,1)S(1)}, bf16[64,768]{1,0:T(8,128)(2,1)S(1)}, u32[]{:S(2)}, u32[]{:S(2)}) collective-permute-start(bf16[64,768]{1,0:T(8,128)(2,1)S(1)} %get-tuple-element.46), channel_id=1, source_target_pairs={{0,16},{8,24},{16,0},{24,8},{1,17},{9,25},{17,1},{25,9},{2,18},{10... | collective-permute-start | bytes 294920 | tf_op jit(solution)/shard_map/ppermute | solution.py:326
  72.7 7.2 %collective-permute-start.16 = (bf16[64,768]{1,0:T(8,128)(2,1)S(1)}, bf16[64,768]{1,0:T(8,128)(2,1)S(1)}, u32[]{:S(2)}, u32[]{:S(2)}) collective-permute-start(bf16[64,768]{1,0:T(8,128)(2,1)S(1)} %get-tuple-element.47), channel_id=1, source_target_pairs={{0,24},{8,16},{16,8},{24,0},{1,25},{9,17},{17,9},{25,1},{2,26},{10... | collective-permute-start | bytes 294920 | tf_op jit(solution)/shard_map/ppermute | solution.py:326
  73.4 13.2 %collective-permute-start.11 = (bf16[64,384]{1,0:T(8,128)(2,1)S(1)}, bf16[64,384]{1,0:T(8,128)(2,1)S(1)}, u32[]{:S(2)}, u32[]{:S(2)}) collective-permute-start(bf16[64,384]{1,0:T(8,128)(2,1)S(1)} %get-tuple-element.42), channel_id=1, source_target_pairs={{0,8},{8,0},{16,24},{24,16},{1,9},{9,1},{17,25},{25,17},{2,10},{10... | collective-permute-start | bytes 147464 | tf_op jit(solution)/shard_map/ppermute | solution.py:326
  80.4 14.9 %collective-permute-start.22 = (bf16[64,768]{1,0:T(8,128)(2,1)S(1)}, bf16[64,768]{1,0:T(8,128)(2,1)S(1)}, u32[]{:S(2)}, u32[]{:S(2)}) collective-permute-start(bf16[64,768]{1,0:T(8,128)(2,1)S(1)} %shard_map.109.refs_6_.refs_2_), channel_id=1, source_target_pairs={{0,24},{8,16},{16,8},{24,0},{1,25},{9,17},{17,9},{25,1},{2,26},{10... | collective-permute-start | bytes 294920 | tf_op jit(solution)/shard_map/ppermute | solution.py:326
  83.0 12.3 %collective-permute-start.21 = (bf16[64,768]{1,0:T(8,128)(2,1)S(1)}, bf16[64,768]{1,0:T(8,128)(2,1)S(1)}, u32[]{:S(2)}, u32[]{:S(2)}) collective-permute-start(bf16[64,768]{1,0:T(8,128)(2,1)S(1)} %shard_map.109.refs_6_.refs_2_), channel_id=1, source_target_pairs={{0,16},{8,24},{16,0},{24,8},{1,17},{9,25},{17,1},{25,9},{2,18},{10... | collective-permute-start | bytes 294920 | tf_op jit(solution)/shard_map/ppermute | solution.py:326
  83.6 11.8 %collective-permute-start.20 = (bf16[64,768]{1,0:T(8,128)(2,1)S(1)}, bf16[64,768]{1,0:T(8,128)(2,1)S(1)}, u32[]{:S(2)}, u32[]{:S(2)}) collective-permute-start(bf16[64,768]{1,0:T(8,128)(2,1)S(1)} %shard_map.109.refs_6_.refs_2_), channel_id=1, source_target_pairs={{0,8},{8,0},{16,24},{24,16},{1,9},{9,1},{17,25},{25,17},{2,10},{10... | collective-permute-start | bytes 294920 | tf_op jit(solution)/shard_map/ppermute | solution.py:326
  84.9 9.9 %collective-permute-start.12 = (bf16[64,384]{1,0:T(8,128)(2,1)S(1)}, bf16[64,384]{1,0:T(8,128)(2,1)S(1)}, u32[]{:S(2)}, u32[]{:S(2)}) collective-permute-start(bf16[64,384]{1,0:T(8,128)(2,1)S(1)} %get-tuple-element.43), channel_id=1, source_target_pairs={{0,16},{8,24},{16,0},{24,8},{1,17},{9,25},{17,1},{25,9},{2,18},{10... | collective-permute-start | bytes 147464 | tf_op jit(solution)/shard_map/ppermute | solution.py:326
  86.6 8.1 %collective-permute-start.13 = (bf16[64,384]{1,0:T(8,128)(2,1)S(1)}, bf16[64,384]{1,0:T(8,128)(2,1)S(1)}, u32[]{:S(2)}, u32[]{:S(2)}) collective-permute-start(bf16[64,384]{1,0:T(8,128)(2,1)S(1)} %get-tuple-element.44), channel_id=1, source_target_pairs={{0,24},{8,16},{16,8},{24,0},{1,25},{9,17},{17,9},{25,1},{2,26},{10... | collective-permute-start | bytes 147464 | tf_op jit(solution)/shard_map/ppermute | solution.py:326
  95.9 7.8 %collective-permute-start.23 = (bf16[256,768]{1,0:T(8,128)(2,1)S(1)}, bf16[256,768]{1,0:T(8,128)(2,1)S(1)}, u32[]{:S(2)}, u32[]{:S(2)}) collective-permute-start(bf16[256,768]{1,0:T(8,128)(2,1)S(1)} %shard_map.111.refs_2_.refs_4_), channel_id=1, source_target_pairs={{0,4},{1,3},{2,6},{3,1},{4,0},{5,7},{6,2},{7,5},{8,12},{9,11},{10,... | collective-permute-start | bytes 1179656 | tf_op jit(solution)/shard_map/ppermute | solution.py:314
  104.4 14.5 %collective-permute-start.26 = (bf16[512,768]{1,0:T(8,128)(2,1)S(1)}, bf16[512,768]{1,0:T(8,128)(2,1)S(1)}, u32[]{:S(2)}, u32[]{:S(2)}) collective-permute-start(bf16[512,768]{1,0:T(8,128)(2,1)S(1)} %shard_map.112.refs_6_.refs_2_), channel_id=1, source_target_pairs={{0,2},{1,5},{2,0},{3,7},{4,6},{5,1},{6,4},{7,3},{8,10},{9,13},{10,... | collective-permute-start | bytes 2359304 | tf_op jit(solution)/shard_map/ppermute | solution.py:314
  104.5 6.3 %collective-permute-start.19 = (bf16[64,384]{1,0:T(8,128)(2,1)S(1)}, bf16[64,384]{1,0:T(8,128)(2,1)S(1)}, u32[]{:S(2)}, u32[]{:S(2)}) collective-permute-start(bf16[64,384]{1,0:T(8,128)(2,1)S(1)} %shard_map.110.refs_6_.refs_2_), channel_id=1, source_target_pairs={{0,24},{8,16},{16,8},{24,0},{1,25},{9,17},{17,9},{25,1},{2,26},{10... | collective-permute-start | bytes 147464 | tf_op jit(solution)/shard_map/ppermute | solution.py:326
  106.2 5.8 %collective-permute-start.18 = (bf16[64,384]{1,0:T(8,128)(2,1)S(1)}, bf16[64,384]{1,0:T(8,128)(2,1)S(1)}, u32[]{:S(2)}, u32[]{:S(2)}) collective-permute-start(bf16[64,384]{1,0:T(8,128)(2,1)S(1)} %shard_map.110.refs_6_.refs_2_), channel_id=1, source_target_pairs={{0,16},{8,24},{16,0},{24,8},{1,17},{9,25},{17,1},{25,9},{2,18},{10... | collective-permute-start | bytes 147464 | tf_op jit(solution)/shard_map/ppermute | solution.py:326
  107.1 4.9 %collective-permute-start.17 = (bf16[64,384]{1,0:T(8,128)(2,1)S(1)}, bf16[64,384]{1,0:T(8,128)(2,1)S(1)}, u32[]{:S(2)}, u32[]{:S(2)}) collective-permute-start(bf16[64,384]{1,0:T(8,128)(2,1)S(1)} %shard_map.110.refs_6_.refs_2_), channel_id=1, source_target_pairs={{0,8},{8,0},{16,24},{24,16},{1,9},{9,1},{17,25},{25,17},{2,10},{10... | collective-permute-start | bytes 147464 | tf_op jit(solution)/shard_map/ppermute | solution.py:326
  112.6 5.7 %collective-permute-start.24 = (bf16[256,384]{1,0:T(8,128)(2,1)S(1)}, bf16[256,384]{1,0:T(8,128)(2,1)S(1)}, u32[]{:S(2)}, u32[]{:S(2)}) collective-permute-start(bf16[256,384]{1,0:T(8,128)(2,1)S(1)} %shard_map.113.refs_2_.refs_4_), channel_id=1, source_target_pairs={{0,4},{1,3},{2,6},{3,1},{4,0},{5,7},{6,2},{7,5},{8,12},{9,11},{10,... | collective-permute-start | bytes 589832 | tf_op jit(solution)/shard_map/ppermute | solution.py:314
  119.6 3.5 %collective-permute-start.27 = (bf16[1024,768]{1,0:T(8,128)(2,1)S(1)}, bf16[1024,768]{1,0:T(8,128)(2,1)S(1)}, u32[]{:S(2)}, u32[]{:S(2)}) collective-permute-start(bf16[1024,768]{1,0:T(8,128)(2,1)S(1)} %shard_map.115.refs_2_.refs_7_), channel_id=1, source_target_pairs={{0,1},{1,0},{2,3},{3,2},{4,5},{5,4},{6,7},{7,6},{8,9},{9,8},{10,11... | collective-permute-start | bytes 4718600 | tf_op jit(solution)/shard_map/ppermute | solution.py:302
  119.8 12.1 %collective-permute-start.25 = (bf16[512,384]{1,0:T(8,128)(2,1)S(1)}, bf16[512,384]{1,0:T(8,128)(2,1)S(1)}, u32[]{:S(2)}, u32[]{:S(2)}) collective-permute-start(bf16[512,384]{1,0:T(8,128)(2,1)S(1)} %shard_map.114.refs_4_.refs_2_), channel_id=1, source_target_pairs={{0,2},{1,5},{2,0},{3,7},{4,6},{5,1},{6,4},{7,3},{8,10},{9,13},{10,... | collective-permute-start | bytes 1179656 | tf_op jit(solution)/shard_map/ppermute | solution.py:314
  132.5 2.4 %collective-permute-start.28 = (bf16[1024,384]{1,0:T(8,128)(2,1)S(1)}, bf16[1024,384]{1,0:T(8,128)(2,1)S(1)}, u32[]{:S(2)}, u32[]{:S(2)}) collective-permute-start(bf16[1024,384]{1,0:T(8,128)(2,1)S(1)} %shard_map.117.refs_2_.refs_12_), channel_id=1, source_target_pairs={{0,1},{1,0},{2,3},{3,2},{4,5},{5,4},{6,7},{7,6},{8,9},{9,8},{10,11... | collective-permute-start | bytes 2359304 | tf_op jit(solution)/shard_map/ppermute | solution.py:302

commit v3 on v2

v3 whole, which is shorter than its diff:
```python
import math

import jax
import jax.numpy as jnp
from jax import lax
from jax.experimental import pallas as pl
from jax.experimental.pallas import tpu as pltpu
from jax.sharding import PartitionSpec as P

BF = jnp.bfloat16
F32 = jnp.float32


def plain_shards(entries, readin, offset, cutoff, writeout, hidden, depth):
    layer = lax.axis_index("layer")
    owner = jnp.logical_and(layer == 0, lax.axis_index("feat") == 0).astype(F32)
    gathered = lax.all_gather(entries, "tok", axis=1, tiled=True)[0]
    inverse = 1.0 / math.sqrt(gathered.shape[0])
    gate = cutoff[0].astype(F32)
    pre = jnp.dot(gathered, readin[0], preferred_element_type=F32) + offset[0][None, :]
    act = (pre * gate).astype(BF)
    live = (layer <= depth).astype(F32)
    targets = writeout.shape[1]
    partials = jnp.stack(
        [jnp.dot(act, writeout[0, t], preferred_element_type=F32) for t in range(targets)]
    )
    rows = hidden.shape[1]
    start = lax.axis_index("tok") * rows
    current = lax.dynamic_slice_in_dim(partials, start, rows, 1)
    partials = lax.dynamic_update_slice_in_dim(
        partials, current - owner * hidden.astype(F32), start, 1
    )
    summed = lax.psum_scatter(
        partials * live[:, None, None], ("feat", "tok"), scatter_dimension=1, tiled=True
    )
    summed = lax.psum(summed, "layer")
    scaled = lax.all_gather((summed * inverse).astype(BF), ("feat", "tok"), axis=1, tiled=True)
    dec = [
        (jnp.einsum("tf,td->fd", act, scaled[t], preferred_element_type=F32) * live[t]).astype(BF)
        for t in range(targets)
    ]
    sens = sum(
        live[t] * jnp.einsum("td,fd->tf", scaled[t], writeout[0, t], preferred_element_type=F32)
        for t in range(targets)
    )
    pre_grad = sens * gate
    enc = jnp.einsum("td,tf->df", gathered, pre_grad.astype(BF), preferred_element_type=F32)
    return enc.astype(BF)[None], jnp.stack(dec)[None], jnp.sum(pre_grad, axis=0)[None]


def column_chunks(width):
    for parts in (3, 2):
        if width % (128 * parts) == 0:
            unit = width // parts
            return [(0, width - unit), (width - unit, width)]
    return [(0, width)]


VMEM_MIB = 16
FEATURE_BLOCK = 512
ROWS_UNIT = 128
SIDE, CORE, FEAT, LAYER = range(4)
HELD = pl.BlockSpec(memory_space=pltpu.VMEM)
ANYWHERE = pl.BlockSpec(memory_space=pl.ANY)


def held(shape, dtype):
    return pltpu.VMEM(shape, dtype)


def array(shape, dtype):
    return jax.ShapeDtypeStruct(shape, dtype)


def block_of(features):
    return FEATURE_BLOCK if features % FEATURE_BLOCK == 0 else features


def span(number, size):
    return pl.ds(pl.multiple_of(number * size, size), size)


class Order:
    def __init__(self, scalars):
        self.scalars = scalars
        self.last = None

    def __call__(
        self, kernel, operands, outs, specs=None, out_specs=None, grid=(1,), scratch=(), aliases=()
    ):
        count = len(operands)
        operands = list(operands)
        specs = list(specs or [HELD] * count)
        waits = [] if self.last is None else [self.last]

        def body(*refs):
            at = len(self.scalars) + count
            kernel(*refs[:at], *refs[at + len(waits) :])

        results = pl.pallas_call(
            body,
            grid_spec=pltpu.PrefetchScalarGridSpec(
                num_scalar_prefetch=len(self.scalars),
                grid=grid,
                in_specs=specs + [ANYWHERE] * len(waits),
                out_specs=list(out_specs or [HELD] * len(outs)),
                scratch_shapes=list(scratch),
            ),
            out_shape=list(outs),
            input_output_aliases={len(self.scalars) + i: o for i, o in aliases},
            compiler_params=pltpu.CompilerParams(vmem_limit_bytes=VMEM_MIB * 1024 * 1024),
            cost_estimate=pl.CostEstimate(flops=1000, bytes_accessed=1000, transcendentals=0),
        )(*self.scalars, *operands, *waits)
        self.last = results[0]
        return results

    def pass_on(self, value):
        def kernel(*refs):
            pass

        like = array(value.shape, value.dtype)
        return self(kernel, [value], [like], [ANYWHERE], [ANYWHERE], aliases=[(0, 0)])[0]


def load(order, *operands):
    parts = []
    for k, o in enumerate(operands):
        axis = max(range(o.ndim - 1), key=lambda i: o.shape[i])
        cuts = 4 if o.shape[axis] % 64 == 0 else 1
        size = o.shape[axis] // cuts
        for c in range(cuts):
            parts.append((k, (slice(None),) * axis + (pl.ds(c * size, size),)))

    def kernel(w, d, *refs):
        *refs, sems = refs
        n = len(operands)
        copies = [
            pltpu.make_async_copy(refs[k].at[at], refs[n + k].at[at], sems.at[i])
            for i, (k, at) in enumerate(parts)
        ]
        for copy in copies:
            copy.start()
        for copy in copies:
            copy.wait()

    return order(
        kernel,
        [pltpu.with_memory_space_constraint(o, pltpu.HBM) for o in operands],
        [held(o.shape, o.dtype) for o in operands],
        specs=[pl.BlockSpec(memory_space=pltpu.HBM)] * len(operands),
        scratch=[pltpu.SemaphoreType.DMA((len(parts),))],
    )


def encode(order, near, parts, readin, offset, cutoff):
    rows, width = parts[0].shape
    count = 2 * rows

    def kernel(w, d, own_ref, other_ref, readin_ref, offset_ref, cutoff_ref, act_ref, both):
        for ref, number in ((own_ref, w[CORE]), (other_ref, 1 - w[CORE])):
            both[span(number, rows), :] = ref[...]
        first = w[SIDE] if near else 1 - w[SIDE]
        pre = jnp.dot(both[...], readin_ref[0], preferred_element_type=F32)
        gate = cutoff_ref[0, span(first, count), :].astype(F32)
        act_ref[...] = ((pre + offset_ref[...]) * gate).astype(BF)

    return order(
        kernel,
        [*parts, readin, offset, cutoff],
        [held((count, readin.shape[-1]), BF)],
        scratch=[pltpu.VMEM((count, width), BF)],
    )[0]


def turn(order, acts, parts):
    count, features = acts[0].shape
    rows, width = parts[0][0].shape

    def kernel(w, d, *refs):
        act_refs, part_refs, (turned_ref, tokens_ref) = refs[:2], refs[2:6], refs[6:]
        for half in range(2):
            turned_ref[:, half * count : (half + 1) * count] = act_refs[half][...].T
            for ref, number in zip(part_refs[2 * half : 2 * half + 2], (w[CORE], 1 - w[CORE])):
                tokens_ref[:, span(2 * half + number, rows)] = ref[...].T

    return order(
        kernel,
        [*acts, *parts[0], *parts[1]],
        [held((features, 2 * count), BF), held((width, 2 * count), BF)],
    )


def decode(order, away, act, writeout, hidden, lo, hi):
    count, features = act.shape
    blocks = 2
    rows = count // blocks
    dtype = BF if away else F32

    def kernel(w, d, act_ref, weight_ref, *rest):
        target = 1 - w[CORE] if away else w[CORE]
        live = jnp.where(w[LAYER] <= d[target], 1.0, 0.0)
        out = jnp.dot(act_ref[...], weight_ref[0, target, :, lo:hi], preferred_element_type=F32)
        parts = [out[b * rows : (b + 1) * rows] for b in range(blocks)]
        if hidden is not None:
            less = rest[0][target, :, lo:hi].astype(F32)
            owner = jnp.logical_and(w[LAYER] == 0, w[FEAT] == 0)
            mine = [jnp.logical_and(owner, w[CORE] == b) for b in range(blocks)]
            parts = [p - jnp.where(m, 1.0, 0.0) * less for p, m in zip(parts, mine)]
        for ref, part in zip(rest[-blocks:], parts):
            ref[...] = (part * live).astype(dtype)

    operands = [act, writeout] + ([] if hidden is None else [hidden])
    return order(kernel, operands, [held((rows, hi - lo), dtype)] * blocks)


def gradients(order, scaled, turned, writeout, lo, hi, sens=None, dec=None, last=None):
    targets, features, width = writeout.shape[1:]
    total, columns = scaled[0].shape
    count = total // 2
    block = block_of(features)
    at = lo // columns

    def kernel(w, d, *refs):
        refs = list(refs)
        s_refs = [refs.pop(0) for _ in range(targets)]
        turned_ref, weight_ref = refs.pop(0), refs.pop(0)
        sens_in = refs.pop(0) if sens is not None else None
        if last is not None:
            cutoff_ref, tokens_ref = refs.pop(0), refs.pop(0)
        if dec is not None:
            refs.pop(0)
        dec_ref = refs.pop(0)
        cols = span(pl.program_id(0), block)
        numbers = [w[CORE], 1 - w[CORE]]
        grad = 0.0 if sens_in is None else sens_in[:, cols]
        for ref, number in zip(s_refs, numbers):
            grad = grad + lax.dot_general(
                ref[...],
                weight_ref[0, number, cols, lo:hi],
                (((1,), (1,)), ((), ())),
                preferred_element_type=F32,
            )
        if last is None:
            refs[0][:, cols] = grad
        else:
            enc_ref, bias_ref, low_ref = refs
            biases = 0.0
            for half, side in enumerate((w[SIDE], 1 - w[SIDE])):
                rows = slice(half * count, (half + 1) * count)
                part = grad[rows] * cutoff_ref[0, span(side, count), cols].astype(F32)
                biases = biases + jnp.sum(part, axis=0, keepdims=True)
                low_ref[rows, :] = part.astype(BF)
            bias_ref[...] = biases
            enc_ref[0] = jnp.dot(
                tokens_ref[...], low_ref[...], preferred_element_type=F32
            ).astype(BF)
        for ref, number in zip(s_refs, numbers):
            out = jnp.dot(turned_ref[cols, :], ref[...], preferred_element_type=F32)
            dec_ref[0, number] = out.astype(BF)

    operands = [*scaled, turned, writeout]
    if sens is not None:
        operands.append(sens)
    if last is not None:
        operands += last
    specs = [HELD] * len(operands)
    aliases = []
    if dec is not None:
        aliases = [(len(operands), 0)]
        operands.append(dec)
        specs.append(ANYWHERE)
    out_specs = [pl.BlockSpec((1, targets, block, columns), lambda i, w, d: (0, 0, i, at))]
    outs = [array(writeout.shape, BF)]
    scratch = []
    if last is not None:
        out_specs.append(pl.BlockSpec((1, width, block), lambda i, w, d: (0, 0, i)))
        out_specs.append(pl.BlockSpec((1, block), lambda i, w, d: (0, i)))
        outs += [array((1, width, features), BF), array((1, features), F32)]
        scratch.append(pltpu.VMEM((total, block), BF))
    else:
        out_specs.append(HELD)
        outs.append(held((total, features), F32))
    results = order(
        kernel, operands, outs, specs, out_specs, (features // block,), scratch, aliases
    )
    if last is None:
        order.last = results[1]
    return results


def pick(flag, a, b):
    return jnp.where(flag, a, b)


def paired_shards(sizes, entries, readin, offset, cutoff, writeout, hidden, depth):
    layers, feats, toks = sizes
    layer, feat, tok = (lax.axis_index(a) for a in ("layer", "feat", "tok"))
    where = jnp.stack([tok // 2, tok % 2, feat, layer]).astype(jnp.int32)
    order = Order((where, depth))

    def to_core(a):
        return lax.ppermute(a, "tok", [(t, t ^ 1) for t in range(toks)])

    def to_side(a):
        return lax.ppermute(a, "tok", [(t, t ^ 2) for t in range(toks)])

    def mixed(first):
        pairs = []
        for f in range(feats):
            for t in range(toks):
                over_side = (t % 2 == 0) == first
                goal = (f, t ^ 2) if over_side else (f ^ 1, t)
                pairs.append((f * toks + t, goal[0] * toks + goal[1]))
        return lambda a: lax.ppermute(a, ("feat", "tok"), pairs)

    to_first, to_second = mixed(True), mixed(False)
    binary = layers & (layers - 1) == 0

    def layer_goal(l, s):
        return l ^ s if binary else lax.rem(l + s, layers)

    def layer_source(l, s):
        return l ^ s if binary else lax.rem(l - s + layers, layers)

    def to_layer(a, s):
        return lax.ppermute(
            a, "layer", [(l, l ^ s if binary else (l + s) % layers) for l in range(layers)]
        )

    own = entries[0]
    rows, width = own.shape
    total = rows * toks
    inverse = 1.0 / math.sqrt(total)
    piece = rows // layers
    chunks = column_chunks(width)

    far = to_side(own)
    near = to_core(own)
    readin, cutoff, writeout, hidden = load(order, readin, cutoff, writeout, hidden)
    act_near = encode(order, True, (own, near), readin, offset, cutoff)

    def partials(act, hidden, lo, hi):
        away = decode(order, True, act, writeout, hidden, lo, hi)
        got = [to_core(a) for a in away]
        return (*decode(order, False, act, writeout, hidden, lo, hi), *got)

    here = partials(act_near, hidden, 0, width)
    far = order.pass_on(far)

    def first_kernel(w, d, kept0, kept1, got0, got1, out):
        other = pick(w[FEAT] == 1, kept0[...], kept1[...])
        out[...] = (other + pick(w[FEAT] == 1, got0[...], got1[...]).astype(F32)).astype(BF)

    send = order(first_kernel, here, [held((rows, width), BF)])[0]
    got_first = to_first(send)

    far_near = to_core(far)
    act_far = encode(order, False, (far, far_near), readin, offset, cutoff)

    def reduce_sides(lo, hi):
        size = hi - lo
        there = partials(act_far, None, lo, hi)

        def second_kernel(
            w, d, hk0, hk1, hg0, hg1, tk0, tk1, tg0, tg1, first, out_first, out_second
        ):
            y0 = w[FEAT] == 0
            here_y = pick(y0, hk0[:, lo:hi], hk1[:, lo:hi])
            here_y += pick(y0, hg0[:, lo:hi], hg1[:, lo:hi]).astype(F32)
            there_other = pick(y0, tk1[...], tk0[...])
            there_other += pick(y0, tg1[...], tg0[...]).astype(F32)
            zero = w[CORE] == 0
            out_first[...] = pick(zero, here_y, there_other).astype(BF)
            rest = pick(zero, there_other, here_y) + first[:, lo:hi].astype(F32)
            out_second[...] = rest.astype(BF)

        sends = order(second_kernel, (*here, *there, got_first), [held((rows, size), BF)] * 2)
        return there, to_first(sends[0]), to_second(sends[1])

    def exchange(previous, reduced):
        ahead = 0 if previous is None else previous[0].shape[1]
        behind = 0 if previous is None else previous[1][0].shape[1] - ahead
        size = 0 if reduced is None else reduced[2].shape[1]

        def kernel(w, d, *refs):
            refs = list(refs)
            if previous is not None:
                value = refs.pop(0)[...]
                for _ in previous[1]:
                    value = value + refs.pop(0)[:, behind:].astype(F32)
                value = (value * inverse).astype(BF)
            if reduced is not None:
                tk0, tk1, tg0, tg1, first, second = (refs.pop(0) for _ in range(6))
                kept = refs.pop()
                y0 = w[FEAT] == 0
                kept[...] = (
                    pick(y0, tk0[...], tk1[...])
                    + pick(y0, tg0[...], tg1[...]).astype(F32)
                    + first[...].astype(F32)
                    + second[...].astype(F32)
                )
            if previous is not None:
                refs.pop(0)[...] = value
            if reduced is not None:
                refs.pop(0)[...] = kept[span(w[LAYER], piece), :]
            for s, out in enumerate(refs, 1):
                if previous is not None:
                    out[:, :ahead] = value
                if reduced is not None:
                    goal = layer_goal(w[LAYER], s)
                    out[:, ahead:] = kept[span(goal, piece), :].astype(BF)

        operands, outs, scratch = [], [], []
        if previous is not None:
            operands += [previous[0], *previous[1]]
            outs.append(held((piece, ahead), BF))
        if reduced is not None:
            there, got, got_second = reduced
            operands += [*there, got, got_second]
            outs.append(held((piece, size), F32))
            scratch.append(pltpu.VMEM((rows, size), F32))
        mine = len(outs)
        outs += [held((piece, ahead + size), BF)] * (layers - 1)
        results = order(kernel, operands, outs, scratch=scratch)
        came = [to_layer(out, s) for s, out in enumerate(results[mine:], 1)]
        scaled = None if previous is None else results[0]
        return scaled, None if reduced is None else results[mine - 1], came

    def join_pieces(scaled, pieces):
        size = scaled.shape[1]

        def kernel(w, d, *refs):
            *refs, out = refs
            out[span(w[LAYER], piece), :] = refs[0][...]
            for s, ref in enumerate(refs[1:], 1):
                out[span(layer_source(w[LAYER], s), piece), :] = ref[:, :size]

        done = order(kernel, (scaled, *pieces), [held((rows, size), BF)])[0]
        return done, to_second(done)

    def join_pair(done, got):
        def kernel(w, d, done_ref, got_ref, out0, out1):
            done_last = jnp.logical_or(w[CORE] == 1, w[FEAT] == 1)
            out0[...] = pick(done_last, got_ref[...], done_ref[...])
            out1[...] = pick(done_last, done_ref[...], got_ref[...])

        pair = order(kernel, (done, got), [held(done.shape, BF)] * 2)
        return pair, [to_first(block) for block in pair]

    def join_all(pair, got):
        def kernel(w, d, pair0, pair1, got0, got1, out):
            zero = w[CORE] == 0
            y = w[FEAT]
            live = jnp.where(w[LAYER] <= d[w[CORE]], 1.0, 0.0).astype(BF)
            for ref, number in (
                (pair0, pick(zero, 2, y)),
                (pair1, pick(zero, 3, 2 + y)),
                (got0, pick(zero, 0, 1 - y)),
                (got1, pick(zero, 1, 3 - y)),
            ):
                out[span(number, rows), :] = ref[...] * live

        size = pair[0].shape[1]
        full = order(kernel, (*pair, *got), [held((total, size), BF)])[0]
        return full, to_core(full)

    reduced = [reduce_sides(lo, hi) for lo, hi in chunks]
    turned, tokens = turn(order, (act_near, act_far), ((own, near), (far, far_near)))
    scaled, mine, came = exchange(None, reduced[0])
    pairs = []
    joined = None
    for k in range(len(chunks)):
        scaled, mine, then = exchange((mine, came), (reduced + [None])[k + 1])
        if joined is not None:
            pairs.append(join_pair(*joined))
        came = then
        joined = join_pieces(scaled, came)
    pairs.append(join_pair(*joined))
    scaled = [join_all(*pair) for pair in pairs]
    sens = dec = None
    for k, (lo, hi) in enumerate(chunks):
        last = (cutoff, tokens) if k == len(chunks) - 1 else None
        dec, *rest = gradients(order, scaled[k], turned, writeout, lo, hi, sens, dec, last)
        sens = rest[0]
    return rest[0], dec, rest[1]


def solution(mesh):
    sizes = tuple(mesh.shape[a] for a in ("layer", "feat", "tok"))

    def shards(*args):
        rows = args[0].shape[1]
        targets = args[4].shape[1]
        paired = sizes[1] == targets == 2 and sizes[2] == 4
        if paired and rows % ROWS_UNIT == 0 and rows % (16 * sizes[0]) == 0:
            return paired_shards(sizes, *args)
        return plain_shards(*args)

    return jax.shard_map(
        shards,
        mesh=mesh,
        in_specs=(
            P("layer", "tok", None),
            P("layer", None, ("feat", "tok")),
            P("layer", ("feat", "tok")),
            P("layer", None, ("feat", "tok")),
            P("layer", None, ("feat", "tok"), None),
            P(None, "tok", None),
            P(),
        ),
        out_specs=(
            P("layer", None, ("feat", "tok")),
            P("layer", None, ("feat", "tok"), None),
            P("layer", ("feat", "tok")),
        ),
        check_vma=False,
    )
```

time: 145 us -> 126 us (0.87)
  waiting for transfers between devices: 55.2 us -> 43.9 us
  Pallas kernels: 55.1 us -> 48.4 us
  starting transfers between devices: 33.2 us -> 31.7 us
    ppermute x1, waiting for transfers between devices: 10.5 us -> 1.12 us  [to_side(): return lax.ppermute(a, 'tok', [(t, t ^ 2) for t in range(toks)])]
    pallas_call x25, Pallas kernels: 55.1 us -> 48.4 us  [__call__(): pl.pallas_call(body, grid_spec=pltpu.PrefetchScalarGridSpec(num_scalar_pr...]
    ppermute x7 -> x10, waiting for transfers between devices: 5.81 us -> 0.25 us  [to_core(): return lax.ppermute(a, 'tok', [(t, t ^ 1) for t in range(toks)])]
    ppermute x12 -> x9, waiting for transfers between devices: 15.4 us -> 20.7 us  [to_layer(): lax.ppermute(a, 'layer', [(l, l ^ s if binary else (l + s) % layers) for...]
    ppermute x12 -> x9, starting transfers between devices: 17.4 us -> 13.5 us  [to_layer(): lax.ppermute(a, 'layer', [(l, l ^ s if binary else (l + s) % layers) for...]
    ppermute x9 -> x11, starting transfers between devices: 11.4 us -> 13.3 us  [mixed(): return lambda a: lax.ppermute(a, ('feat', 'tok'), pairs)]
    ppermute x9 -> x11, waiting for transfers between devices: 23.5 us -> 21.9 us  [mixed(): return lambda a: lax.ppermute(a, ('feat', 'tok'), pairs)]
  transfers between devices with their start and end apart: 29 -> 31, of which waited for: 13 -> 14; matrix products, arithmetic and copies ran while one was open for 0% -> 0% of each run, Pallas kernels for 17% -> 28%
where the time goes in v3:
time: 126 us
  Pallas kernels  48.4 us (38%)
  waiting for transfers between devices  43.9 us (35%)
  starting transfers between devices  31.7 us (25%)
    pallas_call x25, Pallas kernels, __call__(): pl.pallas_call(body, grid_spec=pltpu.PrefetchScalarGridSpec(num_scalar_pr...  48.4 us
    ppermute x11, waiting for transfers between devices, mixed(): return lambda a: lax.ppermute(a, ('feat', 'tok'), pairs)  21.9 us
    ppermute x9, waiting for transfers between devices, to_layer(): lax.ppermute(a, 'layer', [(l, l ^ s if binary else (l + s) % layers) for...  20.7 us
    ppermute x9, starting transfers between devices, to_layer(): lax.ppermute(a, 'layer', [(l, l ^ s if binary else (l + s) % layers) for...  13.5 us
    ppermute x11, starting transfers between devices, mixed(): return lambda a: lax.ppermute(a, ('feat', 'tok'), pairs)  13.3 us
    ppermute x1, starting transfers between devices, to_side(): return lax.ppermute(a, 'tok', [(t, t ^ 2) for t in range(toks)])  2.57 us
  transfers between devices with their start and end apart: 31, of which 14 were waited for; matrix products, arithmetic and copies ran while one was open for 0% of the time, Pallas kernels for 28%

profile of v3, /device:TPU:0, one launch (start us, length us, event | category | flops | bytes accessed | tf_op | source)
XLA Modules:
  0.0 125.8 jit_solution(13871412548454542553)
XLA Ops:
  1.1 2.6 %collective-permute-start = (bf16[256,1152]{1,0:T(8,128)(2,1)}, bf16[256,1152]{1,0:T(8,128)(2,1)S(1)}, u32[]{:S(2)}, u32[]{:S(2)}) collective-permute-start(bf16[256,1152]{1,0:T(8,128)(2,1)} %bitcast.6), channel_id=1, source_target_pairs={{0,2},{1,3},{2,0},{3,1},{4,6},{5,7},{6,4},{7,5},{8,10},{9,11},{10,... | collective-permute-start | bytes 1769480 | tf_op jit(solution)/shard_map/ppermute | solution.py:305
  4.5 5.3 %shard_map.94 = (bf16[1,1152,1024]{2,1,0:T(8,128)(2,1)S(1)}, s32[1,1024,1024]{2,1,0:T(8,128)S(1)}, bf16[1,2,1024,1152]{3,2,1,0:T(8,128)(2,1)S(1)}, bf16[2,256,1152]{2,1,0:T(8,128)(2,1)S(1)}) custom-call(s32[4]{0:T(128)S(1)} %pad_add_fusion.refs_0_, s32[2]{0:T(128)S(1)} %copy-done.1, bf16[1,1152,1024]{2,1,0:T(8,128)(2,1)} %refs_2_.1, ...), custom_call_target="tpu_custom_call" | custom-call | flops 1000 | bytes 1000 | tf_op jit(solution)/shard_map/pallas_call | solution.py:100
  9.8 2.2 %shard_map.95.refs_2_.refs_5_ = bf16[512,1024]{1,0:T(8,128)(2,1)S(1)} custom-call(s32[4]{0:T(128)S(1)} %pad_add_fusion.refs_0_, s32[2]{0:T(128)S(1)} %copy-done.1, bf16[256,1152]{1,0:T(8,128)(2,1)S(1)} %bitcast.7, bf16[256,1152]{1,0:T(8,128)(2,1)S(1)} %collective-permute-done.1.refs_3_.refs_5_, bf16[1,1152,1024]{2,1,0:T(8,128)(2,1)S(1)} %get-tuple-element.47.refs_4_.refs_7_, ...), custom_call_target="tpu_custom_call" | custom-call | flops 1000 | bytes 1000 | tf_op jit(solution)/shard_map/pallas_call | solution.py:100
  12.0 2.1 %shard_map.96 = (bf16[256,1152]{1,0:T(8,128)(2,1)S(1)}, bf16[256,1152]{1,0:T(8,128)(2,1)S(1)}) custom-call(s32[4]{0:T(128)S(1)} %pad_add_fusion.refs_0_, s32[2]{0:T(128)S(1)} %copy-done.1, bf16[512,1024]{1,0:T(8,128)(2,1)S(1)} %shard_map.95.refs_2_.refs_5_, bf16[1,2,1024,1152]{3,2,1,0:T(8,128)(2,1)S(1)} %get-tuple-element.49.refs_3_.refs_5_, ...), custom_call_target="tpu_custom_call" | custom-call | flops 1000 | bytes 1000 | tf_op jit(solution)/shard_map/pallas_call | solution.py:100
  14.6 2.1 %shard_map.97 = (f32[256,1152]{1,0:T(8,128)S(1)}, f32[256,1152]{1,0:T(8,128)S(1)}) custom-call(s32[4]{0:T(128)S(1)} %pad_add_fusion.refs_0_, s32[2]{0:T(128)S(1)} %copy-done.1, bf16[512,1024]{1,0:T(8,128)(2,1)S(1)} %shard_map.95.refs_2_.refs_5_, bf16[1,2,1024,1152]{3,2,1,0:T(8,128)(2,1)S(1)} %get-tuple-element.49.refs_3_.refs_5_, ...), custom_call_target="tpu_custom_call" | custom-call | flops 1000 | bytes 1000 | tf_op jit(solution)/shard_map/pallas_call | solution.py:100
  19.3 1.8 %collective-permute-start.7 = (bf16[256,1152]{1,0:T(8,128)(2,1)S(1)}, bf16[256,1152]{1,0:T(8,128)(2,1)S(1)}, u32[]{:S(2)}, u32[]{:S(2)}) collective-permute-start(bf16[256,1152]{1,0:T(8,128)(2,1)S(1)} %shard_map.99.refs_7_), channel_id=1, source_target_pairs={{0,2},{1,5},{2,0},{3,7},{4,6},{5,1},{6,4},{7,3},{8,10},{9,13},{10,... | collective-permute-start | bytes 1769480 | tf_op jit(solution)/shard_map/ppermute | solution.py:314
  21.1 2.2 %shard_map.100.refs_2_.refs_4_.refs_3_ = bf16[512,1024]{1,0:T(8,128)(2,1)S(1)} custom-call(s32[4]{0:T(128)S(1)} %pad_add_fusion.refs_0_, s32[2]{0:T(128)S(1)} %copy-done.2, bf16[256,1152]{1,0:T(8,128)(2,1)S(1)} %shard_map.98.refs_6_.refs_2_, bf16[256,1152]{1,0:T(8,128)(2,1)S(1)} %collective-permute-done.2.refs_3_.refs_7_, ...), custom_call_target="tpu_custom_call" | custom-call | flops 1000 | bytes 1000 | tf_op jit(solution)/shard_map/pallas_call | solution.py:100
  23.3 1.5 %shard_map.101 = (bf16[256,768]{1,0:T(8,128)(2,1)S(1)}, bf16[256,768]{1,0:T(8,128)(2,1)S(1)}) custom-call(s32[4]{0:T(128)S(1)} %pad_add_fusion.refs_0_, s32[2]{0:T(128)S(1)} %copy-done.2, bf16[512,1024]{1,0:T(8,128)(2,1)S(1)} %shard_map.100.refs_2_.refs_4_.refs_3_, bf16[1,2,1024,1152]{3,2,1,0:T(8,128)(2,1)S(1)} %get-tuple-element.49.refs_3_.refs_5_, ...), custom_call_target="tpu_custom_call" | custom-call | flops 1000 | bytes 1000 | tf_op jit(solution)/shard_map/pallas_call | solution.py:100
  25.4 1.5 %shard_map.102 = (f32[256,768]{1,0:T(8,128)S(1)}, f32[256,768]{1,0:T(8,128)S(1)}) custom-call(s32[4]{0:T(128)S(1)} %pad_add_fusion.refs_0_, s32[2]{0:T(128)S(1)} %copy-done.2, bf16[512,1024]{1,0:T(8,128)(2,1)S(1)} %shard_map.100.refs_2_.refs_4_.refs_3_, bf16[1,2,1024,1152]{3,2,1,0:T(8,128)(2,1)S(1)} %get-tuple-element.49.refs_3_.refs_5_, ...), custom_call_target="tpu_custom_call" | custom-call | flops 1000 | bytes 1000 | tf_op jit(solution)/shard_map/pallas_call | solution.py:100
  27.2 2.0 %collective-permute-done.7.refs_10_ = bf16[256,1152]{1,0:T(8,128)(2,1)S(1)} collective-permute-done((bf16[256,1152]{1,0:T(8,128)(2,1)S(1)}, bf16[256,1152]{1,0:T(8,128)(2,1)S(1)}, u32[]{:S(2)}, u32[]{:S(2)}) %collective-permute-start.7) | collective-permute-done | bytes 589856 | tf_op jit(solution)/shard_map/ppermute | solution.py:314
  30.2 1.9 %collective-permute-start.9 = (bf16[256,768]{1,0:T(8,128)(2,1)S(1)}, bf16[256,768]{1,0:T(8,128)(2,1)S(1)}, u32[]{:S(2)}, u32[]{:S(2)}) collective-permute-start(bf16[256,768]{1,0:T(8,128)(2,1)S(1)} %get-tuple-element.60), channel_id=1, source_target_pairs={{0,4},{1,3},{2,6},{3,1},{4,0},{5,7},{6,2},{7,5},{8,12},{9,11},{10,... | collective-permute-start | bytes 1179656 | tf_op jit(solution)/shard_map/ppermute | solution.py:314
  32.0 1.5 %collective-permute-start.8 = (bf16[256,768]{1,0:T(8,128)(2,1)S(1)}, bf16[256,768]{1,0:T(8,128)(2,1)S(1)}, u32[]{:S(2)}, u32[]{:S(2)}) collective-permute-start(bf16[256,768]{1,0:T(8,128)(2,1)S(1)} %get-tuple-element.59.refs_4_), channel_id=1, source_target_pairs={{0,2},{1,5},{2,0},{3,7},{4,6},{5,1},{6,4},{7,3},{8,10},{9,13},{10,... | collective-permute-start | bytes 1179656 | tf_op jit(solution)/shard_map/ppermute | solution.py:314
  38.2 1.8 %shard_map.107 = (bf16[1024,1024]{1,0:T(8,128)(2,1)S(1)}, bf16[1152,1024]{1,0:T(8,128)(2,1)S(1)}) custom-call(s32[4]{0:T(128)S(1)} %pad_add_fusion.refs_0_, s32[2]{0:T(128)S(1)} %copy-done.2, bf16[512,1024]{1,0:T(8,128)(2,1)S(1)} %shard_map.95.refs_2_.refs_5_, bf16[512,1024]{1,0:T(8,128)(2,1)S(1)} %shard_map.100.refs_2_.refs_4_.refs_3_, ...), custom_call_target="tpu_custom_call" | custom-call | flops 1000 | bytes 1000 | tf_op jit(solution)/shard_map/pallas_call | solution.py:100
  40.0 2.0 %collective-permute-done.9.refs_7_ = bf16[256,768]{1,0:T(8,128)(2,1)S(1)} collective-permute-done((bf16[256,768]{1,0:T(8,128)(2,1)S(1)}, bf16[256,768]{1,0:T(8,128)(2,1)S(1)}, u32[]{:S(2)}, u32[]{:S(2)}) %collective-permute-start.9) | collective-permute-done | bytes 393248 | tf_op jit(solution)/shard_map/ppermute | solution.py:314
  43.0 2.0 %collective-permute-start.12 = (bf16[64,768]{1,0:T(8,128)(2,1)S(1)}, bf16[64,768]{1,0:T(8,128)(2,1)S(1)}, u32[]{:S(2)}, u32[]{:S(2)}) collective-permute-start(bf16[64,768]{1,0:T(8,128)(2,1)S(1)} %get-tuple-element.68), channel_id=1, source_target_pairs={{0,8},{8,0},{16,24},{24,16},{1,9},{9,1},{17,25},{25,17},{2,10},{10... | collective-permute-start | bytes 294920 | tf_op jit(solution)/shard_map/ppermute | solution.py:326
  45.1 2.6 %collective-permute-start.13 = (bf16[64,768]{1,0:T(8,128)(2,1)S(1)}, bf16[64,768]{1,0:T(8,128)(2,1)S(1)}, u32[]{:S(2)}, u32[]{:S(2)}) collective-permute-start(bf16[64,768]{1,0:T(8,128)(2,1)S(1)} %get-tuple-element.69), channel_id=1, source_target_pairs={{0,16},{8,24},{16,0},{24,8},{1,17},{9,25},{17,1},{25,9},{2,18},{10... | collective-permute-start | bytes 294920 | tf_op jit(solution)/shard_map/ppermute | solution.py:326
  48.2 7.3 %collective-permute-done.13.refs_4_ = bf16[64,768]{1,0:T(8,128)(2,1)S(1)} collective-permute-done((bf16[64,768]{1,0:T(8,128)(2,1)S(1)}, bf16[64,768]{1,0:T(8,128)(2,1)S(1)}, u32[]{:S(2)}, u32[]{:S(2)}) %collective-permute-start.13) | collective-permute-done | bytes 98336 | tf_op jit(solution)/shard_map/ppermute | solution.py:326
  56.3 1.7 %collective-permute-start.17 = (bf16[64,1152]{1,0:T(8,128)(2,1)S(1)}, bf16[64,1152]{1,0:T(8,128)(2,1)S(1)}, u32[]{:S(2)}, u32[]{:S(2)}) collective-permute-start(bf16[64,1152]{1,0:T(8,128)(2,1)S(1)} %get-tuple-element.73), channel_id=1, source_target_pairs={{0,8},{8,0},{16,24},{24,16},{1,9},{9,1},{17,25},{25,17},{2,10},{10... | collective-permute-start | bytes 442376 | tf_op jit(solution)/shard_map/ppermute | solution.py:326
  58.0 1.4 %collective-permute-start.18 = (bf16[64,1152]{1,0:T(8,128)(2,1)S(1)}, bf16[64,1152]{1,0:T(8,128)(2,1)S(1)}, u32[]{:S(2)}, u32[]{:S(2)}) collective-permute-start(bf16[64,1152]{1,0:T(8,128)(2,1)S(1)} %get-tuple-element.74), channel_id=1, source_target_pairs={{0,16},{8,24},{16,0},{24,8},{1,17},{9,25},{17,1},{25,9},{2,18},{10... | collective-permute-start | bytes 442376 | tf_op jit(solution)/shard_map/ppermute | solution.py:326
  60.8 2.4 %collective-permute-done.17.refs_3_ = bf16[64,1152]{1,0:T(8,128)(2,1)S(1)} collective-permute-done((bf16[64,1152]{1,0:T(8,128)(2,1)S(1)}, bf16[64,1152]{1,0:T(8,128)(2,1)S(1)}, u32[]{:S(2)}, u32[]{:S(2)}) %collective-permute-start.17) | collective-permute-done | bytes 147488 | tf_op jit(solution)/shard_map/ppermute | solution.py:326
  63.2 7.8 %collective-permute-done.18.refs_4_ = bf16[64,1152]{1,0:T(8,128)(2,1)S(1)} collective-permute-done((bf16[64,1152]{1,0:T(8,128)(2,1)S(1)}, bf16[64,1152]{1,0:T(8,128)(2,1)S(1)}, u32[]{:S(2)}, u32[]{:S(2)}) %collective-permute-start.18) | collective-permute-done | bytes 147488 | tf_op jit(solution)/shard_map/ppermute | solution.py:326
  73.4 8.1 %collective-permute-done.23.refs_3_ = bf16[256,768]{1,0:T(8,128)(2,1)S(1)} collective-permute-done((bf16[256,768]{1,0:T(8,128)(2,1)S(1)}, bf16[256,768]{1,0:T(8,128)(2,1)S(1)}, u32[]{:S(2)}, u32[]{:S(2)}) %collective-permute-start.23) | collective-permute-done | bytes 393248 | tf_op jit(solution)/shard_map/ppermute | solution.py:314
  82.2 2.0 %collective-permute-start.27 = (bf16[256,768]{1,0:T(8,128)(2,1)S(1)}, bf16[256,768]{1,0:T(8,128)(2,1)S(1)}, u32[]{:S(2)}, u32[]{:S(2)}) collective-permute-start(bf16[256,768]{1,0:T(8,128)(2,1)S(1)} %get-tuple-element.81.refs_6_.refs_2_), channel_id=1, source_target_pairs={{0,2},{1,5},{2,0},{3,7},{4,6},{5,1},{6,4},{7,3},{8,10},{9,13},{10,... | collective-permute-start | bytes 1179656 | tf_op jit(solution)/shard_map/ppermute | solution.py:314
  85.2 3.4 %collective-permute-start.22 = (bf16[64,384]{1,0:T(8,128)(2,1)S(1)}, bf16[64,384]{1,0:T(8,128)(2,1)S(1)}, u32[]{:S(2)}, u32[]{:S(2)}) collective-permute-start(bf16[64,384]{1,0:T(8,128)(2,1)S(1)} %get-tuple-element.80), channel_id=1, source_target_pairs={{0,24},{8,16},{16,8},{24,0},{1,25},{9,17},{17,9},{25,1},{2,26},{10... | collective-permute-start | bytes 147464 | tf_op jit(solution)/shard_map/ppermute | solution.py:326
  89.2 2.1 %collective-permute-done.22.refs_5_ = bf16[64,384]{1,0:T(8,128)(2,1)S(1)} collective-permute-done((bf16[64,384]{1,0:T(8,128)(2,1)S(1)}, bf16[64,384]{1,0:T(8,128)(2,1)S(1)}, u32[]{:S(2)}, u32[]{:S(2)}) %collective-permute-start.22) | collective-permute-done | bytes 49184 | tf_op jit(solution)/shard_map/ppermute | solution.py:326
  91.8 1.7 %collective-permute-start.24 = (bf16[256,384]{1,0:T(8,128)(2,1)S(1)}, bf16[256,384]{1,0:T(8,128)(2,1)S(1)}, u32[]{:S(2)}, u32[]{:S(2)}) collective-permute-start(bf16[256,384]{1,0:T(8,128)(2,1)S(1)} %shard_map.113.refs_2_.refs_4_), channel_id=1, source_target_pairs={{0,4},{1,3},{2,6},{3,1},{4,0},{5,7},{6,2},{7,5},{8,12},{9,11},{10,... | collective-permute-start | bytes 589832 | tf_op jit(solution)/shard_map/ppermute | solution.py:314
  93.6 4.0 %collective-permute-done.24.refs_3_ = bf16[256,384]{1,0:T(8,128)(2,1)S(1)} collective-permute-done((bf16[256,384]{1,0:T(8,128)(2,1)S(1)}, bf16[256,384]{1,0:T(8,128)(2,1)S(1)}, u32[]{:S(2)}, u32[]{:S(2)}) %collective-permute-start.24) | collective-permute-done | bytes 196640 | tf_op jit(solution)/shard_map/ppermute | solution.py:314
  99.1 1.9 %collective-permute-start.25 = (bf16[256,384]{1,0:T(8,128)(2,1)S(1)}, bf16[256,384]{1,0:T(8,128)(2,1)S(1)}, u32[]{:S(2)}, u32[]{:S(2)}) collective-permute-start(bf16[256,384]{1,0:T(8,128)(2,1)S(1)} %get-tuple-element.82.refs_6_.refs_2_), channel_id=1, source_target_pairs={{0,2},{1,5},{2,0},{3,7},{4,6},{5,1},{6,4},{7,3},{8,10},{9,13},{10,... | collective-permute-start | bytes 589832 | tf_op jit(solution)/shard_map/ppermute | solution.py:314
  101.0 3.6 %collective-permute-done.26.refs_5_ = bf16[256,384]{1,0:T(8,128)(2,1)S(1)} collective-permute-done((bf16[256,384]{1,0:T(8,128)(2,1)S(1)}, bf16[256,384]{1,0:T(8,128)(2,1)S(1)}, u32[]{:S(2)}, u32[]{:S(2)}) %collective-permute-start.26) | collective-permute-done | bytes 196640 | tf_op jit(solution)/shard_map/ppermute | solution.py:314
  104.7 2.1 %collective-permute-done.25.refs_4_ = bf16[256,384]{1,0:T(8,128)(2,1)S(1)} collective-permute-done((bf16[256,384]{1,0:T(8,128)(2,1)S(1)}, bf16[256,384]{1,0:T(8,128)(2,1)S(1)}, u32[]{:S(2)}, u32[]{:S(2)}) %collective-permute-start.25) | collective-permute-done | bytes 196640 | tf_op jit(solution)/shard_map/ppermute | solution.py:314
  107.5 8.9 %shard_map.117 = (bf16[1,2,1024,1152]{3,2,1,0:T(8,128)(2,1)}, f32[1024,1024]{1,0:T(8,128)S(1)}) custom-call(s32[4]{0:T(128)S(1)} %pad_add_fusion.refs_0_, s32[2]{0:T(128)S(1)} %copy-done.2, bf16[1024,768]{1,0:T(8,128)(2,1)S(1)} %shard_map.115.refs_6_.refs_2_, bf16[1024,768]{1,0:T(8,128)(2,1)S(1)} %collective-permute-done.30.refs_3_, ...), custom_call_target="tpu_custom_call" | custom-call | flops 1000 | bytes 1000 | tf_op jit(solution)/shard_map/pallas_call | solution.py:100
  116.4 9.4 %shard_map.118 = (bf16[1,2,1024,1152]{3,2,1,0:T(8,128)(2,1)}, bf16[1,1152,1024]{2,1,0:T(8,128)(2,1)}, f32[1,1024]{1,0:T(1,128)}) custom-call(s32[4]{0:T(128)S(1)} %pad_add_fusion.refs_0_, s32[2]{0:T(128)S(1)} %copy-done.2, bf16[1024,384]{1,0:T(8,128)(2,1)S(1)} %shard_map.116.refs_6_.refs_2_, ...), custom_call_target="tpu_custom_call", output_to_operand_aliasing={{0}: (9, {})} | custom-call | flops 1000 | bytes 1000 | tf_op jit(solution)/shard_map/pallas_call | solution.py:100
  (64 shorter events, 21.9 us)
Async XLA Ops:
  0.6 9.1 %collective-permute-start.1 = (bf16[256,1152]{1,0:T(8,128)(2,1)}, bf16[256,1152]{1,0:T(8,128)(2,1)S(1)}, u32[]{:S(2)}, u32[]{:S(2)}) collective-permute-start(bf16[256,1152]{1,0:T(8,128)(2,1)} %bitcast.5), channel_id=1, source_target_pairs={{0,1},{1,0},{2,3},{3,2},{4,5},{5,4},{6,7},{7,6},{8,9},{9,8},{10,11... | collective-permute-start | bytes 1769480 | tf_op jit(solution)/shard_map/ppermute | solution.py:302
  1.1 16.7 %collective-permute-start = (bf16[256,1152]{1,0:T(8,128)(2,1)}, bf16[256,1152]{1,0:T(8,128)(2,1)S(1)}, u32[]{:S(2)}, u32[]{:S(2)}) collective-permute-start(bf16[256,1152]{1,0:T(8,128)(2,1)} %bitcast.6), channel_id=1, source_target_pairs={{0,2},{1,3},{2,0},{3,1},{4,6},{5,7},{6,4},{7,5},{8,10},{9,11},{10,... | collective-permute-start | bytes 1769480 | tf_op jit(solution)/shard_map/ppermute | solution.py:305
  4.5 5.3 %copy-start.3 = (f32[1,1024]{1,0:T(1,128)S(1)}, f32[1,1024]{1,0:T(1,128)}, u32[]{:S(2)}) copy-start(f32[1,1024]{1,0:T(1,128)} %refs_5_.5) | copy-start | bytes 12292
  14.1 4.4 %collective-permute-start.4 = (bf16[256,1152]{1,0:T(8,128)(2,1)S(1)}, bf16[256,1152]{1,0:T(8,128)(2,1)S(1)}, u32[]{:S(2)}, u32[]{:S(2)}) collective-permute-start(bf16[256,1152]{1,0:T(8,128)(2,1)S(1)} %get-tuple-element.54), channel_id=1, source_target_pairs={{0,1},{1,0},{2,3},{3,2},{4,5},{5,4},{6,7},{7,6},{8,9},{9,8},{10,11... | collective-permute-start | bytes 1769480 | tf_op jit(solution)/shard_map/ppermute | solution.py:302
  14.3 4.2 %collective-permute-start.3 = (bf16[256,1152]{1,0:T(8,128)(2,1)S(1)}, bf16[256,1152]{1,0:T(8,128)(2,1)S(1)}, u32[]{:S(2)}, u32[]{:S(2)}) collective-permute-start(bf16[256,1152]{1,0:T(8,128)(2,1)S(1)} %get-tuple-element.51.refs_5_), channel_id=1, source_target_pairs={{0,1},{1,0},{2,3},{3,2},{4,5},{5,4},{6,7},{7,6},{8,9},{9,8},{10,11... | collective-permute-start | bytes 1769480 | tf_op jit(solution)/shard_map/ppermute | solution.py:302
  18.4 2.7 %collective-permute-start.2 = (bf16[256,1152]{1,0:T(8,128)(2,1)S(1)}, bf16[256,1152]{1,0:T(8,128)(2,1)S(1)}, u32[]{:S(2)}, u32[]{:S(2)}) collective-permute-start(bf16[256,1152]{1,0:T(8,128)(2,1)S(1)} %shard_map.98.refs_6_.refs_2_), channel_id=1, source_target_pairs={{0,1},{1,0},{2,3},{3,2},{4,5},{5,4},{6,7},{7,6},{8,9},{9,8},{10,11... | collective-permute-start | bytes 1769480 | tf_op jit(solution)/shard_map/ppermute | solution.py:302
  19.3 9.9 %collective-permute-start.7 = (bf16[256,1152]{1,0:T(8,128)(2,1)S(1)}, bf16[256,1152]{1,0:T(8,128)(2,1)S(1)}, u32[]{:S(2)}, u32[]{:S(2)}) collective-permute-start(bf16[256,1152]{1,0:T(8,128)(2,1)S(1)} %shard_map.99.refs_7_), channel_id=1, source_target_pairs={{0,2},{1,5},{2,0},{3,7},{4,6},{5,1},{6,4},{7,3},{8,10},{9,13},{10,... | collective-permute-start | bytes 1769480 | tf_op jit(solution)/shard_map/ppermute | solution.py:314
  24.8 2.1 %collective-permute-start.6 = (bf16[256,768]{1,0:T(8,128)(2,1)S(1)}, bf16[256,768]{1,0:T(8,128)(2,1)S(1)}, u32[]{:S(2)}, u32[]{:S(2)}) collective-permute-start(bf16[256,768]{1,0:T(8,128)(2,1)S(1)} %get-tuple-element.58), channel_id=1, source_target_pairs={{0,1},{1,0},{2,3},{3,2},{4,5},{5,4},{6,7},{7,6},{8,9},{9,8},{10,11... | collective-permute-start | bytes 1179656 | tf_op jit(solution)/shard_map/ppermute | solution.py:302
  25.1 2.1 %collective-permute-start.5 = (bf16[256,768]{1,0:T(8,128)(2,1)S(1)}, bf16[256,768]{1,0:T(8,128)(2,1)S(1)}, u32[]{:S(2)}, u32[]{:S(2)}) collective-permute-start(bf16[256,768]{1,0:T(8,128)(2,1)S(1)} %get-tuple-element.55.refs_4_), channel_id=1, source_target_pairs={{0,1},{1,0},{2,3},{3,2},{4,5},{5,4},{6,7},{7,6},{8,9},{9,8},{10,11... | collective-permute-start | bytes 1179656 | tf_op jit(solution)/shard_map/ppermute | solution.py:302
  30.2 11.9 %collective-permute-start.9 = (bf16[256,768]{1,0:T(8,128)(2,1)S(1)}, bf16[256,768]{1,0:T(8,128)(2,1)S(1)}, u32[]{:S(2)}, u32[]{:S(2)}) collective-permute-start(bf16[256,768]{1,0:T(8,128)(2,1)S(1)} %get-tuple-element.60), channel_id=1, source_target_pairs={{0,4},{1,3},{2,6},{3,1},{4,0},{5,7},{6,2},{7,5},{8,12},{9,11},{10,... | collective-permute-start | bytes 1179656 | tf_op jit(solution)/shard_map/ppermute | solution.py:314
  32.0 10.1 %collective-permute-start.8 = (bf16[256,768]{1,0:T(8,128)(2,1)S(1)}, bf16[256,768]{1,0:T(8,128)(2,1)S(1)}, u32[]{:S(2)}, u32[]{:S(2)}) collective-permute-start(bf16[256,768]{1,0:T(8,128)(2,1)S(1)} %get-tuple-element.59.refs_4_), channel_id=1, source_target_pairs={{0,2},{1,5},{2,0},{3,7},{4,6},{5,1},{6,4},{7,3},{8,10},{9,13},{10,... | collective-permute-start | bytes 1179656 | tf_op jit(solution)/shard_map/ppermute | solution.py:314
  34.8 1.8 %collective-permute-start.11 = (bf16[256,384]{1,0:T(8,128)(2,1)S(1)}, bf16[256,384]{1,0:T(8,128)(2,1)S(1)}, u32[]{:S(2)}, u32[]{:S(2)}) collective-permute-start(bf16[256,384]{1,0:T(8,128)(2,1)S(1)} %get-tuple-element.64), channel_id=1, source_target_pairs={{0,1},{1,0},{2,3},{3,2},{4,5},{5,4},{6,7},{7,6},{8,9},{9,8},{10,11... | collective-permute-start | bytes 589832 | tf_op jit(solution)/shard_map/ppermute | solution.py:302
  34.8 1.8 %collective-permute-start.10 = (bf16[256,384]{1,0:T(8,128)(2,1)S(1)}, bf16[256,384]{1,0:T(8,128)(2,1)S(1)}, u32[]{:S(2)}, u32[]{:S(2)}) collective-permute-start(bf16[256,384]{1,0:T(8,128)(2,1)S(1)} %get-tuple-element.61.refs_4_), channel_id=1, source_target_pairs={{0,1},{1,0},{2,3},{3,2},{4,5},{5,4},{6,7},{7,6},{8,9},{9,8},{10,11... | collective-permute-start | bytes 589832 | tf_op jit(solution)/shard_map/ppermute | solution.py:302
  37.4 10.3 %collective-permute-start.16 = (bf16[256,384]{1,0:T(8,128)(2,1)S(1)}, bf16[256,384]{1,0:T(8,128)(2,1)S(1)}, u32[]{:S(2)}, u32[]{:S(2)}) collective-permute-start(bf16[256,384]{1,0:T(8,128)(2,1)S(1)} %get-tuple-element.71), channel_id=1, source_target_pairs={{0,4},{1,3},{2,6},{3,1},{4,0},{5,7},{6,2},{7,5},{8,12},{9,11},{10,... | collective-permute-start | bytes 589832 | tf_op jit(solution)/shard_map/ppermute | solution.py:314
  37.9 9.7 %collective-permute-start.15 = (bf16[256,384]{1,0:T(8,128)(2,1)S(1)}, bf16[256,384]{1,0:T(8,128)(2,1)S(1)}, u32[]{:S(2)}, u32[]{:S(2)}) collective-permute-start(bf16[256,384]{1,0:T(8,128)(2,1)S(1)} %get-tuple-element.65.refs_8_), channel_id=1, source_target_pairs={{0,2},{1,5},{2,0},{3,7},{4,6},{5,1},{6,4},{7,3},{8,10},{9,13},{10,... | collective-permute-start | bytes 589832 | tf_op jit(solution)/shard_map/ppermute | solution.py:314
  43.0 5.1 %collective-permute-start.12 = (bf16[64,768]{1,0:T(8,128)(2,1)S(1)}, bf16[64,768]{1,0:T(8,128)(2,1)S(1)}, u32[]{:S(2)}, u32[]{:S(2)}) collective-permute-start(bf16[64,768]{1,0:T(8,128)(2,1)S(1)} %get-tuple-element.68), channel_id=1, source_target_pairs={{0,8},{8,0},{16,24},{24,16},{1,9},{9,1},{17,25},{25,17},{2,10},{10... | collective-permute-start | bytes 294920 | tf_op jit(solution)/shard_map/ppermute | solution.py:326
  45.1 10.4 %collective-permute-start.13 = (bf16[64,768]{1,0:T(8,128)(2,1)S(1)}, bf16[64,768]{1,0:T(8,128)(2,1)S(1)}, u32[]{:S(2)}, u32[]{:S(2)}) collective-permute-start(bf16[64,768]{1,0:T(8,128)(2,1)S(1)} %get-tuple-element.69), channel_id=1, source_target_pairs={{0,16},{8,24},{16,0},{24,8},{1,17},{9,25},{17,1},{25,9},{2,18},{10... | collective-permute-start | bytes 294920 | tf_op jit(solution)/shard_map/ppermute | solution.py:326
  47.7 7.8 %collective-permute-start.14 = (bf16[64,768]{1,0:T(8,128)(2,1)S(1)}, bf16[64,768]{1,0:T(8,128)(2,1)S(1)}, u32[]{:S(2)}, u32[]{:S(2)}) collective-permute-start(bf16[64,768]{1,0:T(8,128)(2,1)S(1)} %get-tuple-element.70), channel_id=1, source_target_pairs={{0,24},{8,16},{16,8},{24,0},{1,25},{9,17},{17,9},{25,1},{2,26},{10... | collective-permute-start | bytes 294920 | tf_op jit(solution)/shard_map/ppermute | solution.py:326
  56.3 6.9 %collective-permute-start.17 = (bf16[64,1152]{1,0:T(8,128)(2,1)S(1)}, bf16[64,1152]{1,0:T(8,128)(2,1)S(1)}, u32[]{:S(2)}, u32[]{:S(2)}) collective-permute-start(bf16[64,1152]{1,0:T(8,128)(2,1)S(1)} %get-tuple-element.73), channel_id=1, source_target_pairs={{0,8},{8,0},{16,24},{24,16},{1,9},{9,1},{17,25},{25,17},{2,10},{10... | collective-permute-start | bytes 442376 | tf_op jit(solution)/shard_map/ppermute | solution.py:326
  58.0 12.9 %collective-permute-start.18 = (bf16[64,1152]{1,0:T(8,128)(2,1)S(1)}, bf16[64,1152]{1,0:T(8,128)(2,1)S(1)}, u32[]{:S(2)}, u32[]{:S(2)}) collective-permute-start(bf16[64,1152]{1,0:T(8,128)(2,1)S(1)} %get-tuple-element.74), channel_id=1, source_target_pairs={{0,16},{8,24},{16,0},{24,8},{1,17},{9,25},{17,1},{25,9},{2,18},{10... | collective-permute-start | bytes 442376 | tf_op jit(solution)/shard_map/ppermute | solution.py:326
  59.4 11.5 %collective-permute-start.19 = (bf16[64,1152]{1,0:T(8,128)(2,1)S(1)}, bf16[64,1152]{1,0:T(8,128)(2,1)S(1)}, u32[]{:S(2)}, u32[]{:S(2)}) collective-permute-start(bf16[64,1152]{1,0:T(8,128)(2,1)S(1)} %get-tuple-element.75), channel_id=1, source_target_pairs={{0,24},{8,16},{16,8},{24,0},{1,25},{9,17},{17,9},{25,1},{2,26},{10... | collective-permute-start | bytes 442376 | tf_op jit(solution)/shard_map/ppermute | solution.py:326
  71.5 10.0 %collective-permute-start.23 = (bf16[256,768]{1,0:T(8,128)(2,1)S(1)}, bf16[256,768]{1,0:T(8,128)(2,1)S(1)}, u32[]{:S(2)}, u32[]{:S(2)}) collective-permute-start(bf16[256,768]{1,0:T(8,128)(2,1)S(1)} %shard_map.110.refs_6_.refs_2_), channel_id=1, source_target_pairs={{0,4},{1,3},{2,6},{3,1},{4,0},{5,7},{6,2},{7,5},{8,12},{9,11},{10,... | collective-permute-start | bytes 1179656 | tf_op jit(solution)/shard_map/ppermute | solution.py:314
  82.1 16.1 %collective-permute-start.28 = (bf16[256,768]{1,0:T(8,128)(2,1)S(1)}, bf16[256,768]{1,0:T(8,128)(2,1)S(1)}, u32[]{:S(2)}, u32[]{:S(2)}) collective-permute-start(bf16[256,768]{1,0:T(8,128)(2,1)S(1)} %get-tuple-element.84.refs_3_), channel_id=1, source_target_pairs={{0,2},{1,5},{2,0},{3,7},{4,6},{5,1},{6,4},{7,3},{8,10},{9,13},{10,... | collective-permute-start | bytes 1179656 | tf_op jit(solution)/shard_map/ppermute | solution.py:314
  82.2 16.0 %collective-permute-start.27 = (bf16[256,768]{1,0:T(8,128)(2,1)S(1)}, bf16[256,768]{1,0:T(8,128)(2,1)S(1)}, u32[]{:S(2)}, u32[]{:S(2)}) collective-permute-start(bf16[256,768]{1,0:T(8,128)(2,1)S(1)} %get-tuple-element.81.refs_6_.refs_2_), channel_id=1, source_target_pairs={{0,2},{1,5},{2,0},{3,7},{4,6},{5,1},{6,4},{7,3},{8,10},{9,13},{10,... | collective-permute-start | bytes 1179656 | tf_op jit(solution)/shard_map/ppermute | solution.py:314
  84.2 4.4 %collective-permute-start.20 = (bf16[64,384]{1,0:T(8,128)(2,1)S(1)}, bf16[64,384]{1,0:T(8,128)(2,1)S(1)}, u32[]{:S(2)}, u32[]{:S(2)}) collective-permute-start(bf16[64,384]{1,0:T(8,128)(2,1)S(1)} %get-tuple-element.78), channel_id=1, source_target_pairs={{0,8},{8,0},{16,24},{24,16},{1,9},{9,1},{17,25},{25,17},{2,10},{10... | collective-permute-start | bytes 147464 | tf_op jit(solution)/shard_map/ppermute | solution.py:326
  84.2 5.0 %collective-permute-start.21 = (bf16[64,384]{1,0:T(8,128)(2,1)S(1)}, bf16[64,384]{1,0:T(8,128)(2,1)S(1)}, u32[]{:S(2)}, u32[]{:S(2)}) collective-permute-start(bf16[64,384]{1,0:T(8,128)(2,1)S(1)} %get-tuple-element.79), channel_id=1, source_target_pairs={{0,16},{8,24},{16,0},{24,8},{1,17},{9,25},{17,1},{25,9},{2,18},{10... | collective-permute-start | bytes 147464 | tf_op jit(solution)/shard_map/ppermute | solution.py:326
  85.2 6.1 %collective-permute-start.22 = (bf16[64,384]{1,0:T(8,128)(2,1)S(1)}, bf16[64,384]{1,0:T(8,128)(2,1)S(1)}, u32[]{:S(2)}, u32[]{:S(2)}) collective-permute-start(bf16[64,384]{1,0:T(8,128)(2,1)S(1)} %get-tuple-element.80), channel_id=1, source_target_pairs={{0,24},{8,16},{16,8},{24,0},{1,25},{9,17},{17,9},{25,1},{2,26},{10... | collective-permute-start | bytes 147464 | tf_op jit(solution)/shard_map/ppermute | solution.py:326
  91.8 5.7 %collective-permute-start.24 = (bf16[256,384]{1,0:T(8,128)(2,1)S(1)}, bf16[256,384]{1,0:T(8,128)(2,1)S(1)}, u32[]{:S(2)}, u32[]{:S(2)}) collective-permute-start(bf16[256,384]{1,0:T(8,128)(2,1)S(1)} %shard_map.113.refs_2_.refs_4_), channel_id=1, source_target_pairs={{0,4},{1,3},{2,6},{3,1},{4,0},{5,7},{6,2},{7,5},{8,12},{9,11},{10,... | collective-permute-start | bytes 589832 | tf_op jit(solution)/shard_map/ppermute | solution.py:314
  98.9 8.6 %collective-permute-start.30 = (bf16[1024,768]{1,0:T(8,128)(2,1)S(1)}, bf16[1024,768]{1,0:T(8,128)(2,1)S(1)}, u32[]{:S(2)}, u32[]{:S(2)}) collective-permute-start(bf16[1024,768]{1,0:T(8,128)(2,1)S(1)} %shard_map.115.refs_6_.refs_2_), channel_id=1, source_target_pairs={{0,1},{1,0},{2,3},{3,2},{4,5},{5,4},{6,7},{7,6},{8,9},{9,8},{10,11... | collective-permute-start | bytes 4718600 | tf_op jit(solution)/shard_map/ppermute | solution.py:302
  98.9 5.7 %collective-permute-start.26 = (bf16[256,384]{1,0:T(8,128)(2,1)S(1)}, bf16[256,384]{1,0:T(8,128)(2,1)S(1)}, u32[]{:S(2)}, u32[]{:S(2)}) collective-permute-start(bf16[256,384]{1,0:T(8,128)(2,1)S(1)} %get-tuple-element.83.refs_3_), channel_id=1, source_target_pairs={{0,2},{1,5},{2,0},{3,7},{4,6},{5,1},{6,4},{7,3},{8,10},{9,13},{10,... | collective-permute-start | bytes 589832 | tf_op jit(solution)/shard_map/ppermute | solution.py:314
  99.1 7.7 %collective-permute-start.25 = (bf16[256,384]{1,0:T(8,128)(2,1)S(1)}, bf16[256,384]{1,0:T(8,128)(2,1)S(1)}, u32[]{:S(2)}, u32[]{:S(2)}) collective-permute-start(bf16[256,384]{1,0:T(8,128)(2,1)S(1)} %get-tuple-element.82.refs_6_.refs_2_), channel_id=1, source_target_pairs={{0,2},{1,5},{2,0},{3,7},{4,6},{5,1},{6,4},{7,3},{8,10},{9,13},{10,... | collective-permute-start | bytes 589832 | tf_op jit(solution)/shard_map/ppermute | solution.py:314
  107.4 9.0 %collective-permute-start.29 = (bf16[1024,384]{1,0:T(8,128)(2,1)S(1)}, bf16[1024,384]{1,0:T(8,128)(2,1)S(1)}, u32[]{:S(2)}, u32[]{:S(2)}) collective-permute-start(bf16[1024,384]{1,0:T(8,128)(2,1)S(1)} %shard_map.116.refs_6_.refs_2_), channel_id=1, source_target_pairs={{0,1},{1,0},{2,3},{3,2},{4,5},{5,4},{6,7},{7,6},{8,9},{9,8},{10,11... | collective-permute-start | bytes 2359304 | tf_op jit(solution)/shard_map/ppermute | solution.py:302
  (3 other events, 8.6 us)

commit v4 on v3

--- a/solution.py
+++ b/solution.py
@@ -59,6 +59,7 @@
 VMEM_MIB = 16
 FEATURE_BLOCK = 512
 ROWS_UNIT = 128
+HEAVY = 10**11
 SIDE, CORE, FEAT, LAYER = range(4)
 HELD = pl.BlockSpec(memory_space=pltpu.VMEM)
 ANYWHERE = pl.BlockSpec(memory_space=pl.ANY)
@@ -84,33 +85,46 @@
     def __init__(self, scalars):
         self.scalars = scalars
         self.last = None
+        self.keep = []
 
     def __call__(
-        self, kernel, operands, outs, specs=None, out_specs=None, grid=(1,), scratch=(), aliases=()
+        self,
+        kernel,
+        operands,
+        outs,
+        specs=None,
+        out_specs=None,
+        grid=(1,),
+        scratch=(),
+        aliases=(),
+        heavy=False,
     ):
         count = len(operands)
         operands = list(operands)
         specs = list(specs or [HELD] * count)
         waits = [] if self.last is None else [self.last]
+        keep = [k for k in self.keep if all(k is not o for o in operands)]
 
         def body(*refs):
             at = len(self.scalars) + count
-            kernel(*refs[:at], *refs[at + len(waits) :])
+            kernel(*refs[:at], *refs[at + len(waits) + len(keep) :])
 
         results = pl.pallas_call(
             body,
             grid_spec=pltpu.PrefetchScalarGridSpec(
                 num_scalar_prefetch=len(self.scalars),
                 grid=grid,
-                in_specs=specs + [ANYWHERE] * len(waits),
+                in_specs=specs + [ANYWHERE] * len(waits) + [HELD] * len(keep),
                 out_specs=list(out_specs or [HELD] * len(outs)),
                 scratch_shapes=list(scratch),
             ),
             out_shape=list(outs),
             input_output_aliases={len(self.scalars) + i: o for i, o in aliases},
             compiler_params=pltpu.CompilerParams(vmem_limit_bytes=VMEM_MIB * 1024 * 1024),
-            cost_estimate=pl.CostEstimate(flops=1000, bytes_accessed=1000, transcendentals=0),
-        )(*self.scalars, *operands, *waits)
+            cost_estimate=pl.CostEstimate(
+                flops=HEAVY if heavy else 1000, bytes_accessed=1000, transcendentals=0
+            ),
+        )(*self.scalars, *operands, *waits, *keep)
         self.last = results[0]
         return results
 
@@ -149,6 +163,7 @@
         [held(o.shape, o.dtype) for o in operands],
         specs=[pl.BlockSpec(memory_space=pltpu.HBM)] * len(operands),
         scratch=[pltpu.SemaphoreType.DMA((len(parts),))],
+        heavy=True,
     )
 
 
@@ -169,6 +184,7 @@
         [*parts, readin, offset, cutoff],
         [held((count, readin.shape[-1]), BF)],
         scratch=[pltpu.VMEM((count, width), BF)],
+        heavy=not near,
     )[0]
 
 
@@ -190,27 +206,42 @@
     )
 
 
-def decode(order, away, act, writeout, hidden, lo, hi):
+def decode_near(order, away, act, writeout, hidden):
     count, features = act.shape
     blocks = 2
     rows = count // blocks
     dtype = BF if away else F32
 
-    def kernel(w, d, act_ref, weight_ref, *rest):
+    def kernel(w, d, act_ref, weight_ref, hidden_ref, *outs):
         target = 1 - w[CORE] if away else w[CORE]
         live = jnp.where(w[LAYER] <= d[target], 1.0, 0.0)
-        out = jnp.dot(act_ref[...], weight_ref[0, target, :, lo:hi], preferred_element_type=F32)
-        parts = [out[b * rows : (b + 1) * rows] for b in range(blocks)]
-        if hidden is not None:
-            less = rest[0][target, :, lo:hi].astype(F32)
-            owner = jnp.logical_and(w[LAYER] == 0, w[FEAT] == 0)
-            mine = [jnp.logical_and(owner, w[CORE] == b) for b in range(blocks)]
-            parts = [p - jnp.where(m, 1.0, 0.0) * less for p, m in zip(parts, mine)]
-        for ref, part in zip(rest[-blocks:], parts):
-            ref[...] = (part * live).astype(dtype)
-
-    operands = [act, writeout] + ([] if hidden is None else [hidden])
-    return order(kernel, operands, [held((rows, hi - lo), dtype)] * blocks)
+        out = jnp.dot(act_ref[...], weight_ref[0, target], preferred_element_type=F32)
+        less = hidden_ref[target].astype(F32)
+        owner = jnp.logical_and(w[LAYER] == 0, w[FEAT] == 0)
+        for b, ref in enumerate(outs):
+            mine = jnp.where(jnp.logical_and(owner, w[CORE] == b), 1.0, 0.0)
+            ref[...] = ((out[b * rows : (b + 1) * rows] - mine * less) * live).astype(dtype)
+
+    outs = [held((rows, writeout.shape[-1]), dtype)] * blocks
+    return order(kernel, [act, writeout, hidden], outs)
+
+
+def decode_far(order, away, other, act, writeout, cuts, heavy=False):
+    count, features = act.shape
+    rows = count // 2
+    part = rows // cuts
+    dtype = BF if away else F32
+
+    def kernel(w, d, act_ref, weight_ref, *outs):
+        target = 1 - w[CORE] if away else w[CORE]
+        live = jnp.where(w[LAYER] <= d[target], 1.0, 0.0)
+        block = act_ref[span(1 - w[FEAT] if other else w[FEAT], rows), :]
+        out = jnp.dot(block, weight_ref[0, target], preferred_element_type=F32) * live
+        for k, ref in enumerate(outs):
+            ref[...] = out[k * part : (k + 1) * part].astype(dtype)
+
+    outs = [held((part, writeout.shape[-1]), dtype)] * cuts
+    return order(kernel, [act, writeout], outs, heavy=heavy)
 
 
 def gradients(order, scaled, turned, writeout, lo, hi, sens=None, dec=None, last=None):
@@ -339,92 +370,85 @@
     readin, cutoff, writeout, hidden = load(order, readin, cutoff, writeout, hidden)
     act_near = encode(order, True, (own, near), readin, offset, cutoff)
 
-    def partials(act, hidden, lo, hi):
-        away = decode(order, True, act, writeout, hidden, lo, hi)
-        got = [to_core(a) for a in away]
-        return (*decode(order, False, act, writeout, hidden, lo, hi), *got)
-
-    here = partials(act_near, hidden, 0, width)
+    away = decode_near(order, True, act_near, writeout, hidden)
+    here_got = [to_core(a) for a in away]
+    here = [*decode_near(order, False, act_near, writeout, hidden), *here_got]
     far = order.pass_on(far)
 
-    def first_kernel(w, d, kept0, kept1, got0, got1, out):
-        other = pick(w[FEAT] == 1, kept0[...], kept1[...])
-        out[...] = (other + pick(w[FEAT] == 1, got0[...], got1[...]).astype(F32)).astype(BF)
-
-    send = order(first_kernel, here, [held((rows, width), BF)])[0]
-    got_first = to_first(send)
+    def first_kernel(w, d, kept0, kept1, got0, got1, *outs):
+        y1 = w[FEAT] == 1
+        other = pick(y1, kept0[...], kept1[...]) + pick(y1, got0[...], got1[...]).astype(F32)
+        for (lo, hi), out in zip(chunks, outs):
+            out[...] = other[:, lo:hi].astype(BF)
+
+    sends = order(first_kernel, here, [held((rows, hi - lo), BF) for lo, hi in chunks])
+    got_first = [to_first(send) for send in sends]
 
     far_near = to_core(far)
     act_far = encode(order, False, (far, far_near), readin, offset, cutoff)
 
-    def reduce_sides(lo, hi):
+    def far_block(other, cuts):
+        away = decode_far(order, True, other, act_far, writeout, cuts)
+        got = [to_core(a) for a in away]
+        return (*decode_far(order, False, other, act_far, writeout, 1), *got)
+
+    def joined_rows(refs, at):
+        return jnp.concatenate([ref[:, at] for ref in refs]).astype(F32)
+
+    there_other = far_block(True, 2)
+
+    def reduce_sides(lo, hi, got_first, heavy):
         size = hi - lo
-        there = partials(act_far, None, lo, hi)
-
-        def second_kernel(
-            w, d, hk0, hk1, hg0, hg1, tk0, tk1, tg0, tg1, first, out_first, out_second
-        ):
+        at = slice(lo, hi)
+
+        def second_kernel(w, d, hk0, hk1, hg0, hg1, first, tk, *refs):
+            *tg, out_first, out_second = refs
             y0 = w[FEAT] == 0
-            here_y = pick(y0, hk0[:, lo:hi], hk1[:, lo:hi])
-            here_y += pick(y0, hg0[:, lo:hi], hg1[:, lo:hi]).astype(F32)
-            there_other = pick(y0, tk1[...], tk0[...])
-            there_other += pick(y0, tg1[...], tg0[...]).astype(F32)
+            here_y = pick(y0, hk0[:, at], hk1[:, at])
+            here_y += pick(y0, hg0[:, at], hg1[:, at]).astype(F32)
+            there_other = tk[:, at] + joined_rows(tg, at)
             zero = w[CORE] == 0
             out_first[...] = pick(zero, here_y, there_other).astype(BF)
-            rest = pick(zero, there_other, here_y) + first[:, lo:hi].astype(F32)
+            rest = pick(zero, there_other, here_y) + first[...].astype(F32)
             out_second[...] = rest.astype(BF)
 
-        sends = order(second_kernel, (*here, *there, got_first), [held((rows, size), BF)] * 2)
-        return there, to_first(sends[0]), to_second(sends[1])
-
-    def exchange(previous, reduced):
-        ahead = 0 if previous is None else previous[0].shape[1]
-        behind = 0 if previous is None else previous[1][0].shape[1] - ahead
-        size = 0 if reduced is None else reduced[2].shape[1]
+        operands = (*here, got_first, *there_other)
+        sends = order(second_kernel, operands, [held((rows, size), BF)] * 2, heavy=heavy)
+        return lo, hi, to_first(sends[0]), to_second(sends[1])
+
+    def send_pieces(lo, hi, got, got_second, heavy):
+        size = hi - lo
 
         def kernel(w, d, *refs):
-            refs = list(refs)
-            if previous is not None:
-                value = refs.pop(0)[...]
-                for _ in previous[1]:
-                    value = value + refs.pop(0)[:, behind:].astype(F32)
-                value = (value * inverse).astype(BF)
-            if reduced is not None:
-                tk0, tk1, tg0, tg1, first, second = (refs.pop(0) for _ in range(6))
-                kept = refs.pop()
-                y0 = w[FEAT] == 0
-                kept[...] = (
-                    pick(y0, tk0[...], tk1[...])
-                    + pick(y0, tg0[...], tg1[...]).astype(F32)
-                    + first[...].astype(F32)
-                    + second[...].astype(F32)
-                )
-            if previous is not None:
-                refs.pop(0)[...] = value
-            if reduced is not None:
-                refs.pop(0)[...] = kept[span(w[LAYER], piece), :]
-            for s, out in enumerate(refs, 1):
-                if previous is not None:
-                    out[:, :ahead] = value
-                if reduced is not None:
-                    goal = layer_goal(w[LAYER], s)
-                    out[:, ahead:] = kept[span(goal, piece), :].astype(BF)
-
-        operands, outs, scratch = [], [], []
-        if previous is not None:
-            operands += [previous[0], *previous[1]]
-            outs.append(held((piece, ahead), BF))
-        if reduced is not None:
-            there, got, got_second = reduced
-            operands += [*there, got, got_second]
-            outs.append(held((piece, size), F32))
-            scratch.append(pltpu.VMEM((rows, size), F32))
-        mine = len(outs)
-        outs += [held((piece, ahead + size), BF)] * (layers - 1)
-        results = order(kernel, operands, outs, scratch=scratch)
-        came = [to_layer(out, s) for s, out in enumerate(results[mine:], 1)]
-        scaled = None if previous is None else results[0]
-        return scaled, None if reduced is None else results[mine - 1], came
+            tk, *tg = refs[: len(there)]
+            first, second, mine, *outs, kept = refs[len(there) :]
+            kept[...] = (
+                tk[:, lo:hi]
+                + joined_rows(tg, slice(lo, hi))
+                + first[...].astype(F32)
+                + second[...].astype(F32)
+            )
+            mine[...] = kept[span(w[LAYER], piece), :]
+            for s, out in enumerate(outs, 1):
+                out[...] = kept[span(layer_goal(w[LAYER], s), piece), :].astype(BF)
+
+        outs = [held((piece, size), F32)] + [held((piece, size), BF)] * (layers - 1)
+        scratch = [pltpu.VMEM((rows, size), F32)]
+        mine, *outs = order(
+            kernel, (*there, got, got_second), outs, scratch=scratch, heavy=heavy
+        )
+        return mine, [to_layer(out, s) for s, out in enumerate(outs, 1)]
+
+    def scale_piece(mine, pieces):
+        def kernel(w, d, mine_ref, *refs):
+            *refs, out = refs
+            value = mine_ref[...]
+            for ref in refs:
+                value = value + ref[...].astype(F32)
+            out[...] = (value * inverse).astype(BF)
+
+        scaled = order(kernel, (mine, *pieces), [held(mine.shape, BF)], heavy=True)[0]
+        return scaled, [to_layer(scaled, s) for s in range(1, layers)]
 
     def join_pieces(scaled, pieces):
         size = scaled.shape[1]
@@ -433,9 +457,9 @@
             *refs, out = refs
             out[span(w[LAYER], piece), :] = refs[0][...]
             for s, ref in enumerate(refs[1:], 1):
-                out[span(layer_source(w[LAYER], s), piece), :] = ref[:, :size]
-
-        done = order(kernel, (scaled, *pieces), [held((rows, size), BF)])[0]
+                out[span(layer_source(w[LAYER], s), piece), :] = ref[...]
+
+        done = order(kernel, (scaled, *pieces), [held((rows, size), BF)], heavy=True)[0]
         return done, to_second(done)
 
     def join_pair(done, got):
@@ -444,7 +468,7 @@
             out0[...] = pick(done_last, got_ref[...], done_ref[...])
             out1[...] = pick(done_last, done_ref[...], got_ref[...])
 
-        pair = order(kernel, (done, got), [held(done.shape, BF)] * 2)
+        pair = order(kernel, (done, got), [held(done.shape, BF)] * 2, heavy=True)
         return pair, [to_first(block) for block in pair]
 
     def join_all(pair, got):
@@ -461,22 +485,21 @@
                 out[span(number, rows), :] = ref[...] * live
 
         size = pair[0].shape[1]
-        full = order(kernel, (*pair, *got), [held((total, size), BF)])[0]
+        full = order(kernel, (*pair, *got), [held((total, size), BF)], heavy=True)[0]
         return full, to_core(full)
 
-    reduced = [reduce_sides(lo, hi) for lo, hi in chunks]
+    reduced = [
+        reduce_sides(*chunk, got, k > 0) for k, (chunk, got) in enumerate(zip(chunks, got_first))
+    ]
+    there = far_block(False, 4)
     turned, tokens = turn(order, (act_near, act_far), ((own, near), (far, far_near)))
-    scaled, mine, came = exchange(None, reduced[0])
-    pairs = []
-    joined = None
-    for k in range(len(chunks)):
-        scaled, mine, then = exchange((mine, came), (reduced + [None])[k + 1])
-        if joined is not None:
-            pairs.append(join_pair(*joined))
-        came = then
-        joined = join_pieces(scaled, came)
-    pairs.append(join_pair(*joined))
-    scaled = [join_all(*pair) for pair in pairs]
+    order.keep = [writeout, cutoff, turned, tokens]
+    stages = [send_pieces(*r, k > 0) for k, r in enumerate(reduced)]
+    stages = [scale_piece(*stage) for stage in stages]
+    stages = [join_pieces(*stage) for stage in stages]
+    stages = [join_pair(*stage) for stage in stages]
+    scaled = [join_all(*stage) for stage in stages]
+    order.keep = []
     sens = dec = None
     for k, (lo, hi) in enumerate(chunks):
         last = (cutoff, tokens) if k == len(chunks) - 1 else None

time: 126 us -> 117 us (0.929)
  waiting for transfers between devices: 43.9 us -> 26.8 us
  starting transfers between devices: 31.7 us -> 39.4 us
    ppermute x9 -> x12, waiting for transfers between devices: 20.7 us -> 5.22 us  [to_layer(): lax.ppermute(a, 'layer', [(l, l ^ s if binary else (l + s) % layers) for...]
    ppermute x9 -> x12, starting transfers between devices: 13.5 us -> 20.7 us  [to_layer(): lax.ppermute(a, 'layer', [(l, l ^ s if binary else (l + s) % layers) for...]
    ppermute x11 -> x12, waiting for transfers between devices: 21.9 us -> 19.7 us  [mixed(): return lambda a: lax.ppermute(a, ('feat', 'tok'), pairs)]
    ppermute x11 -> x12, starting transfers between devices: 13.3 us -> 13.6 us  [mixed(): return lambda a: lax.ppermute(a, ('feat', 'tok'), pairs)]
    pallas_call x25 -> x26, Pallas kernels: 48.4 us -> 48.6 us  [__call__(): pl.pallas_call(body, grid_spec=pltpu.PrefetchScalarGridSpec(num_scalar_pr...]
    ppermute x10 -> x12, starting transfers between devices: 2.45 us -> 2.53 us  [to_core(): return lax.ppermute(a, 'tok', [(t, t ^ 1) for t in range(toks)])]
  transfers between devices with their start and end apart: 31 -> 37, of which waited for: 14 -> 14; matrix products, arithmetic and copies ran while one was open for 0% -> 0% of each run, Pallas kernels for 28% -> 34%
where the time goes in v4:
time: 117 us
  Pallas kernels  48.6 us (42%)
  starting transfers between devices  39.4 us (34%)
  waiting for transfers between devices  26.8 us (23%)
    pallas_call x26, Pallas kernels, __call__(): pl.pallas_call(body, grid_spec=pltpu.PrefetchScalarGridSpec(num_scalar_pr...  48.6 us
    ppermute x12, starting transfers between devices, to_layer(): lax.ppermute(a, 'layer', [(l, l ^ s if binary else (l + s) % layers) for...  20.7 us
    ppermute x12, waiting for transfers between devices, mixed(): return lambda a: lax.ppermute(a, ('feat', 'tok'), pairs)  19.7 us
    ppermute x12, starting transfers between devices, mixed(): return lambda a: lax.ppermute(a, ('feat', 'tok'), pairs)  13.6 us
    ppermute x12, waiting for transfers between devices, to_layer(): lax.ppermute(a, 'layer', [(l, l ^ s if binary else (l + s) % layers) for...  5.22 us
    ppermute x1, starting transfers between devices, to_side(): return lax.ppermute(a, 'tok', [(t, t ^ 2) for t in range(toks)])  2.57 us
    ppermute x12, starting transfers between devices, to_core(): return lax.ppermute(a, 'tok', [(t, t ^ 1) for t in range(toks)])  2.53 us
  transfers between devices with their start and end apart: 37, of which 14 were waited for; matrix products, arithmetic and copies ran while one was open for 0% of the time, Pallas kernels for 34%

profile of v4, /device:TPU:0, one launch (start us, length us, event | category | flops | bytes accessed | tf_op | source)
XLA Modules:
  0.0 116.5 jit_solution(14462568884824781850)
XLA Ops:
  1.1 2.6 %collective-permute-start = (bf16[256,1152]{1,0:T(8,128)(2,1)}, bf16[256,1152]{1,0:T(8,128)(2,1)S(1)}, u32[]{:S(2)}, u32[]{:S(2)}) collective-permute-start(bf16[256,1152]{1,0:T(8,128)(2,1)} %bitcast.6), channel_id=1, source_target_pairs={{0,2},{1,3},{2,0},{3,1},{4,6},{5,7},{6,4},{7,5},{8,10},{9,11},{10,... | collective-permute-start | bytes 1769480 | tf_op jit(solution)/shard_map/ppermute | solution.py:336
  4.5 5.3 %shard_map.94 = (bf16[1,1152,1024]{2,1,0:T(8,128)(2,1)S(1)}, s32[1,1024,1024]{2,1,0:T(8,128)S(1)}, bf16[1,2,1024,1152]{3,2,1,0:T(8,128)(2,1)S(1)}, bf16[2,256,1152]{2,1,0:T(8,128)(2,1)S(1)}) custom-call(s32[4]{0:T(128)S(1)} %pad_add_fusion.refs_0_, s32[2]{0:T(128)S(1)} %copy-done.4, bf16[1,1152,1024]{2,1,0:T(8,128)(2,1)} %refs_2_.1, ...), custom_call_target="tpu_custom_call" | custom-call | flops 99999997952 | bytes 1000 | tf_op jit(solution)/shard_map/pallas_call | solution.py:112
  9.8 2.2 %shard_map.95.refs_2_.refs_5_ = bf16[512,1024]{1,0:T(8,128)(2,1)S(1)} custom-call(s32[4]{0:T(128)S(1)} %pad_add_fusion.refs_0_, s32[2]{0:T(128)S(1)} %copy-done.5, bf16[256,1152]{1,0:T(8,128)(2,1)S(1)} %bitcast.7, bf16[256,1152]{1,0:T(8,128)(2,1)S(1)} %collective-permute-done.1.refs_3_.refs_5_, bf16[1,1152,1024]{2,1,0:T(8,128)(2,1)S(1)} %get-tuple-element.42.refs_4_.refs_7_, ...), custom_call_target="tpu_custom_call" | custom-call | flops 1000 | bytes 1000 | tf_op jit(solution)/shard_map/pallas_call | solution.py:112
  12.0 2.1 %shard_map.96 = (bf16[256,1152]{1,0:T(8,128)(2,1)S(1)}, bf16[256,1152]{1,0:T(8,128)(2,1)S(1)}) custom-call(s32[4]{0:T(128)S(1)} %pad_add_fusion.refs_0_, s32[2]{0:T(128)S(1)} %copy-done.5, bf16[512,1024]{1,0:T(8,128)(2,1)S(1)} %shard_map.95.refs_2_.refs_5_, bf16[1,2,1024,1152]{3,2,1,0:T(8,128)(2,1)S(1)} %get-tuple-element.44.refs_3_.refs_10_.refs_7_.refs_5_, ...), custom_call_target="tpu_custom_call" | custom-call | flops 1000 | bytes 1000 | tf_op jit(solution)/shard_map/pallas_call | solution.py:112
  14.7 2.1 %shard_map.97 = (f32[256,1152]{1,0:T(8,128)S(1)}, f32[256,1152]{1,0:T(8,128)S(1)}) custom-call(s32[4]{0:T(128)S(1)} %pad_add_fusion.refs_0_, s32[2]{0:T(128)S(1)} %copy-done.5, bf16[512,1024]{1,0:T(8,128)(2,1)S(1)} %shard_map.95.refs_2_.refs_5_, bf16[1,2,1024,1152]{3,2,1,0:T(8,128)(2,1)S(1)} %get-tuple-element.44.refs_3_.refs_10_.refs_7_.refs_5_, ...), custom_call_target="tpu_custom_call" | custom-call | flops 1000 | bytes 1000 | tf_op jit(solution)/shard_map/pallas_call | solution.py:112
  19.2 1.8 %collective-permute-start.8 = (bf16[256,768]{1,0:T(8,128)(2,1)S(1)}, bf16[256,768]{1,0:T(8,128)(2,1)S(1)}, u32[]{:S(2)}, u32[]{:S(2)}) collective-permute-start(bf16[256,768]{1,0:T(8,128)(2,1)S(1)} %get-tuple-element.50.refs_7_), channel_id=1, source_target_pairs={{0,2},{1,5},{2,0},{3,7},{4,6},{5,1},{6,4},{7,3},{8,10},{9,13},{10,... | collective-permute-start | bytes 1179656 | tf_op jit(solution)/shard_map/ppermute | solution.py:345
  21.1 2.2 %shard_map.100.refs_2_.refs_4_.refs_3_ = bf16[512,1024]{1,0:T(8,128)(2,1)S(1)} custom-call(s32[4]{0:T(128)S(1)} %pad_add_fusion.refs_0_, s32[2]{0:T(128)S(1)} %copy-done.5, bf16[256,1152]{1,0:T(8,128)(2,1)S(1)} %shard_map.98.refs_6_.refs_2_, bf16[256,1152]{1,0:T(8,128)(2,1)S(1)} %collective-permute-done.2.refs_3_.refs_7_, ...), custom_call_target="tpu_custom_call" | custom-call | flops 99999997952 | bytes 1000 | tf_op jit(solution)/shard_map/pallas_call | solution.py:112
  23.3 1.4 %shard_map.101 = (bf16[128,1152]{1,0:T(8,128)(2,1)S(1)}, bf16[128,1152]{1,0:T(8,128)(2,1)S(1)}) custom-call(s32[4]{0:T(128)S(1)} %pad_add_fusion.refs_0_, s32[2]{0:T(128)S(1)} %copy-done.5, bf16[512,1024]{1,0:T(8,128)(2,1)S(1)} %shard_map.100.refs_2_.refs_4_.refs_3_, bf16[1,2,1024,1152]{3,2,1,0:T(8,128)(2,1)S(1)} %get-tuple-element.44.refs_3_.refs_10_.refs_7_.refs_5_, ...), custom_call_target="tpu_custom_call" | custom-call | flops 1000 | bytes 1000 | tf_op jit(solution)/shard_map/pallas_call | solution.py:112
  25.2 1.3 %collective-permute-start.5 = (bf16[256,384]{1,0:T(8,128)(2,1)S(1)}, bf16[256,384]{1,0:T(8,128)(2,1)S(1)}, u32[]{:S(2)}, u32[]{:S(2)}) collective-permute-start(bf16[256,384]{1,0:T(8,128)(2,1)S(1)} %get-tuple-element.51), channel_id=1, source_target_pairs={{0,2},{1,5},{2,0},{3,7},{4,6},{5,1},{6,4},{7,3},{8,10},{9,13},{10,... | collective-permute-start | bytes 589832 | tf_op jit(solution)/shard_map/ppermute | solution.py:345
  26.5 1.4 %shard_map.102.refs_7_.refs_10_ = f32[256,1152]{1,0:T(8,128)S(1)} custom-call(s32[4]{0:T(128)S(1)} %pad_add_fusion.refs_0_, s32[2]{0:T(128)S(1)} %copy-done.5, bf16[512,1024]{1,0:T(8,128)(2,1)S(1)} %shard_map.100.refs_2_.refs_4_.refs_3_, bf16[1,2,1024,1152]{3,2,1,0:T(8,128)(2,1)S(1)} %get-tuple-element.44.refs_3_.refs_10_.refs_7_.refs_5_, ...), custom_call_target="tpu_custom_call" | custom-call | flops 1000 | bytes 1000 | tf_op jit(solution)/shard_map/pallas_call | solution.py:112
  28.9 1.4 %collective-permute-start.16 = (bf16[256,768]{1,0:T(8,128)(2,1)S(1)}, bf16[256,768]{1,0:T(8,128)(2,1)S(1)}, u32[]{:S(2)}, u32[]{:S(2)}) collective-permute-start(bf16[256,768]{1,0:T(8,128)(2,1)S(1)} %get-tuple-element.61), channel_id=1, source_target_pairs={{0,4},{1,3},{2,6},{3,1},{4,0},{5,7},{6,2},{7,5},{8,12},{9,11},{10,... | collective-permute-start | bytes 1179656 | tf_op jit(solution)/shard_map/ppermute | solution.py:345
  32.1 1.4 %shard_map.105 = (bf16[64,1152]{1,0:T(8,128)(2,1)S(1)}, bf16[64,1152]{1,0:T(8,128)(2,1)S(1)}, bf16[64,1152]{1,0:T(8,128)(2,1)S(1)}, bf16[64,1152]{1,0:T(8,128)(2,1)S(1)}) custom-call(s32[4]{0:T(128)S(1)} %pad_add_fusion.refs_0_, s32[2]{0:T(128)S(1)} %copy-done.5, bf16[512,1024]{1,0:T(8,128)(2,1)S(1)} %shard_map.100.refs_2_.refs_4_.refs_3_, ...), custom_call_target="tpu_custom_call" | custom-call | flops 1000 | bytes 1000 | tf_op jit(solution)/shard_map/pallas_call | solution.py:112
  34.9 1.2 %collective-permute-start.14 = (bf16[256,384]{1,0:T(8,128)(2,1)S(1)}, bf16[256,384]{1,0:T(8,128)(2,1)S(1)}, u32[]{:S(2)}, u32[]{:S(2)}) collective-permute-start(bf16[256,384]{1,0:T(8,128)(2,1)S(1)} %get-tuple-element.60), channel_id=1, source_target_pairs={{0,4},{1,3},{2,6},{3,1},{4,0},{5,7},{6,2},{7,5},{8,12},{9,11},{10,... | collective-permute-start | bytes 589832 | tf_op jit(solution)/shard_map/ppermute | solution.py:345
  37.2 1.4 %shard_map.106.refs_8_.refs_2_ = f32[256,1152]{1,0:T(8,128)S(1)} custom-call(s32[4]{0:T(128)S(1)} %pad_add_fusion.refs_0_, s32[2]{0:T(128)S(1)} %copy-done.5, bf16[512,1024]{1,0:T(8,128)(2,1)S(1)} %shard_map.100.refs_2_.refs_4_.refs_3_, bf16[1,2,1024,1152]{3,2,1,0:T(8,128)(2,1)S(1)} %get-tuple-element.44.refs_3_.refs_10_.refs_7_.refs_5_, ...), custom_call_target="tpu_custom_call" | custom-call | flops 1000 | bytes 1000 | tf_op jit(solution)/shard_map/pallas_call | solution.py:112
  38.6 1.8 %shard_map.107 = (bf16[1024,1024]{1,0:T(8,128)(2,1)S(1)}, bf16[1152,1024]{1,0:T(8,128)(2,1)S(1)}) custom-call(s32[4]{0:T(128)S(1)} %pad_add_fusion.refs_0_, s32[2]{0:T(128)S(1)} %copy-done.5, bf16[512,1024]{1,0:T(8,128)(2,1)S(1)} %copy-done.1, bf16[512,1024]{1,0:T(8,128)(2,1)S(1)} %shard_map.100.refs_2_.refs_4_.refs_3_, bf16[256,1152]{1,0:T(8,128)(2,1)S(1)} %bitcast.8, ...), custom_call_target="tpu_custom_call" | custom-call | flops 1000 | bytes 1000 | tf_op jit(solution)/shard_map/pallas_call | solution.py:112
  40.9 1.2 collective-permute-done.15.refs_7_
  42.9 1.6 %collective-permute-start.20 = (bf16[64,768]{1,0:T(8,128)(2,1)S(1)}, bf16[64,768]{1,0:T(8,128)(2,1)S(1)}, u32[]{:S(2)}, u32[]{:S(2)}) collective-permute-start(bf16[64,768]{1,0:T(8,128)(2,1)S(1)} %get-tuple-element.69), channel_id=1, source_target_pairs={{0,8},{8,0},{16,24},{24,16},{1,9},{9,1},{17,25},{25,17},{2,10},{10... | collective-permute-start | bytes 294920 | tf_op jit(solution)/shard_map/ppermute | solution.py:357
  44.6 2.6 %collective-permute-start.21 = (bf16[64,768]{1,0:T(8,128)(2,1)S(1)}, bf16[64,768]{1,0:T(8,128)(2,1)S(1)}, u32[]{:S(2)}, u32[]{:S(2)}) collective-permute-start(bf16[64,768]{1,0:T(8,128)(2,1)S(1)} %get-tuple-element.70), channel_id=1, source_target_pairs={{0,16},{8,24},{16,0},{24,8},{1,17},{9,25},{17,1},{25,9},{2,18},{10... | collective-permute-start | bytes 294920 | tf_op jit(solution)/shard_map/ppermute | solution.py:357
  48.8 3.5 %collective-permute-start.18 = (bf16[64,384]{1,0:T(8,128)(2,1)S(1)}, bf16[64,384]{1,0:T(8,128)(2,1)S(1)}, u32[]{:S(2)}, u32[]{:S(2)}) collective-permute-start(bf16[64,384]{1,0:T(8,128)(2,1)S(1)} %get-tuple-element.67), channel_id=1, source_target_pairs={{0,16},{8,24},{16,0},{24,8},{1,17},{9,25},{17,1},{25,9},{2,18},{10... | collective-permute-start | bytes 147464 | tf_op jit(solution)/shard_map/ppermute | solution.py:357
  52.6 3.4 %collective-permute-done.21.refs_4_ = bf16[64,768]{1,0:T(8,128)(2,1)S(1)} collective-permute-done((bf16[64,768]{1,0:T(8,128)(2,1)S(1)}, bf16[64,768]{1,0:T(8,128)(2,1)S(1)}, u32[]{:S(2)}, u32[]{:S(2)}) %collective-permute-start.21) | collective-permute-done | bytes 98336 | tf_op jit(solution)/shard_map/ppermute | solution.py:357
  56.6 4.5 %collective-permute-start.28 = (bf16[64,768]{1,0:T(8,128)(2,1)S(1)}, bf16[64,768]{1,0:T(8,128)(2,1)S(1)}, u32[]{:S(2)}, u32[]{:S(2)}) collective-permute-start(bf16[64,768]{1,0:T(8,128)(2,1)S(1)} %shard_map.110.refs_6_.refs_2_), channel_id=1, source_target_pairs={{0,24},{8,16},{16,8},{24,0},{1,25},{9,17},{17,9},{25,1},{2,26},{10... | collective-permute-start | bytes 294920 | tf_op jit(solution)/shard_map/ppermute | solution.py:357
  61.1 2.3 %collective-permute-start.27 = (bf16[64,768]{1,0:T(8,128)(2,1)S(1)}, bf16[64,768]{1,0:T(8,128)(2,1)S(1)}, u32[]{:S(2)}, u32[]{:S(2)}) collective-permute-start(bf16[64,768]{1,0:T(8,128)(2,1)S(1)} %shard_map.110.refs_6_.refs_2_), channel_id=1, source_target_pairs={{0,16},{8,24},{16,0},{24,8},{1,17},{9,25},{17,1},{25,9},{2,18},{10... | collective-permute-start | bytes 294920 | tf_op jit(solution)/shard_map/ppermute | solution.py:357
  64.5 2.4 %collective-permute-start.25 = (bf16[64,384]{1,0:T(8,128)(2,1)S(1)}, bf16[64,384]{1,0:T(8,128)(2,1)S(1)}, u32[]{:S(2)}, u32[]{:S(2)}) collective-permute-start(bf16[64,384]{1,0:T(8,128)(2,1)S(1)} %shard_map.111.refs_6_.refs_2_), channel_id=1, source_target_pairs={{0,24},{8,16},{16,8},{24,0},{1,25},{9,17},{17,9},{25,1},{2,26},{10... | collective-permute-start | bytes 147464 | tf_op jit(solution)/shard_map/ppermute | solution.py:357
  67.6 1.4 %collective-permute-start.23 = (bf16[64,384]{1,0:T(8,128)(2,1)S(1)}, bf16[64,384]{1,0:T(8,128)(2,1)S(1)}, u32[]{:S(2)}, u32[]{:S(2)}) collective-permute-start(bf16[64,384]{1,0:T(8,128)(2,1)S(1)} %shard_map.111.refs_6_.refs_2_), channel_id=1, source_target_pairs={{0,8},{8,0},{16,24},{24,16},{1,9},{9,1},{17,25},{25,17},{2,10},{10... | collective-permute-start | bytes 147464 | tf_op jit(solution)/shard_map/ppermute | solution.py:357
  73.5 7.3 %collective-permute-done.30.refs_3_ = bf16[256,768]{1,0:T(8,128)(2,1)S(1)} collective-permute-done((bf16[256,768]{1,0:T(8,128)(2,1)S(1)}, bf16[256,768]{1,0:T(8,128)(2,1)S(1)}, u32[]{:S(2)}, u32[]{:S(2)}) %collective-permute-start.30) | collective-permute-done | bytes 393248 | tf_op jit(solution)/shard_map/ppermute | solution.py:345
  83.5 1.5 %collective-permute-done.29.refs_3_ = bf16[256,384]{1,0:T(8,128)(2,1)S(1)} collective-permute-done((bf16[256,384]{1,0:T(8,128)(2,1)S(1)}, bf16[256,384]{1,0:T(8,128)(2,1)S(1)}, u32[]{:S(2)}, u32[]{:S(2)}) %collective-permute-start.29) | collective-permute-done | bytes 196640 | tf_op jit(solution)/shard_map/ppermute | solution.py:345
  87.7 1.6 %collective-permute-done.34.refs_5_ = bf16[256,768]{1,0:T(8,128)(2,1)S(1)} collective-permute-done((bf16[256,768]{1,0:T(8,128)(2,1)S(1)}, bf16[256,768]{1,0:T(8,128)(2,1)S(1)}, u32[]{:S(2)}, u32[]{:S(2)}) %collective-permute-start.34) | collective-permute-done | bytes 393248 | tf_op jit(solution)/shard_map/ppermute | solution.py:345
  89.3 4.2 %collective-permute-done.33.refs_4_ = bf16[256,768]{1,0:T(8,128)(2,1)S(1)} collective-permute-done((bf16[256,768]{1,0:T(8,128)(2,1)S(1)}, bf16[256,768]{1,0:T(8,128)(2,1)S(1)}, u32[]{:S(2)}, u32[]{:S(2)}) %collective-permute-start.33) | collective-permute-done | bytes 393248 | tf_op jit(solution)/shard_map/ppermute | solution.py:345
  94.2 1.4 %collective-permute-done.32.refs_5_ = bf16[256,384]{1,0:T(8,128)(2,1)S(1)} collective-permute-done((bf16[256,384]{1,0:T(8,128)(2,1)S(1)}, bf16[256,384]{1,0:T(8,128)(2,1)S(1)}, u32[]{:S(2)}, u32[]{:S(2)}) %collective-permute-start.32) | collective-permute-done | bytes 196640 | tf_op jit(solution)/shard_map/ppermute | solution.py:345
  95.6 2.1 %collective-permute-done.31.refs_4_ = bf16[256,384]{1,0:T(8,128)(2,1)S(1)} collective-permute-done((bf16[256,384]{1,0:T(8,128)(2,1)S(1)}, bf16[256,384]{1,0:T(8,128)(2,1)S(1)}, u32[]{:S(2)}, u32[]{:S(2)}) %collective-permute-start.31) | collective-permute-done | bytes 196640 | tf_op jit(solution)/shard_map/ppermute | solution.py:345
  98.4 8.7 %shard_map.118 = (bf16[1,2,1024,1152]{3,2,1,0:T(8,128)(2,1)}, f32[1024,1024]{1,0:T(8,128)S(1)}) custom-call(s32[4]{0:T(128)S(1)} %pad_add_fusion.refs_0_, s32[2]{0:T(128)S(1)} %copy-done.5, bf16[1024,768]{1,0:T(8,128)(2,1)S(1)} %shard_map.116.refs_6_.refs_2_, bf16[1024,768]{1,0:T(8,128)(2,1)S(1)} %collective-permute-done.36.refs_3_, ...), custom_call_target="tpu_custom_call" | custom-call | flops 1000 | bytes 1000 | tf_op jit(solution)/shard_map/pallas_call | solution.py:112
  107.1 9.4 %shard_map.119 = (bf16[1,2,1024,1152]{3,2,1,0:T(8,128)(2,1)}, bf16[1,1152,1024]{2,1,0:T(8,128)(2,1)}, f32[1,1024]{1,0:T(1,128)}) custom-call(s32[4]{0:T(128)S(1)} %pad_add_fusion.refs_0_, s32[2]{0:T(128)S(1)} %copy-done.5, bf16[1024,384]{1,0:T(8,128)(2,1)S(1)} %shard_map.117.refs_6_.refs_2_, ...), custom_call_target="tpu_custom_call", output_to_operand_aliasing={{0}: (9, {})} | custom-call | flops 1000 | bytes 1000 | tf_op jit(solution)/shard_map/pallas_call | solution.py:112
  (83 shorter events, 26.9 us)
Async XLA Ops:
  0.6 9.1 %collective-permute-start.1 = (bf16[256,1152]{1,0:T(8,128)(2,1)}, bf16[256,1152]{1,0:T(8,128)(2,1)S(1)}, u32[]{:S(2)}, u32[]{:S(2)}) collective-permute-start(bf16[256,1152]{1,0:T(8,128)(2,1)} %bitcast.5), channel_id=1, source_target_pairs={{0,1},{1,0},{2,3},{3,2},{4,5},{5,4},{6,7},{7,6},{8,9},{9,8},{10,11... | collective-permute-start | bytes 1769480 | tf_op jit(solution)/shard_map/ppermute | solution.py:333
  1.1 16.7 %collective-permute-start = (bf16[256,1152]{1,0:T(8,128)(2,1)}, bf16[256,1152]{1,0:T(8,128)(2,1)S(1)}, u32[]{:S(2)}, u32[]{:S(2)}) collective-permute-start(bf16[256,1152]{1,0:T(8,128)(2,1)} %bitcast.6), channel_id=1, source_target_pairs={{0,2},{1,3},{2,0},{3,1},{4,6},{5,7},{6,4},{7,5},{8,10},{9,11},{10,... | collective-permute-start | bytes 1769480 | tf_op jit(solution)/shard_map/ppermute | solution.py:336
  14.1 4.4 %collective-permute-start.4 = (bf16[256,1152]{1,0:T(8,128)(2,1)S(1)}, bf16[256,1152]{1,0:T(8,128)(2,1)S(1)}, u32[]{:S(2)}, u32[]{:S(2)}) collective-permute-start(bf16[256,1152]{1,0:T(8,128)(2,1)S(1)} %get-tuple-element.49), channel_id=1, source_target_pairs={{0,1},{1,0},{2,3},{3,2},{4,5},{5,4},{6,7},{7,6},{8,9},{9,8},{10,11... | collective-permute-start | bytes 1769480 | tf_op jit(solution)/shard_map/ppermute | solution.py:333
  14.3 4.2 %collective-permute-start.3 = (bf16[256,1152]{1,0:T(8,128)(2,1)S(1)}, bf16[256,1152]{1,0:T(8,128)(2,1)S(1)}, u32[]{:S(2)}, u32[]{:S(2)}) collective-permute-start(bf16[256,1152]{1,0:T(8,128)(2,1)S(1)} %get-tuple-element.46.refs_5_), channel_id=1, source_target_pairs={{0,1},{1,0},{2,3},{3,2},{4,5},{5,4},{6,7},{7,6},{8,9},{9,8},{10,11... | collective-permute-start | bytes 1769480 | tf_op jit(solution)/shard_map/ppermute | solution.py:333
  19.2 8.7 %collective-permute-start.8 = (bf16[256,768]{1,0:T(8,128)(2,1)S(1)}, bf16[256,768]{1,0:T(8,128)(2,1)S(1)}, u32[]{:S(2)}, u32[]{:S(2)}) collective-permute-start(bf16[256,768]{1,0:T(8,128)(2,1)S(1)} %get-tuple-element.50.refs_7_), channel_id=1, source_target_pairs={{0,2},{1,5},{2,0},{3,7},{4,6},{5,1},{6,4},{7,3},{8,10},{9,13},{10,... | collective-permute-start | bytes 1179656 | tf_op jit(solution)/shard_map/ppermute | solution.py:345
  24.7 3.3 %collective-permute-start.7 = (bf16[128,1152]{1,0:T(8,128)(2,1)S(1)}, bf16[128,1152]{1,0:T(8,128)(2,1)S(1)}, u32[]{:S(2)}, u32[]{:S(2)}) collective-permute-start(bf16[128,1152]{1,0:T(8,128)(2,1)S(1)} %get-tuple-element.53), channel_id=1, source_target_pairs={{0,1},{1,0},{2,3},{3,2},{4,5},{5,4},{6,7},{7,6},{8,9},{9,8},{10,11... | collective-permute-start | bytes 884744 | tf_op jit(solution)/shard_map/ppermute | solution.py:333
  25.2 6.1 %collective-permute-start.5 = (bf16[256,384]{1,0:T(8,128)(2,1)S(1)}, bf16[256,384]{1,0:T(8,128)(2,1)S(1)}, u32[]{:S(2)}, u32[]{:S(2)}) collective-permute-start(bf16[256,384]{1,0:T(8,128)(2,1)S(1)} %get-tuple-element.51), channel_id=1, source_target_pairs={{0,2},{1,5},{2,0},{3,7},{4,6},{5,1},{6,4},{7,3},{8,10},{9,13},{10,... | collective-permute-start | bytes 589832 | tf_op jit(solution)/shard_map/ppermute | solution.py:345
  28.9 12.1 %collective-permute-start.16 = (bf16[256,768]{1,0:T(8,128)(2,1)S(1)}, bf16[256,768]{1,0:T(8,128)(2,1)S(1)}, u32[]{:S(2)}, u32[]{:S(2)}) collective-permute-start(bf16[256,768]{1,0:T(8,128)(2,1)S(1)} %get-tuple-element.61), channel_id=1, source_target_pairs={{0,4},{1,3},{2,6},{3,1},{4,0},{5,7},{6,2},{7,5},{8,12},{9,11},{10,... | collective-permute-start | bytes 1179656 | tf_op jit(solution)/shard_map/ppermute | solution.py:345
  30.3 11.8 %collective-permute-start.15 = (bf16[256,768]{1,0:T(8,128)(2,1)S(1)}, bf16[256,768]{1,0:T(8,128)(2,1)S(1)}, u32[]{:S(2)}, u32[]{:S(2)}) collective-permute-start(bf16[256,768]{1,0:T(8,128)(2,1)S(1)} %get-tuple-element.54.refs_10_), channel_id=1, source_target_pairs={{0,2},{1,5},{2,0},{3,7},{4,6},{5,1},{6,4},{7,3},{8,10},{9,13},{10,... | collective-permute-start | bytes 1179656 | tf_op jit(solution)/shard_map/ppermute | solution.py:345
  34.9 12.5 %collective-permute-start.14 = (bf16[256,384]{1,0:T(8,128)(2,1)S(1)}, bf16[256,384]{1,0:T(8,128)(2,1)S(1)}, u32[]{:S(2)}, u32[]{:S(2)}) collective-permute-start(bf16[256,384]{1,0:T(8,128)(2,1)S(1)} %get-tuple-element.60), channel_id=1, source_target_pairs={{0,4},{1,3},{2,6},{3,1},{4,0},{5,7},{6,2},{7,5},{8,12},{9,11},{10,... | collective-permute-start | bytes 589832 | tf_op jit(solution)/shard_map/ppermute | solution.py:345
  36.2 11.2 %collective-permute-start.13 = (bf16[256,384]{1,0:T(8,128)(2,1)S(1)}, bf16[256,384]{1,0:T(8,128)(2,1)S(1)}, u32[]{:S(2)}, u32[]{:S(2)}) collective-permute-start(bf16[256,384]{1,0:T(8,128)(2,1)S(1)} %get-tuple-element.55.refs_4_), channel_id=1, source_target_pairs={{0,2},{1,5},{2,0},{3,7},{4,6},{5,1},{6,4},{7,3},{8,10},{9,13},{10,... | collective-permute-start | bytes 589832 | tf_op jit(solution)/shard_map/ppermute | solution.py:345
  37.2 3.3 %collective-permute-start.9 = (bf16[64,1152]{1,0:T(8,128)(2,1)S(1)}, bf16[64,1152]{1,0:T(8,128)(2,1)S(1)}, u32[]{:S(2)}, u32[]{:S(2)}) collective-permute-start(bf16[64,1152]{1,0:T(8,128)(2,1)S(1)} %get-tuple-element.56.refs_4_), channel_id=1, source_target_pairs={{0,1},{1,0},{2,3},{3,2},{4,5},{5,4},{6,7},{7,6},{8,9},{9,8},{10,11... | collective-permute-start | bytes 442376 | tf_op jit(solution)/shard_map/ppermute | solution.py:333
  42.9 9.4 %collective-permute-start.20 = (bf16[64,768]{1,0:T(8,128)(2,1)S(1)}, bf16[64,768]{1,0:T(8,128)(2,1)S(1)}, u32[]{:S(2)}, u32[]{:S(2)}) collective-permute-start(bf16[64,768]{1,0:T(8,128)(2,1)S(1)} %get-tuple-element.69), channel_id=1, source_target_pairs={{0,8},{8,0},{16,24},{24,16},{1,9},{9,1},{17,25},{25,17},{2,10},{10... | collective-permute-start | bytes 294920 | tf_op jit(solution)/shard_map/ppermute | solution.py:357
  44.6 11.4 %collective-permute-start.21 = (bf16[64,768]{1,0:T(8,128)(2,1)S(1)}, bf16[64,768]{1,0:T(8,128)(2,1)S(1)}, u32[]{:S(2)}, u32[]{:S(2)}) collective-permute-start(bf16[64,768]{1,0:T(8,128)(2,1)S(1)} %get-tuple-element.70), channel_id=1, source_target_pairs={{0,16},{8,24},{16,0},{24,8},{1,17},{9,25},{17,1},{25,9},{2,18},{10... | collective-permute-start | bytes 294920 | tf_op jit(solution)/shard_map/ppermute | solution.py:357
  47.2 8.8 %collective-permute-start.22 = (bf16[64,768]{1,0:T(8,128)(2,1)S(1)}, bf16[64,768]{1,0:T(8,128)(2,1)S(1)}, u32[]{:S(2)}, u32[]{:S(2)}) collective-permute-start(bf16[64,768]{1,0:T(8,128)(2,1)S(1)} %get-tuple-element.71), channel_id=1, source_target_pairs={{0,24},{8,16},{16,8},{24,0},{1,25},{9,17},{17,9},{25,1},{2,26},{10... | collective-permute-start | bytes 294920 | tf_op jit(solution)/shard_map/ppermute | solution.py:357
  48.1 15.3 %collective-permute-start.17 = (bf16[64,384]{1,0:T(8,128)(2,1)S(1)}, bf16[64,384]{1,0:T(8,128)(2,1)S(1)}, u32[]{:S(2)}, u32[]{:S(2)}) collective-permute-start(bf16[64,384]{1,0:T(8,128)(2,1)S(1)} %get-tuple-element.66), channel_id=1, source_target_pairs={{0,8},{8,0},{16,24},{24,16},{1,9},{9,1},{17,25},{25,17},{2,10},{10... | collective-permute-start | bytes 147464 | tf_op jit(solution)/shard_map/ppermute | solution.py:357
  48.8 15.1 %collective-permute-start.18 = (bf16[64,384]{1,0:T(8,128)(2,1)S(1)}, bf16[64,384]{1,0:T(8,128)(2,1)S(1)}, u32[]{:S(2)}, u32[]{:S(2)}) collective-permute-start(bf16[64,384]{1,0:T(8,128)(2,1)S(1)} %get-tuple-element.67), channel_id=1, source_target_pairs={{0,16},{8,24},{16,0},{24,8},{1,17},{9,25},{17,1},{25,9},{2,18},{10... | collective-permute-start | bytes 147464 | tf_op jit(solution)/shard_map/ppermute | solution.py:357
  52.3 11.6 %collective-permute-start.19 = (bf16[64,384]{1,0:T(8,128)(2,1)S(1)}, bf16[64,384]{1,0:T(8,128)(2,1)S(1)}, u32[]{:S(2)}, u32[]{:S(2)}) collective-permute-start(bf16[64,384]{1,0:T(8,128)(2,1)S(1)} %get-tuple-element.68), channel_id=1, source_target_pairs={{0,24},{8,16},{16,8},{24,0},{1,25},{9,17},{17,9},{25,1},{2,26},{10... | collective-permute-start | bytes 147464 | tf_op jit(solution)/shard_map/ppermute | solution.py:357
  56.6 11.0 %collective-permute-start.28 = (bf16[64,768]{1,0:T(8,128)(2,1)S(1)}, bf16[64,768]{1,0:T(8,128)(2,1)S(1)}, u32[]{:S(2)}, u32[]{:S(2)}) collective-permute-start(bf16[64,768]{1,0:T(8,128)(2,1)S(1)} %shard_map.110.refs_6_.refs_2_), channel_id=1, source_target_pairs={{0,24},{8,16},{16,8},{24,0},{1,25},{9,17},{17,9},{25,1},{2,26},{10... | collective-permute-start | bytes 294920 | tf_op jit(solution)/shard_map/ppermute | solution.py:357
  61.1 8.8 %collective-permute-start.27 = (bf16[64,768]{1,0:T(8,128)(2,1)S(1)}, bf16[64,768]{1,0:T(8,128)(2,1)S(1)}, u32[]{:S(2)}, u32[]{:S(2)}) collective-permute-start(bf16[64,768]{1,0:T(8,128)(2,1)S(1)} %shard_map.110.refs_6_.refs_2_), channel_id=1, source_target_pairs={{0,16},{8,24},{16,0},{24,8},{1,17},{9,25},{17,1},{25,9},{2,18},{10... | collective-permute-start | bytes 294920 | tf_op jit(solution)/shard_map/ppermute | solution.py:357
  63.4 6.5 %collective-permute-start.26 = (bf16[64,768]{1,0:T(8,128)(2,1)S(1)}, bf16[64,768]{1,0:T(8,128)(2,1)S(1)}, u32[]{:S(2)}, u32[]{:S(2)}) collective-permute-start(bf16[64,768]{1,0:T(8,128)(2,1)S(1)} %shard_map.110.refs_6_.refs_2_), channel_id=1, source_target_pairs={{0,8},{8,0},{16,24},{24,16},{1,9},{9,1},{17,25},{25,17},{2,10},{10... | collective-permute-start | bytes 294920 | tf_op jit(solution)/shard_map/ppermute | solution.py:357
  64.5 6.8 %collective-permute-start.25 = (bf16[64,384]{1,0:T(8,128)(2,1)S(1)}, bf16[64,384]{1,0:T(8,128)(2,1)S(1)}, u32[]{:S(2)}, u32[]{:S(2)}) collective-permute-start(bf16[64,384]{1,0:T(8,128)(2,1)S(1)} %shard_map.111.refs_6_.refs_2_), channel_id=1, source_target_pairs={{0,24},{8,16},{16,8},{24,0},{1,25},{9,17},{17,9},{25,1},{2,26},{10... | collective-permute-start | bytes 147464 | tf_op jit(solution)/shard_map/ppermute | solution.py:357
  66.9 5.1 %collective-permute-start.24 = (bf16[64,384]{1,0:T(8,128)(2,1)S(1)}, bf16[64,384]{1,0:T(8,128)(2,1)S(1)}, u32[]{:S(2)}, u32[]{:S(2)}) collective-permute-start(bf16[64,384]{1,0:T(8,128)(2,1)S(1)} %shard_map.111.refs_6_.refs_2_), channel_id=1, source_target_pairs={{0,16},{8,24},{16,0},{24,8},{1,17},{9,25},{17,1},{25,9},{2,18},{10... | collective-permute-start | bytes 147464 | tf_op jit(solution)/shard_map/ppermute | solution.py:357
  67.6 4.6 %collective-permute-start.23 = (bf16[64,384]{1,0:T(8,128)(2,1)S(1)}, bf16[64,384]{1,0:T(8,128)(2,1)S(1)}, u32[]{:S(2)}, u32[]{:S(2)}) collective-permute-start(bf16[64,384]{1,0:T(8,128)(2,1)S(1)} %shard_map.111.refs_6_.refs_2_), channel_id=1, source_target_pairs={{0,8},{8,0},{16,24},{24,16},{1,9},{9,1},{17,25},{25,17},{2,10},{10... | collective-permute-start | bytes 147464 | tf_op jit(solution)/shard_map/ppermute | solution.py:357
  70.5 10.3 %collective-permute-start.30 = (bf16[256,768]{1,0:T(8,128)(2,1)S(1)}, bf16[256,768]{1,0:T(8,128)(2,1)S(1)}, u32[]{:S(2)}, u32[]{:S(2)}) collective-permute-start(bf16[256,768]{1,0:T(8,128)(2,1)S(1)} %shard_map.112.refs_6_.refs_2_), channel_id=1, source_target_pairs={{0,4},{1,3},{2,6},{3,1},{4,0},{5,7},{6,2},{7,5},{8,12},{9,11},{10,... | collective-permute-start | bytes 1179656 | tf_op jit(solution)/shard_map/ppermute | solution.py:345
  72.7 12.3 %collective-permute-start.29 = (bf16[256,384]{1,0:T(8,128)(2,1)S(1)}, bf16[256,384]{1,0:T(8,128)(2,1)S(1)}, u32[]{:S(2)}, u32[]{:S(2)}) collective-permute-start(bf16[256,384]{1,0:T(8,128)(2,1)S(1)} %shard_map.113.refs_4_.refs_2_), channel_id=1, source_target_pairs={{0,4},{1,3},{2,6},{3,1},{4,0},{5,7},{6,2},{7,5},{8,12},{9,11},{10,... | collective-permute-start | bytes 589832 | tf_op jit(solution)/shard_map/ppermute | solution.py:345
  81.4 7.8 %collective-permute-start.34 = (bf16[256,768]{1,0:T(8,128)(2,1)S(1)}, bf16[256,768]{1,0:T(8,128)(2,1)S(1)}, u32[]{:S(2)}, u32[]{:S(2)}) collective-permute-start(bf16[256,768]{1,0:T(8,128)(2,1)S(1)} %get-tuple-element.75.refs_3_), channel_id=1, source_target_pairs={{0,2},{1,5},{2,0},{3,7},{4,6},{5,1},{6,4},{7,3},{8,10},{9,13},{10,... | collective-permute-start | bytes 1179656 | tf_op jit(solution)/shard_map/ppermute | solution.py:345
  82.4 11.1 %collective-permute-start.33 = (bf16[256,768]{1,0:T(8,128)(2,1)S(1)}, bf16[256,768]{1,0:T(8,128)(2,1)S(1)}, u32[]{:S(2)}, u32[]{:S(2)}) collective-permute-start(bf16[256,768]{1,0:T(8,128)(2,1)S(1)} %get-tuple-element.72.refs_4_.refs_2_), channel_id=1, source_target_pairs={{0,2},{1,5},{2,0},{3,7},{4,6},{5,1},{6,4},{7,3},{8,10},{9,13},{10,... | collective-permute-start | bytes 1179656 | tf_op jit(solution)/shard_map/ppermute | solution.py:345
  85.6 10.0 %collective-permute-start.32 = (bf16[256,384]{1,0:T(8,128)(2,1)S(1)}, bf16[256,384]{1,0:T(8,128)(2,1)S(1)}, u32[]{:S(2)}, u32[]{:S(2)}) collective-permute-start(bf16[256,384]{1,0:T(8,128)(2,1)S(1)} %get-tuple-element.74.refs_3_), channel_id=1, source_target_pairs={{0,2},{1,5},{2,0},{3,7},{4,6},{5,1},{6,4},{7,3},{8,10},{9,13},{10,... | collective-permute-start | bytes 589832 | tf_op jit(solution)/shard_map/ppermute | solution.py:345
  86.6 11.1 %collective-permute-start.31 = (bf16[256,384]{1,0:T(8,128)(2,1)S(1)}, bf16[256,384]{1,0:T(8,128)(2,1)S(1)}, u32[]{:S(2)}, u32[]{:S(2)}) collective-permute-start(bf16[256,384]{1,0:T(8,128)(2,1)S(1)} %get-tuple-element.73.refs_6_.refs_2_), channel_id=1, source_target_pairs={{0,2},{1,5},{2,0},{3,7},{4,6},{5,1},{6,4},{7,3},{8,10},{9,13},{10,... | collective-permute-start | bytes 589832 | tf_op jit(solution)/shard_map/ppermute | solution.py:345
  94.1 4.3 %collective-permute-start.36 = (bf16[1024,768]{1,0:T(8,128)(2,1)S(1)}, bf16[1024,768]{1,0:T(8,128)(2,1)S(1)}, u32[]{:S(2)}, u32[]{:S(2)}) collective-permute-start(bf16[1024,768]{1,0:T(8,128)(2,1)S(1)} %shard_map.116.refs_6_.refs_2_), channel_id=1, source_target_pairs={{0,1},{1,0},{2,3},{3,2},{4,5},{5,4},{6,7},{7,6},{8,9},{9,8},{10,11... | collective-permute-start | bytes 4718600 | tf_op jit(solution)/shard_map/ppermute | solution.py:333
  98.3 8.8 %collective-permute-start.35 = (bf16[1024,384]{1,0:T(8,128)(2,1)S(1)}, bf16[1024,384]{1,0:T(8,128)(2,1)S(1)}, u32[]{:S(2)}, u32[]{:S(2)}) collective-permute-start(bf16[1024,384]{1,0:T(8,128)(2,1)S(1)} %shard_map.117.refs_6_.refs_2_), channel_id=1, source_target_pairs={{0,1},{1,0},{2,3},{3,2},{4,5},{5,4},{6,7},{7,6},{8,9},{9,8},{10,11... | collective-permute-start | bytes 2359304 | tf_op jit(solution)/shard_map/ppermute | solution.py:333
  (12 other events, 35.0 us)

commit v5 on v4

--- a/solution.py
+++ b/solution.py
@@ -242,6 +242,43 @@
 
     outs = [held((part, writeout.shape[-1]), dtype)] * cuts
     return order(kernel, [act, writeout], outs, heavy=heavy)
+
+
+def target_gradients(order, mine, scaled, turned, writeout, lo, hi, sens, dec):
+    features = writeout.shape[2]
+    total, columns = scaled.shape
+    block = block_of(features)
+    at = lo // columns
+
+    def target(w):
+        return w[CORE] if mine else 1 - w[CORE]
+
+    def kernel(w, d, s_ref, turned_ref, weight_ref, *refs):
+        dec_ref, out_ref = refs[-2:]
+        cols = span(pl.program_id(0), block)
+        grad = lax.dot_general(
+            s_ref[...],
+            weight_ref[0, target(w), cols, lo:hi],
+            (((1,), (1,)), ((), ())),
+            preferred_element_type=F32,
+        )
+        out_ref[:, cols] = grad if sens is None else refs[0][:, cols] + grad
+        out = jnp.dot(turned_ref[cols, :], s_ref[...], preferred_element_type=F32)
+        dec_ref[0, 0] = out.astype(BF)
+
+    operands = [scaled, turned, writeout] + ([] if sens is None else [sens])
+    before = [] if dec is None else [dec]
+    dec, sens = order(
+        kernel,
+        operands + before,
+        [array(writeout.shape, BF), held((total, features), F32)],
+        [HELD] * len(operands) + [ANYWHERE] * len(before),
+        [pl.BlockSpec((1, 1, block, columns), lambda i, w, d: (0, target(w), i, at)), HELD],
+        grid=(features // block,),
+        aliases=[(len(operands), 0)] if before else (),
+    )
+    order.last = sens
+    return dec, sens
 
 
 def gradients(order, scaled, turned, writeout, lo, hi, sens=None, dec=None, last=None):
@@ -462,13 +499,13 @@
         done = order(kernel, (scaled, *pieces), [held((rows, size), BF)], heavy=True)[0]
         return done, to_second(done)
 
-    def join_pair(done, got):
+    def join_pair(done, got, heavy):
         def kernel(w, d, done_ref, got_ref, out0, out1):
             done_last = jnp.logical_or(w[CORE] == 1, w[FEAT] == 1)
             out0[...] = pick(done_last, got_ref[...], done_ref[...])
             out1[...] = pick(done_last, done_ref[...], got_ref[...])
 
-        pair = order(kernel, (done, got), [held(done.shape, BF)] * 2, heavy=True)
+        pair = order(kernel, (done, got), [held(done.shape, BF)] * 2, heavy=heavy)
         return pair, [to_first(block) for block in pair]
 
     def join_all(pair, got):
@@ -494,18 +531,30 @@
     there = far_block(False, 4)
     turned, tokens = turn(order, (act_near, act_far), ((own, near), (far, far_near)))
     order.keep = [writeout, cutoff, turned, tokens]
-    stages = [send_pieces(*r, k > 0) for k, r in enumerate(reduced)]
-    stages = [scale_piece(*stage) for stage in stages]
-    stages = [join_pieces(*stage) for stage in stages]
-    stages = [join_pair(*stage) for stage in stages]
-    scaled = [join_all(*stage) for stage in stages]
+    count = len(chunks)
+    sent, joined, pairs = send_pieces(*reduced[0], False), [], []
+    for k in range(count):
+        scaled = scale_piece(*sent)
+        if k + 1 < count:
+            sent = send_pieces(*reduced[k + 1], True)
+        if k > 0:
+            pairs.append(join_pair(*joined[k - 1], True))
+        joined.append(join_pieces(*scaled))
+    pairs.append(join_pair(*joined[-1], False))
+    scaled = join_all(*pairs[0])
+    sens = dec = None
+    for k, (lo, hi) in enumerate(chunks[:-1]):
+        own, other = scaled
+        dec, sens = target_gradients(order, True, own, turned, writeout, lo, hi, sens, dec)
+        following = join_all(*pairs[k + 1])
+        dec, sens = target_gradients(order, False, other, turned, writeout, lo, hi, sens, dec)
+        scaled = following
     order.keep = []
-    sens = dec = None
-    for k, (lo, hi) in enumerate(chunks):
-        last = (cutoff, tokens) if k == len(chunks) - 1 else None
-        dec, *rest = gradients(order, scaled[k], turned, writeout, lo, hi, sens, dec, last)
-        sens = rest[0]
-    return rest[0], dec, rest[1]
+    lo, hi = chunks[-1]
+    dec, enc, bias = gradients(
+        order, scaled, turned, writeout, lo, hi, sens, dec, (cutoff, tokens)
+    )
+    return enc, dec, bias
 
 
 def solution(mesh):

time: 117 us -> 114 us (0.974)
  starting transfers between devices: 39.4 us -> 35.7 us
  Pallas kernels: 48.6 us -> 50.4 us
    ppermute x12, waiting for transfers between devices: 19.7 us -> 13.7 us  [mixed(): return lambda a: lax.ppermute(a, ('feat', 'tok'), pairs)]
    ppermute x12, waiting for transfers between devices: 5.22 us -> 10.1 us  [to_layer(): lax.ppermute(a, 'layer', [(l, l ^ s if binary else (l + s) % layers) for...]
    ppermute x12, starting transfers between devices: 20.7 us -> 18.3 us  [to_layer(): lax.ppermute(a, 'layer', [(l, l ^ s if binary else (l + s) % layers) for...]
    pallas_call x26 -> x27, Pallas kernels: 48.6 us -> 50.4 us  [__call__(): pl.pallas_call(body, grid_spec=pltpu.PrefetchScalarGridSpec(num_scalar_pr...]
    ppermute x12, starting transfers between devices: 13.6 us -> 11.9 us  [mixed(): return lambda a: lax.ppermute(a, ('feat', 'tok'), pairs)]
  transfers between devices with their start and end apart: 37 -> 37, of which waited for: 14 -> 8; matrix products, arithmetic and copies ran while one was open for 0% -> 0% of each run, Pallas kernels for 34% -> 35%
where the time goes in v5:
time: 114 us
  Pallas kernels  50.4 us (44%)
  starting transfers between devices  35.7 us (31%)
  waiting for transfers between devices  25.7 us (23%)
    pallas_call x27, Pallas kernels, __call__(): pl.pallas_call(body, grid_spec=pltpu.PrefetchScalarGridSpec(num_scalar_pr...  50.4 us
    ppermute x12, starting transfers between devices, to_layer(): lax.ppermute(a, 'layer', [(l, l ^ s if binary else (l + s) % layers) for...  18.3 us
    ppermute x12, waiting for transfers between devices, mixed(): return lambda a: lax.ppermute(a, ('feat', 'tok'), pairs)  13.7 us
    ppermute x12, starting transfers between devices, mixed(): return lambda a: lax.ppermute(a, ('feat', 'tok'), pairs)  11.9 us
    ppermute x12, waiting for transfers between devices, to_layer(): lax.ppermute(a, 'layer', [(l, l ^ s if binary else (l + s) % layers) for...  10.1 us
    ppermute x12, starting transfers between devices, to_core(): return lax.ppermute(a, 'tok', [(t, t ^ 1) for t in range(toks)])  2.97 us
    ppermute x1, starting transfers between devices, to_side(): return lax.ppermute(a, 'tok', [(t, t ^ 2) for t in range(toks)])  2.57 us
  transfers between devices with their start and end apart: 37, of which 8 were waited for; matrix products, arithmetic and copies ran while one was open for 0% of the time, Pallas kernels for 35%

profile of v5, /device:TPU:0, one launch (start us, length us, event | category | flops | bytes accessed | tf_op | source)
XLA Modules:
  0.0 113.5 jit_solution(5505689613174054330)
XLA Ops:
  1.1 2.6 %collective-permute-start = (bf16[256,1152]{1,0:T(8,128)(2,1)}, bf16[256,1152]{1,0:T(8,128)(2,1)S(1)}, u32[]{:S(2)}, u32[]{:S(2)}) collective-permute-start(bf16[256,1152]{1,0:T(8,128)(2,1)} %bitcast.6), channel_id=1, source_target_pairs={{0,2},{1,3},{2,0},{3,1},{4,6},{5,7},{6,4},{7,5},{8,10},{9,11},{10,... | collective-permute-start | bytes 1769480 | tf_op jit(solution)/shard_map/ppermute | solution.py:373
  4.5 5.3 %shard_map.94 = (bf16[1,1152,1024]{2,1,0:T(8,128)(2,1)S(1)}, s32[1,1024,1024]{2,1,0:T(8,128)S(1)}, bf16[1,2,1024,1152]{3,2,1,0:T(8,128)(2,1)S(1)}, bf16[2,256,1152]{2,1,0:T(8,128)(2,1)S(1)}) custom-call(s32[4]{0:T(128)S(1)} %pad_add_fusion.refs_0_, s32[2]{0:T(128)S(1)} %copy-done.4, bf16[1,1152,1024]{2,1,0:T(8,128)(2,1)} %refs_2_.1, ...), custom_call_target="tpu_custom_call" | custom-call | flops 99999997952 | bytes 1000 | tf_op jit(solution)/shard_map/pallas_call | solution.py:112
  9.8 2.2 %shard_map.95.refs_2_.refs_5_ = bf16[512,1024]{1,0:T(8,128)(2,1)S(1)} custom-call(s32[4]{0:T(128)S(1)} %pad_add_fusion.refs_0_, s32[2]{0:T(128)S(1)} %copy-done.5, bf16[256,1152]{1,0:T(8,128)(2,1)S(1)} %bitcast.7, bf16[256,1152]{1,0:T(8,128)(2,1)S(1)} %collective-permute-done.1.refs_3_.refs_5_, bf16[1,1152,1024]{2,1,0:T(8,128)(2,1)S(1)} %get-tuple-element.44.refs_4_.refs_7_, ...), custom_call_target="tpu_custom_call" | custom-call | flops 1000 | bytes 1000 | tf_op jit(solution)/shard_map/pallas_call | solution.py:112
  12.0 2.1 %shard_map.96 = (bf16[256,1152]{1,0:T(8,128)(2,1)S(1)}, bf16[256,1152]{1,0:T(8,128)(2,1)S(1)}) custom-call(s32[4]{0:T(128)S(1)} %pad_add_fusion.refs_0_, s32[2]{0:T(128)S(1)} %copy-done.5, bf16[512,1024]{1,0:T(8,128)(2,1)S(1)} %shard_map.95.refs_2_.refs_5_, bf16[1,2,1024,1152]{3,2,1,0:T(8,128)(2,1)S(1)} %get-tuple-element.46.refs_3_.refs_10_.refs_7_.refs_5_.refs_4_, ...), custom_call_target="tpu_custom_call" | custom-call | flops 1000 | bytes 1000 | tf_op jit(solution)/shard_map/pallas_call | solution.py:112
  14.7 2.1 %shard_map.97 = (f32[256,1152]{1,0:T(8,128)S(1)}, f32[256,1152]{1,0:T(8,128)S(1)}) custom-call(s32[4]{0:T(128)S(1)} %pad_add_fusion.refs_0_, s32[2]{0:T(128)S(1)} %copy-done.5, bf16[512,1024]{1,0:T(8,128)(2,1)S(1)} %shard_map.95.refs_2_.refs_5_, bf16[1,2,1024,1152]{3,2,1,0:T(8,128)(2,1)S(1)} %get-tuple-element.46.refs_3_.refs_10_.refs_7_.refs_5_.refs_4_, ...), custom_call_target="tpu_custom_call" | custom-call | flops 1000 | bytes 1000 | tf_op jit(solution)/shard_map/pallas_call | solution.py:112
  19.2 1.8 %collective-permute-start.8 = (bf16[256,768]{1,0:T(8,128)(2,1)S(1)}, bf16[256,768]{1,0:T(8,128)(2,1)S(1)}, u32[]{:S(2)}, u32[]{:S(2)}) collective-permute-start(bf16[256,768]{1,0:T(8,128)(2,1)S(1)} %get-tuple-element.52.refs_7_), channel_id=1, source_target_pairs={{0,2},{1,5},{2,0},{3,7},{4,6},{5,1},{6,4},{7,3},{8,10},{9,13},{10,... | collective-permute-start | bytes 1179656 | tf_op jit(solution)/shard_map/ppermute | solution.py:382
  21.1 2.2 %shard_map.100.refs_2_.refs_4_.refs_3_ = bf16[512,1024]{1,0:T(8,128)(2,1)S(1)} custom-call(s32[4]{0:T(128)S(1)} %pad_add_fusion.refs_0_, s32[2]{0:T(128)S(1)} %copy-done.5, bf16[256,1152]{1,0:T(8,128)(2,1)S(1)} %shard_map.98.refs_6_.refs_2_, bf16[256,1152]{1,0:T(8,128)(2,1)S(1)} %collective-permute-done.2.refs_3_.refs_7_, ...), custom_call_target="tpu_custom_call" | custom-call | flops 99999997952 | bytes 1000 | tf_op jit(solution)/shard_map/pallas_call | solution.py:112
  23.2 1.4 %shard_map.101 = (bf16[128,1152]{1,0:T(8,128)(2,1)S(1)}, bf16[128,1152]{1,0:T(8,128)(2,1)S(1)}) custom-call(s32[4]{0:T(128)S(1)} %pad_add_fusion.refs_0_, s32[2]{0:T(128)S(1)} %copy-done.5, bf16[512,1024]{1,0:T(8,128)(2,1)S(1)} %shard_map.100.refs_2_.refs_4_.refs_3_, ...), custom_call_target="tpu_custom_call" | custom-call | flops 1000 | bytes 1000 | tf_op jit(solution)/shard_map/pallas_call | solution.py:112
  25.2 1.3 %collective-permute-start.5 = (bf16[256,384]{1,0:T(8,128)(2,1)S(1)}, bf16[256,384]{1,0:T(8,128)(2,1)S(1)}, u32[]{:S(2)}, u32[]{:S(2)}) collective-permute-start(bf16[256,384]{1,0:T(8,128)(2,1)S(1)} %get-tuple-element.53), channel_id=1, source_target_pairs={{0,2},{1,5},{2,0},{3,7},{4,6},{5,1},{6,4},{7,3},{8,10},{9,13},{10,... | collective-permute-start | bytes 589832 | tf_op jit(solution)/shard_map/ppermute | solution.py:382
  26.5 1.4 %shard_map.102.refs_7_.refs_10_ = f32[256,1152]{1,0:T(8,128)S(1)} custom-call(s32[4]{0:T(128)S(1)} %pad_add_fusion.refs_0_, s32[2]{0:T(128)S(1)} %copy-done.5, bf16[512,1024]{1,0:T(8,128)(2,1)S(1)} %shard_map.100.refs_2_.refs_4_.refs_3_, bf16[1,2,1024,1152]{3,2,1,0:T(8,128)(2,1)S(1)} %get-tuple-element.46.refs_3_.refs_10_.refs_7_.refs_5_.refs_4_, ...), custom_call_target="tpu_custom_call" | custom-call | flops 1000 | bytes 1000 | tf_op jit(solution)/shard_map/pallas_call | solution.py:112
  28.8 1.5 %collective-permute-start.16 = (bf16[256,768]{1,0:T(8,128)(2,1)S(1)}, bf16[256,768]{1,0:T(8,128)(2,1)S(1)}, u32[]{:S(2)}, u32[]{:S(2)}) collective-permute-start(bf16[256,768]{1,0:T(8,128)(2,1)S(1)} %get-tuple-element.63), channel_id=1, source_target_pairs={{0,4},{1,3},{2,6},{3,1},{4,0},{5,7},{6,2},{7,5},{8,12},{9,11},{10,... | collective-permute-start | bytes 1179656 | tf_op jit(solution)/shard_map/ppermute | solution.py:382
  32.0 1.4 %shard_map.105 = (bf16[64,1152]{1,0:T(8,128)(2,1)S(1)}, bf16[64,1152]{1,0:T(8,128)(2,1)S(1)}, bf16[64,1152]{1,0:T(8,128)(2,1)S(1)}, bf16[64,1152]{1,0:T(8,128)(2,1)S(1)}) custom-call(s32[4]{0:T(128)S(1)} %pad_add_fusion.refs_0_, s32[2]{0:T(128)S(1)} %copy-done.5, bf16[512,1024]{1,0:T(8,128)(2,1)S(1)} %shard_map.100.refs_2_.refs_4_.refs_3_, ...), custom_call_target="tpu_custom_call" | custom-call | flops 1000 | bytes 1000 | tf_op jit(solution)/shard_map/pallas_call | solution.py:112
  35.0 1.4 %shard_map.106.refs_8_.refs_2_ = f32[256,1152]{1,0:T(8,128)S(1)} custom-call(s32[4]{0:T(128)S(1)} %pad_add_fusion.refs_0_, s32[2]{0:T(128)S(1)} %copy-done.5, bf16[512,1024]{1,0:T(8,128)(2,1)S(1)} %shard_map.100.refs_2_.refs_4_.refs_3_, bf16[1,2,1024,1152]{3,2,1,0:T(8,128)(2,1)S(1)} %get-tuple-element.46.refs_3_.refs_10_.refs_7_.refs_5_.refs_4_, ...), custom_call_target="tpu_custom_call" | custom-call | flops 1000 | bytes 1000 | tf_op jit(solution)/shard_map/pallas_call | solution.py:112
  36.4 1.8 %shard_map.107 = (bf16[1024,1024]{1,0:T(8,128)(2,1)S(1)}, bf16[1152,1024]{1,0:T(8,128)(2,1)S(1)}) custom-call(s32[4]{0:T(128)S(1)} %pad_add_fusion.refs_0_, s32[2]{0:T(128)S(1)} %copy-done.5, bf16[512,1024]{1,0:T(8,128)(2,1)S(1)} %copy-done.1, bf16[512,1024]{1,0:T(8,128)(2,1)S(1)} %shard_map.100.refs_2_.refs_4_.refs_3_, bf16[256,1152]{1,0:T(8,128)(2,1)S(1)} %bitcast.8, ...), custom_call_target="tpu_custom_call" | custom-call | flops 1000 | bytes 1000 | tf_op jit(solution)/shard_map/pallas_call | solution.py:112
  38.3 2.5 %collective-permute-done.16.refs_8_ = bf16[256,768]{1,0:T(8,128)(2,1)S(1)} collective-permute-done((bf16[256,768]{1,0:T(8,128)(2,1)S(1)}, bf16[256,768]{1,0:T(8,128)(2,1)S(1)}, u32[]{:S(2)}, u32[]{:S(2)}) %collective-permute-start.16) | collective-permute-done | bytes 393248 | tf_op jit(solution)/shard_map/ppermute | solution.py:382
  41.7 1.6 %collective-permute-start.17 = (bf16[64,768]{1,0:T(8,128)(2,1)S(1)}, bf16[64,768]{1,0:T(8,128)(2,1)S(1)}, u32[]{:S(2)}, u32[]{:S(2)}) collective-permute-start(bf16[64,768]{1,0:T(8,128)(2,1)S(1)} %get-tuple-element.67), channel_id=1, source_target_pairs={{0,8},{8,0},{16,24},{24,16},{1,9},{9,1},{17,25},{25,17},{2,10},{10... | collective-permute-start | bytes 294920 | tf_op jit(solution)/shard_map/ppermute | solution.py:394
  43.4 2.6 %collective-permute-start.18 = (bf16[64,768]{1,0:T(8,128)(2,1)S(1)}, bf16[64,768]{1,0:T(8,128)(2,1)S(1)}, u32[]{:S(2)}, u32[]{:S(2)}) collective-permute-start(bf16[64,768]{1,0:T(8,128)(2,1)S(1)} %get-tuple-element.68), channel_id=1, source_target_pairs={{0,16},{8,24},{16,0},{24,8},{1,17},{9,25},{17,1},{25,9},{2,18},{10... | collective-permute-start | bytes 294920 | tf_op jit(solution)/shard_map/ppermute | solution.py:394
  47.7 6.4 %collective-permute-done.18.refs_4_ = bf16[64,768]{1,0:T(8,128)(2,1)S(1)} collective-permute-done((bf16[64,768]{1,0:T(8,128)(2,1)S(1)}, bf16[64,768]{1,0:T(8,128)(2,1)S(1)}, u32[]{:S(2)}, u32[]{:S(2)}) %collective-permute-start.18) | collective-permute-done | bytes 98336 | tf_op jit(solution)/shard_map/ppermute | solution.py:394
  54.7 2.6 %collective-permute-start.25 = (bf16[64,768]{1,0:T(8,128)(2,1)S(1)}, bf16[64,768]{1,0:T(8,128)(2,1)S(1)}, u32[]{:S(2)}, u32[]{:S(2)}) collective-permute-start(bf16[64,768]{1,0:T(8,128)(2,1)S(1)} %shard_map.109.refs_9_.refs_2_), channel_id=1, source_target_pairs={{0,24},{8,16},{16,8},{24,0},{1,25},{9,17},{17,9},{25,1},{2,26},{10... | collective-permute-start | bytes 294920 | tf_op jit(solution)/shard_map/ppermute | solution.py:394
  57.9 1.2 %collective-permute-start.23 = (bf16[64,768]{1,0:T(8,128)(2,1)S(1)}, bf16[64,768]{1,0:T(8,128)(2,1)S(1)}, u32[]{:S(2)}, u32[]{:S(2)}) collective-permute-start(bf16[64,768]{1,0:T(8,128)(2,1)S(1)} %shard_map.109.refs_9_.refs_2_), channel_id=1, source_target_pairs={{0,8},{8,0},{16,24},{24,16},{1,9},{9,1},{17,25},{25,17},{2,10},{10... | collective-permute-start | bytes 294920 | tf_op jit(solution)/shard_map/ppermute | solution.py:394
  60.7 2.3 %collective-permute-start.21 = (bf16[64,384]{1,0:T(8,128)(2,1)S(1)}, bf16[64,384]{1,0:T(8,128)(2,1)S(1)}, u32[]{:S(2)}, u32[]{:S(2)}) collective-permute-start(bf16[64,384]{1,0:T(8,128)(2,1)S(1)} %get-tuple-element.72), channel_id=1, source_target_pairs={{0,16},{8,24},{16,0},{24,8},{1,17},{9,25},{17,1},{25,9},{2,18},{10... | collective-permute-start | bytes 147464 | tf_op jit(solution)/shard_map/ppermute | solution.py:394
  63.0 1.8 %collective-permute-start.22 = (bf16[64,384]{1,0:T(8,128)(2,1)S(1)}, bf16[64,384]{1,0:T(8,128)(2,1)S(1)}, u32[]{:S(2)}, u32[]{:S(2)}) collective-permute-start(bf16[64,384]{1,0:T(8,128)(2,1)S(1)} %get-tuple-element.73), channel_id=1, source_target_pairs={{0,24},{8,16},{16,8},{24,0},{1,25},{9,17},{17,9},{25,1},{2,26},{10... | collective-permute-start | bytes 147464 | tf_op jit(solution)/shard_map/ppermute | solution.py:394
  64.8 3.6 %collective-permute-done.24.refs_4_ = bf16[64,768]{1,0:T(8,128)(2,1)S(1)} collective-permute-done((bf16[64,768]{1,0:T(8,128)(2,1)S(1)}, bf16[64,768]{1,0:T(8,128)(2,1)S(1)}, u32[]{:S(2)}, u32[]{:S(2)}) %collective-permute-start.24) | collective-permute-done | bytes 98336 | tf_op jit(solution)/shard_map/ppermute | solution.py:394
  70.0 1.4 %collective-permute-start.28 = (bf16[64,384]{1,0:T(8,128)(2,1)S(1)}, bf16[64,384]{1,0:T(8,128)(2,1)S(1)}, u32[]{:S(2)}, u32[]{:S(2)}) collective-permute-start(bf16[64,384]{1,0:T(8,128)(2,1)S(1)} %shard_map.112.refs_4_.refs_2_), channel_id=1, source_target_pairs={{0,24},{8,16},{16,8},{24,0},{1,25},{9,17},{17,9},{25,1},{2,26},{10... | collective-permute-start | bytes 147464 | tf_op jit(solution)/shard_map/ppermute | solution.py:394
  72.6 1.8 %collective-permute-start.26 = (bf16[64,384]{1,0:T(8,128)(2,1)S(1)}, bf16[64,384]{1,0:T(8,128)(2,1)S(1)}, u32[]{:S(2)}, u32[]{:S(2)}) collective-permute-start(bf16[64,384]{1,0:T(8,128)(2,1)S(1)} %shard_map.112.refs_4_.refs_2_), channel_id=1, source_target_pairs={{0,8},{8,0},{16,24},{24,16},{1,9},{9,1},{17,25},{25,17},{2,10},{10... | collective-permute-start | bytes 147464 | tf_op jit(solution)/shard_map/ppermute | solution.py:394
  74.4 3.5 %collective-permute-done.29.refs_3_ = bf16[256,768]{1,0:T(8,128)(2,1)S(1)} collective-permute-done((bf16[256,768]{1,0:T(8,128)(2,1)S(1)}, bf16[256,768]{1,0:T(8,128)(2,1)S(1)}, u32[]{:S(2)}, u32[]{:S(2)}) %collective-permute-start.29) | collective-permute-done | bytes 393248 | tf_op jit(solution)/shard_map/ppermute | solution.py:382
  78.9 1.7 %collective-permute-start.33 = (bf16[256,768]{1,0:T(8,128)(2,1)S(1)}, bf16[256,768]{1,0:T(8,128)(2,1)S(1)}, u32[]{:S(2)}, u32[]{:S(2)}) collective-permute-start(bf16[256,768]{1,0:T(8,128)(2,1)S(1)} %get-tuple-element.74.refs_6_.refs_2_), channel_id=1, source_target_pairs={{0,2},{1,5},{2,0},{3,7},{4,6},{5,1},{6,4},{7,3},{8,10},{9,13},{10,... | collective-permute-start | bytes 1179656 | tf_op jit(solution)/shard_map/ppermute | solution.py:382
  81.5 7.6 %collective-permute-done.30.refs_3_ = bf16[256,384]{1,0:T(8,128)(2,1)S(1)} collective-permute-done((bf16[256,384]{1,0:T(8,128)(2,1)S(1)}, bf16[256,384]{1,0:T(8,128)(2,1)S(1)}, u32[]{:S(2)}, u32[]{:S(2)}) %collective-permute-start.30) | collective-permute-done | bytes 196640 | tf_op jit(solution)/shard_map/ppermute | solution.py:382
  90.1 1.7 %collective-permute-start.31 = (bf16[256,384]{1,0:T(8,128)(2,1)S(1)}, bf16[256,384]{1,0:T(8,128)(2,1)S(1)}, u32[]{:S(2)}, u32[]{:S(2)}) collective-permute-start(bf16[256,384]{1,0:T(8,128)(2,1)S(1)} %get-tuple-element.75.refs_6_.refs_2_), channel_id=1, source_target_pairs={{0,2},{1,5},{2,0},{3,7},{4,6},{5,1},{6,4},{7,3},{8,10},{9,13},{10,... | collective-permute-start | bytes 589832 | tf_op jit(solution)/shard_map/ppermute | solution.py:382
  92.6 5.4 %shard_map.117 = (bf16[1,2,1024,1152]{3,2,1,0:T(8,128)(2,1)}, f32[1024,1024]{1,0:T(8,128)S(1)}) custom-call(s32[4]{0:T(128)S(1)} %pad_add_fusion.refs_0_, s32[2]{0:T(128)S(1)} %copy-done.5, bf16[1024,768]{1,0:T(8,128)(2,1)S(1)} %shard_map.116.refs_2_.refs_5_, bf16[1024,1024]{1,0:T(8,128)(2,1)S(1)} %get-tuple-element.64.refs_9_.refs_12_.refs_7_.refs_3_.refs_4_, ...), custom_call_target="tpu_custom_call" | custom-call | flops 1000 | bytes 1000 | tf_op jit(solution)/shard_map/pallas_call | solution.py:112
  98.9 5.2 %shard_map.119 = (bf16[1,2,1024,1152]{3,2,1,0:T(8,128)(2,1)}, f32[1024,1024]{1,0:T(8,128)S(1)}) custom-call(s32[4]{0:T(128)S(1)} %pad_add_fusion.refs_0_, s32[2]{0:T(128)S(1)} %copy-done.5, bf16[1024,768]{1,0:T(8,128)(2,1)S(1)} %collective-permute-done.36.refs_2_, ...), custom_call_target="tpu_custom_call", output_to_operand_aliasing={{0}: (6, {})} | custom-call | flops 1000 | bytes 1000 | tf_op jit(solution)/shard_map/pallas_call | solution.py:112
  104.1 9.4 %shard_map.120 = (bf16[1,2,1024,1152]{3,2,1,0:T(8,128)(2,1)}, bf16[1,1152,1024]{2,1,0:T(8,128)(2,1)}, f32[1,1024]{1,0:T(1,128)}) custom-call(s32[4]{0:T(128)S(1)} %pad_add_fusion.refs_0_, s32[2]{0:T(128)S(1)} %copy-done.5, bf16[1024,384]{1,0:T(8,128)(2,1)S(1)} %shard_map.118.refs_7_.refs_2_, ...), custom_call_target="tpu_custom_call", output_to_operand_aliasing={{0}: (9, {})} | custom-call | flops 1000 | bytes 1000 | tf_op jit(solution)/shard_map/pallas_call | solution.py:112
  (84 shorter events, 21.8 us)
Async XLA Ops:
  0.6 9.1 %collective-permute-start.1 = (bf16[256,1152]{1,0:T(8,128)(2,1)}, bf16[256,1152]{1,0:T(8,128)(2,1)S(1)}, u32[]{:S(2)}, u32[]{:S(2)}) collective-permute-start(bf16[256,1152]{1,0:T(8,128)(2,1)} %bitcast.5), channel_id=1, source_target_pairs={{0,1},{1,0},{2,3},{3,2},{4,5},{5,4},{6,7},{7,6},{8,9},{9,8},{10,11... | collective-permute-start | bytes 1769480 | tf_op jit(solution)/shard_map/ppermute | solution.py:370
  1.1 16.7 %collective-permute-start = (bf16[256,1152]{1,0:T(8,128)(2,1)}, bf16[256,1152]{1,0:T(8,128)(2,1)S(1)}, u32[]{:S(2)}, u32[]{:S(2)}) collective-permute-start(bf16[256,1152]{1,0:T(8,128)(2,1)} %bitcast.6), channel_id=1, source_target_pairs={{0,2},{1,3},{2,0},{3,1},{4,6},{5,7},{6,4},{7,5},{8,10},{9,11},{10,... | collective-permute-start | bytes 1769480 | tf_op jit(solution)/shard_map/ppermute | solution.py:373
  14.1 4.4 %collective-permute-start.4 = (bf16[256,1152]{1,0:T(8,128)(2,1)S(1)}, bf16[256,1152]{1,0:T(8,128)(2,1)S(1)}, u32[]{:S(2)}, u32[]{:S(2)}) collective-permute-start(bf16[256,1152]{1,0:T(8,128)(2,1)S(1)} %get-tuple-element.51), channel_id=1, source_target_pairs={{0,1},{1,0},{2,3},{3,2},{4,5},{5,4},{6,7},{7,6},{8,9},{9,8},{10,11... | collective-permute-start | bytes 1769480 | tf_op jit(solution)/shard_map/ppermute | solution.py:370
  14.3 4.2 %collective-permute-start.3 = (bf16[256,1152]{1,0:T(8,128)(2,1)S(1)}, bf16[256,1152]{1,0:T(8,128)(2,1)S(1)}, u32[]{:S(2)}, u32[]{:S(2)}) collective-permute-start(bf16[256,1152]{1,0:T(8,128)(2,1)S(1)} %get-tuple-element.48.refs_5_), channel_id=1, source_target_pairs={{0,1},{1,0},{2,3},{3,2},{4,5},{5,4},{6,7},{7,6},{8,9},{9,8},{10,11... | collective-permute-start | bytes 1769480 | tf_op jit(solution)/shard_map/ppermute | solution.py:370
  19.2 8.7 %collective-permute-start.8 = (bf16[256,768]{1,0:T(8,128)(2,1)S(1)}, bf16[256,768]{1,0:T(8,128)(2,1)S(1)}, u32[]{:S(2)}, u32[]{:S(2)}) collective-permute-start(bf16[256,768]{1,0:T(8,128)(2,1)S(1)} %get-tuple-element.52.refs_7_), channel_id=1, source_target_pairs={{0,2},{1,5},{2,0},{3,7},{4,6},{5,1},{6,4},{7,3},{8,10},{9,13},{10,... | collective-permute-start | bytes 1179656 | tf_op jit(solution)/shard_map/ppermute | solution.py:382
  25.2 6.1 %collective-permute-start.5 = (bf16[256,384]{1,0:T(8,128)(2,1)S(1)}, bf16[256,384]{1,0:T(8,128)(2,1)S(1)}, u32[]{:S(2)}, u32[]{:S(2)}) collective-permute-start(bf16[256,384]{1,0:T(8,128)(2,1)S(1)} %get-tuple-element.53), channel_id=1, source_target_pairs={{0,2},{1,5},{2,0},{3,7},{4,6},{5,1},{6,4},{7,3},{8,10},{9,13},{10,... | collective-permute-start | bytes 589832 | tf_op jit(solution)/shard_map/ppermute | solution.py:382
  28.8 12.0 %collective-permute-start.16 = (bf16[256,768]{1,0:T(8,128)(2,1)S(1)}, bf16[256,768]{1,0:T(8,128)(2,1)S(1)}, u32[]{:S(2)}, u32[]{:S(2)}) collective-permute-start(bf16[256,768]{1,0:T(8,128)(2,1)S(1)} %get-tuple-element.63), channel_id=1, source_target_pairs={{0,4},{1,3},{2,6},{3,1},{4,0},{5,7},{6,2},{7,5},{8,12},{9,11},{10,... | collective-permute-start | bytes 1179656 | tf_op jit(solution)/shard_map/ppermute | solution.py:382
  30.3 10.6 %collective-permute-start.15 = (bf16[256,768]{1,0:T(8,128)(2,1)S(1)}, bf16[256,768]{1,0:T(8,128)(2,1)S(1)}, u32[]{:S(2)}, u32[]{:S(2)}) collective-permute-start(bf16[256,768]{1,0:T(8,128)(2,1)S(1)} %get-tuple-element.56.refs_10_), channel_id=1, source_target_pairs={{0,2},{1,5},{2,0},{3,7},{4,6},{5,1},{6,4},{7,3},{8,10},{9,13},{10,... | collective-permute-start | bytes 1179656 | tf_op jit(solution)/shard_map/ppermute | solution.py:382
  33.5 4.8 %collective-permute-start.11 = (bf16[64,1152]{1,0:T(8,128)(2,1)S(1)}, bf16[64,1152]{1,0:T(8,128)(2,1)S(1)}, u32[]{:S(2)}, u32[]{:S(2)}) collective-permute-start(bf16[64,1152]{1,0:T(8,128)(2,1)S(1)} %get-tuple-element.60), channel_id=1, source_target_pairs={{0,1},{1,0},{2,3},{3,2},{4,5},{5,4},{6,7},{7,6},{8,9},{9,8},{10,11... | collective-permute-start | bytes 442376 | tf_op jit(solution)/shard_map/ppermute | solution.py:370
  34.0 4.3 %collective-permute-start.12 = (bf16[64,1152]{1,0:T(8,128)(2,1)S(1)}, bf16[64,1152]{1,0:T(8,128)(2,1)S(1)}, u32[]{:S(2)}, u32[]{:S(2)}) collective-permute-start(bf16[64,1152]{1,0:T(8,128)(2,1)S(1)} %get-tuple-element.61), channel_id=1, source_target_pairs={{0,1},{1,0},{2,3},{3,2},{4,5},{5,4},{6,7},{7,6},{8,9},{9,8},{10,11... | collective-permute-start | bytes 442376 | tf_op jit(solution)/shard_map/ppermute | solution.py:370
  41.7 5.9 %collective-permute-start.17 = (bf16[64,768]{1,0:T(8,128)(2,1)S(1)}, bf16[64,768]{1,0:T(8,128)(2,1)S(1)}, u32[]{:S(2)}, u32[]{:S(2)}) collective-permute-start(bf16[64,768]{1,0:T(8,128)(2,1)S(1)} %get-tuple-element.67), channel_id=1, source_target_pairs={{0,8},{8,0},{16,24},{24,16},{1,9},{9,1},{17,25},{25,17},{2,10},{10... | collective-permute-start | bytes 294920 | tf_op jit(solution)/shard_map/ppermute | solution.py:394
  43.4 10.7 %collective-permute-start.18 = (bf16[64,768]{1,0:T(8,128)(2,1)S(1)}, bf16[64,768]{1,0:T(8,128)(2,1)S(1)}, u32[]{:S(2)}, u32[]{:S(2)}) collective-permute-start(bf16[64,768]{1,0:T(8,128)(2,1)S(1)} %get-tuple-element.68), channel_id=1, source_target_pairs={{0,16},{8,24},{16,0},{24,8},{1,17},{9,25},{17,1},{25,9},{2,18},{10... | collective-permute-start | bytes 294920 | tf_op jit(solution)/shard_map/ppermute | solution.py:394
  46.0 8.1 %collective-permute-start.19 = (bf16[64,768]{1,0:T(8,128)(2,1)S(1)}, bf16[64,768]{1,0:T(8,128)(2,1)S(1)}, u32[]{:S(2)}, u32[]{:S(2)}) collective-permute-start(bf16[64,768]{1,0:T(8,128)(2,1)S(1)} %get-tuple-element.69), channel_id=1, source_target_pairs={{0,24},{8,16},{16,8},{24,0},{1,25},{9,17},{17,9},{25,1},{2,26},{10... | collective-permute-start | bytes 294920 | tf_op jit(solution)/shard_map/ppermute | solution.py:394
  46.2 12.9 %collective-permute-start.13 = (bf16[256,384]{1,0:T(8,128)(2,1)S(1)}, bf16[256,384]{1,0:T(8,128)(2,1)S(1)}, u32[]{:S(2)}, u32[]{:S(2)}) collective-permute-start(bf16[256,384]{1,0:T(8,128)(2,1)S(1)} %get-tuple-element.57.refs_4_), channel_id=1, source_target_pairs={{0,2},{1,5},{2,0},{3,7},{4,6},{5,1},{6,4},{7,3},{8,10},{9,13},{10,... | collective-permute-start | bytes 589832 | tf_op jit(solution)/shard_map/ppermute | solution.py:382
  47.0 12.1 %collective-permute-start.14 = (bf16[256,384]{1,0:T(8,128)(2,1)S(1)}, bf16[256,384]{1,0:T(8,128)(2,1)S(1)}, u32[]{:S(2)}, u32[]{:S(2)}) collective-permute-start(bf16[256,384]{1,0:T(8,128)(2,1)S(1)} %get-tuple-element.62), channel_id=1, source_target_pairs={{0,4},{1,3},{2,6},{3,1},{4,0},{5,7},{6,2},{7,5},{8,12},{9,11},{10,... | collective-permute-start | bytes 589832 | tf_op jit(solution)/shard_map/ppermute | solution.py:382
  54.7 8.3 %collective-permute-start.25 = (bf16[64,768]{1,0:T(8,128)(2,1)S(1)}, bf16[64,768]{1,0:T(8,128)(2,1)S(1)}, u32[]{:S(2)}, u32[]{:S(2)}) collective-permute-start(bf16[64,768]{1,0:T(8,128)(2,1)S(1)} %shard_map.109.refs_9_.refs_2_), channel_id=1, source_target_pairs={{0,24},{8,16},{16,8},{24,0},{1,25},{9,17},{17,9},{25,1},{2,26},{10... | collective-permute-start | bytes 294920 | tf_op jit(solution)/shard_map/ppermute | solution.py:394
  57.3 11.1 %collective-permute-start.24 = (bf16[64,768]{1,0:T(8,128)(2,1)S(1)}, bf16[64,768]{1,0:T(8,128)(2,1)S(1)}, u32[]{:S(2)}, u32[]{:S(2)}) collective-permute-start(bf16[64,768]{1,0:T(8,128)(2,1)S(1)} %shard_map.109.refs_9_.refs_2_), channel_id=1, source_target_pairs={{0,16},{8,24},{16,0},{24,8},{1,17},{9,25},{17,1},{25,9},{2,18},{10... | collective-permute-start | bytes 294920 | tf_op jit(solution)/shard_map/ppermute | solution.py:394
  57.9 10.5 %collective-permute-start.23 = (bf16[64,768]{1,0:T(8,128)(2,1)S(1)}, bf16[64,768]{1,0:T(8,128)(2,1)S(1)}, u32[]{:S(2)}, u32[]{:S(2)}) collective-permute-start(bf16[64,768]{1,0:T(8,128)(2,1)S(1)} %shard_map.109.refs_9_.refs_2_), channel_id=1, source_target_pairs={{0,8},{8,0},{16,24},{24,16},{1,9},{9,1},{17,25},{25,17},{2,10},{10... | collective-permute-start | bytes 294920 | tf_op jit(solution)/shard_map/ppermute | solution.py:394
  59.8 9.5 %collective-permute-start.20 = (bf16[64,384]{1,0:T(8,128)(2,1)S(1)}, bf16[64,384]{1,0:T(8,128)(2,1)S(1)}, u32[]{:S(2)}, u32[]{:S(2)}) collective-permute-start(bf16[64,384]{1,0:T(8,128)(2,1)S(1)} %get-tuple-element.71), channel_id=1, source_target_pairs={{0,8},{8,0},{16,24},{24,16},{1,9},{9,1},{17,25},{25,17},{2,10},{10... | collective-permute-start | bytes 147464 | tf_op jit(solution)/shard_map/ppermute | solution.py:394
  60.7 8.7 %collective-permute-start.21 = (bf16[64,384]{1,0:T(8,128)(2,1)S(1)}, bf16[64,384]{1,0:T(8,128)(2,1)S(1)}, u32[]{:S(2)}, u32[]{:S(2)}) collective-permute-start(bf16[64,384]{1,0:T(8,128)(2,1)S(1)} %get-tuple-element.72), channel_id=1, source_target_pairs={{0,16},{8,24},{16,0},{24,8},{1,17},{9,25},{17,1},{25,9},{2,18},{10... | collective-permute-start | bytes 147464 | tf_op jit(solution)/shard_map/ppermute | solution.py:394
  63.0 6.4 %collective-permute-start.22 = (bf16[64,384]{1,0:T(8,128)(2,1)S(1)}, bf16[64,384]{1,0:T(8,128)(2,1)S(1)}, u32[]{:S(2)}, u32[]{:S(2)}) collective-permute-start(bf16[64,384]{1,0:T(8,128)(2,1)S(1)} %get-tuple-element.73), channel_id=1, source_target_pairs={{0,24},{8,16},{16,8},{24,0},{1,25},{9,17},{17,9},{25,1},{2,26},{10... | collective-permute-start | bytes 147464 | tf_op jit(solution)/shard_map/ppermute | solution.py:394
  68.9 9.0 %collective-permute-start.29 = (bf16[256,768]{1,0:T(8,128)(2,1)S(1)}, bf16[256,768]{1,0:T(8,128)(2,1)S(1)}, u32[]{:S(2)}, u32[]{:S(2)}) collective-permute-start(bf16[256,768]{1,0:T(8,128)(2,1)S(1)} %shard_map.111.refs_6_.refs_2_), channel_id=1, source_target_pairs={{0,4},{1,3},{2,6},{3,1},{4,0},{5,7},{6,2},{7,5},{8,12},{9,11},{10,... | collective-permute-start | bytes 1179656 | tf_op jit(solution)/shard_map/ppermute | solution.py:382
  70.0 10.7 %collective-permute-start.28 = (bf16[64,384]{1,0:T(8,128)(2,1)S(1)}, bf16[64,384]{1,0:T(8,128)(2,1)S(1)}, u32[]{:S(2)}, u32[]{:S(2)}) collective-permute-start(bf16[64,384]{1,0:T(8,128)(2,1)S(1)} %shard_map.112.refs_4_.refs_2_), channel_id=1, source_target_pairs={{0,24},{8,16},{16,8},{24,0},{1,25},{9,17},{17,9},{25,1},{2,26},{10... | collective-permute-start | bytes 147464 | tf_op jit(solution)/shard_map/ppermute | solution.py:394
  71.4 9.3 %collective-permute-start.27 = (bf16[64,384]{1,0:T(8,128)(2,1)S(1)}, bf16[64,384]{1,0:T(8,128)(2,1)S(1)}, u32[]{:S(2)}, u32[]{:S(2)}) collective-permute-start(bf16[64,384]{1,0:T(8,128)(2,1)S(1)} %shard_map.112.refs_4_.refs_2_), channel_id=1, source_target_pairs={{0,16},{8,24},{16,0},{24,8},{1,17},{9,25},{17,1},{25,9},{2,18},{10... | collective-permute-start | bytes 147464 | tf_op jit(solution)/shard_map/ppermute | solution.py:394
  72.6 8.1 %collective-permute-start.26 = (bf16[64,384]{1,0:T(8,128)(2,1)S(1)}, bf16[64,384]{1,0:T(8,128)(2,1)S(1)}, u32[]{:S(2)}, u32[]{:S(2)}) collective-permute-start(bf16[64,384]{1,0:T(8,128)(2,1)S(1)} %shard_map.112.refs_4_.refs_2_), channel_id=1, source_target_pairs={{0,8},{8,0},{16,24},{24,16},{1,9},{9,1},{17,25},{25,17},{2,10},{10... | collective-permute-start | bytes 147464 | tf_op jit(solution)/shard_map/ppermute | solution.py:394
  78.5 13.3 %collective-permute-start.34 = (bf16[256,768]{1,0:T(8,128)(2,1)S(1)}, bf16[256,768]{1,0:T(8,128)(2,1)S(1)}, u32[]{:S(2)}, u32[]{:S(2)}) collective-permute-start(bf16[256,768]{1,0:T(8,128)(2,1)S(1)} %get-tuple-element.77.refs_3_), channel_id=1, source_target_pairs={{0,2},{1,5},{2,0},{3,7},{4,6},{5,1},{6,4},{7,3},{8,10},{9,13},{10,... | collective-permute-start | bytes 1179656 | tf_op jit(solution)/shard_map/ppermute | solution.py:382
  78.9 12.9 %collective-permute-start.33 = (bf16[256,768]{1,0:T(8,128)(2,1)S(1)}, bf16[256,768]{1,0:T(8,128)(2,1)S(1)}, u32[]{:S(2)}, u32[]{:S(2)}) collective-permute-start(bf16[256,768]{1,0:T(8,128)(2,1)S(1)} %get-tuple-element.74.refs_6_.refs_2_), channel_id=1, source_target_pairs={{0,2},{1,5},{2,0},{3,7},{4,6},{5,1},{6,4},{7,3},{8,10},{9,13},{10,... | collective-permute-start | bytes 1179656 | tf_op jit(solution)/shard_map/ppermute | solution.py:382
  81.2 7.9 %collective-permute-start.30 = (bf16[256,384]{1,0:T(8,128)(2,1)S(1)}, bf16[256,384]{1,0:T(8,128)(2,1)S(1)}, u32[]{:S(2)}, u32[]{:S(2)}) collective-permute-start(bf16[256,384]{1,0:T(8,128)(2,1)S(1)} %shard_map.114.refs_2_.refs_4_), channel_id=1, source_target_pairs={{0,4},{1,3},{2,6},{3,1},{4,0},{5,7},{6,2},{7,5},{8,12},{9,11},{10,... | collective-permute-start | bytes 589832 | tf_op jit(solution)/shard_map/ppermute | solution.py:382
  89.7 8.2 %collective-permute-start.32 = (bf16[256,384]{1,0:T(8,128)(2,1)S(1)}, bf16[256,384]{1,0:T(8,128)(2,1)S(1)}, u32[]{:S(2)}, u32[]{:S(2)}) collective-permute-start(bf16[256,384]{1,0:T(8,128)(2,1)S(1)} %get-tuple-element.76.refs_3_), channel_id=1, source_target_pairs={{0,2},{1,5},{2,0},{3,7},{4,6},{5,1},{6,4},{7,3},{8,10},{9,13},{10,... | collective-permute-start | bytes 589832 | tf_op jit(solution)/shard_map/ppermute | solution.py:382
  90.1 7.8 %collective-permute-start.31 = (bf16[256,384]{1,0:T(8,128)(2,1)S(1)}, bf16[256,384]{1,0:T(8,128)(2,1)S(1)}, u32[]{:S(2)}, u32[]{:S(2)}) collective-permute-start(bf16[256,384]{1,0:T(8,128)(2,1)S(1)} %get-tuple-element.75.refs_6_.refs_2_), channel_id=1, source_target_pairs={{0,2},{1,5},{2,0},{3,7},{4,6},{5,1},{6,4},{7,3},{8,10},{9,13},{10,... | collective-permute-start | bytes 589832 | tf_op jit(solution)/shard_map/ppermute | solution.py:382
  92.5 6.4 %collective-permute-start.36 = (bf16[1024,768]{1,0:T(8,128)(2,1)S(1)}, bf16[1024,768]{1,0:T(8,128)(2,1)S(1)}, u32[]{:S(2)}, u32[]{:S(2)}) collective-permute-start(bf16[1024,768]{1,0:T(8,128)(2,1)S(1)} %shard_map.116.refs_2_.refs_5_), channel_id=1, source_target_pairs={{0,1},{1,0},{2,3},{3,2},{4,5},{5,4},{6,7},{7,6},{8,9},{9,8},{10,11... | collective-permute-start | bytes 4718600 | tf_op jit(solution)/shard_map/ppermute | solution.py:370
  98.6 5.6 %collective-permute-start.35 = (bf16[1024,384]{1,0:T(8,128)(2,1)S(1)}, bf16[1024,384]{1,0:T(8,128)(2,1)S(1)}, u32[]{:S(2)}, u32[]{:S(2)}) collective-permute-start(bf16[1024,384]{1,0:T(8,128)(2,1)S(1)} %shard_map.118.refs_7_.refs_2_), channel_id=1, source_target_pairs={{0,1},{1,0},{2,3},{3,2},{4,5},{5,4},{6,7},{7,6},{8,9},{9,8},{10,11... | collective-permute-start | bytes 2359304 | tf_op jit(solution)/shard_map/ppermute | solution.py:370
  (12 other events, 36.2 us)

commit v6 on v5

--- a/solution.py
+++ b/solution.py
@@ -98,11 +98,12 @@
         scratch=(),
         aliases=(),
         heavy=False,
+        wait=(),
     ):
         count = len(operands)
         operands = list(operands)
         specs = list(specs or [HELD] * count)
-        waits = [] if self.last is None else [self.last]
+        waits = [*([] if self.last is None else [self.last]), *wait]
         keep = [k for k in self.keep if all(k is not o for o in operands)]
 
         def body(*refs):
@@ -487,7 +488,7 @@
         scaled = order(kernel, (mine, *pieces), [held(mine.shape, BF)], heavy=True)[0]
         return scaled, [to_layer(scaled, s) for s in range(1, layers)]
 
-    def join_pieces(scaled, pieces):
+    def join_pieces(scaled, pieces, wait):
         size = scaled.shape[1]
 
         def kernel(w, d, *refs):
@@ -496,33 +497,24 @@
             for s, ref in enumerate(refs[1:], 1):
                 out[span(layer_source(w[LAYER], s), piece), :] = ref[...]
 
-        done = order(kernel, (scaled, *pieces), [held((rows, size), BF)], heavy=True)[0]
-        return done, to_second(done)
-
-    def join_pair(done, got, heavy):
-        def kernel(w, d, done_ref, got_ref, out0, out1):
-            done_last = jnp.logical_or(w[CORE] == 1, w[FEAT] == 1)
-            out0[...] = pick(done_last, got_ref[...], done_ref[...])
-            out1[...] = pick(done_last, done_ref[...], got_ref[...])
-
-        pair = order(kernel, (done, got), [held(done.shape, BF)] * 2, heavy=heavy)
-        return pair, [to_first(block) for block in pair]
-
-    def join_all(pair, got):
-        def kernel(w, d, pair0, pair1, got0, got1, out):
+        outs = [held((rows, size), BF)]
+        done = order(kernel, (scaled, *pieces), outs, heavy=True, wait=wait)[0]
+        got_second, got_first = to_second(done), to_first(done)
+        return done, got_second, got_first, to_first(got_second)
+
+    def join_all(*blocks):
+        size = blocks[0].shape[1]
+
+        def kernel(w, d, *refs):
+            *refs, out = refs
+            y = w[FEAT]
             zero = w[CORE] == 0
-            y = w[FEAT]
             live = jnp.where(w[LAYER] <= d[w[CORE]], 1.0, 0.0).astype(BF)
-            for ref, number in (
-                (pair0, pick(zero, 2, y)),
-                (pair1, pick(zero, 3, 2 + y)),
-                (got0, pick(zero, 0, 1 - y)),
-                (got1, pick(zero, 1, 3 - y)),
-            ):
+            numbers = (2 + y, pick(zero, 3 - y, y), pick(zero, y, 3 - y), 1 - y)
+            for ref, number in zip(refs, numbers):
                 out[span(number, rows), :] = ref[...] * live
 
-        size = pair[0].shape[1]
-        full = order(kernel, (*pair, *got), [held((total, size), BF)], heavy=True)[0]
+        full = order(kernel, blocks, [held((total, size), BF)], heavy=True)[0]
         return full, to_core(full)
 
     reduced = [
@@ -532,21 +524,18 @@
     turned, tokens = turn(order, (act_near, act_far), ((own, near), (far, far_near)))
     order.keep = [writeout, cutoff, turned, tokens]
     count = len(chunks)
-    sent, joined, pairs = send_pieces(*reduced[0], False), [], []
+    sent, joined = send_pieces(*reduced[0], False), []
     for k in range(count):
         scaled = scale_piece(*sent)
         if k + 1 < count:
             sent = send_pieces(*reduced[k + 1], True)
-        if k > 0:
-            pairs.append(join_pair(*joined[k - 1], True))
-        joined.append(join_pieces(*scaled))
-    pairs.append(join_pair(*joined[-1], False))
-    scaled = join_all(*pairs[0])
+        joined.append(join_pieces(*scaled, [joined[k - 1][2]] if k > 0 else []))
+    scaled = join_all(*joined[0])
     sens = dec = None
     for k, (lo, hi) in enumerate(chunks[:-1]):
         own, other = scaled
         dec, sens = target_gradients(order, True, own, turned, writeout, lo, hi, sens, dec)
-        following = join_all(*pairs[k + 1])
+        following = join_all(*joined[k + 1])
         dec, sens = target_gradients(order, False, other, turned, writeout, lo, hi, sens, dec)
         scaled = following
     order.keep = []

time: 114 us -> 111 us (0.974)
  waiting for transfers between devices: 25.7 us -> 24.4 us
  Pallas kernels: 50.4 us -> 49.2 us
    ppermute x12, waiting for transfers between devices: 13.7 us -> 12.5 us  [mixed(): return lambda a: lax.ppermute(a, ('feat', 'tok'), pairs)]
    pallas_call x27 -> x25, Pallas kernels: 50.4 us -> 49.2 us  [__call__(): pl.pallas_call(body, grid_spec=pltpu.PrefetchScalarGridSpec(num_scalar_pr...]
  transfers between devices with their start and end apart: 37 -> 37, of which waited for: 8 -> 7; matrix products, arithmetic and copies ran while one was open for 0% -> 0% of each run, Pallas kernels for 35% -> 35%
where the time goes in v6:
time: 111 us
  Pallas kernels  49.2 us (44%)
  starting transfers between devices  35.6 us (32%)
  waiting for transfers between devices  24.4 us (22%)
    pallas_call x25, Pallas kernels, __call__(): pl.pallas_call(body, grid_spec=pltpu.PrefetchScalarGridSpec(num_scalar_pr...  49.2 us
    ppermute x12, starting transfers between devices, to_layer(): lax.ppermute(a, 'layer', [(l, l ^ s if binary else (l + s) % layers) for...  18.3 us
    ppermute x12, waiting for transfers between devices, mixed(): return lambda a: lax.ppermute(a, ('feat', 'tok'), pairs)  12.5 us
    ppermute x12, starting transfers between devices, mixed(): return lambda a: lax.ppermute(a, ('feat', 'tok'), pairs)  11.5 us
    ppermute x12, waiting for transfers between devices, to_layer(): lax.ppermute(a, 'layer', [(l, l ^ s if binary else (l + s) % layers) for...  9.98 us
    ppermute x12, starting transfers between devices, to_core(): return lax.ppermute(a, 'tok', [(t, t ^ 1) for t in range(toks)])  3.17 us
    ppermute x1, starting transfers between devices, to_side(): return lax.ppermute(a, 'tok', [(t, t ^ 2) for t in range(toks)])  2.57 us
  transfers between devices with their start and end apart: 37, of which 7 were waited for; matrix products, arithmetic and copies ran while one was open for 0% of the time, Pallas kernels for 35%

profile of v6, /device:TPU:0, one launch (start us, length us, event | category | flops | bytes accessed | tf_op | source)
XLA Modules:
  0.0 110.9 jit_solution(18163285139791416718)
XLA Ops:
  1.1 2.6 %collective-permute-start = (bf16[256,1152]{1,0:T(8,128)(2,1)}, bf16[256,1152]{1,0:T(8,128)(2,1)S(1)}, u32[]{:S(2)}, u32[]{:S(2)}) collective-permute-start(bf16[256,1152]{1,0:T(8,128)(2,1)} %bitcast.6), channel_id=1, source_target_pairs={{0,2},{1,3},{2,0},{3,1},{4,6},{5,7},{6,4},{7,5},{8,10},{9,11},{10,... | collective-permute-start | bytes 1769480 | tf_op jit(solution)/shard_map/ppermute | solution.py:374
  4.5 5.3 %shard_map.94 = (bf16[1,1152,1024]{2,1,0:T(8,128)(2,1)S(1)}, s32[1,1024,1024]{2,1,0:T(8,128)S(1)}, bf16[1,2,1024,1152]{3,2,1,0:T(8,128)(2,1)S(1)}, bf16[2,256,1152]{2,1,0:T(8,128)(2,1)S(1)}) custom-call(s32[4]{0:T(128)S(1)} %pad_add_fusion.refs_0_, s32[2]{0:T(128)S(1)} %copy-done.4, bf16[1,1152,1024]{2,1,0:T(8,128)(2,1)} %refs_2_.1, ...), custom_call_target="tpu_custom_call" | custom-call | flops 99999997952 | bytes 1000 | tf_op jit(solution)/shard_map/pallas_call | solution.py:113
  9.8 2.2 %shard_map.95.refs_2_.refs_5_ = bf16[512,1024]{1,0:T(8,128)(2,1)S(1)} custom-call(s32[4]{0:T(128)S(1)} %pad_add_fusion.refs_0_, s32[2]{0:T(128)S(1)} %copy-done.5, bf16[256,1152]{1,0:T(8,128)(2,1)S(1)} %bitcast.7, bf16[256,1152]{1,0:T(8,128)(2,1)S(1)} %collective-permute-done.1.refs_3_.refs_5_, bf16[1,1152,1024]{2,1,0:T(8,128)(2,1)S(1)} %get-tuple-element.40.refs_4_.refs_7_, ...), custom_call_target="tpu_custom_call" | custom-call | flops 1000 | bytes 1000 | tf_op jit(solution)/shard_map/pallas_call | solution.py:113
  12.0 2.1 %shard_map.96 = (bf16[256,1152]{1,0:T(8,128)(2,1)S(1)}, bf16[256,1152]{1,0:T(8,128)(2,1)S(1)}) custom-call(s32[4]{0:T(128)S(1)} %pad_add_fusion.refs_0_, s32[2]{0:T(128)S(1)} %copy-done.5, bf16[512,1024]{1,0:T(8,128)(2,1)S(1)} %shard_map.95.refs_2_.refs_5_, bf16[1,2,1024,1152]{3,2,1,0:T(8,128)(2,1)S(1)} %get-tuple-element.42.refs_3_.refs_10_.refs_7_.refs_8_.refs_4_.refs_5_, ...), custom_call_target="tpu_custom_call" | custom-call | flops 1000 | bytes 1000 | tf_op jit(solution)/shard_map/pallas_call | solution.py:113
  14.7 2.1 %shard_map.97 = (f32[256,1152]{1,0:T(8,128)S(1)}, f32[256,1152]{1,0:T(8,128)S(1)}) custom-call(s32[4]{0:T(128)S(1)} %pad_add_fusion.refs_0_, s32[2]{0:T(128)S(1)} %copy-done.5, bf16[512,1024]{1,0:T(8,128)(2,1)S(1)} %shard_map.95.refs_2_.refs_5_, bf16[1,2,1024,1152]{3,2,1,0:T(8,128)(2,1)S(1)} %get-tuple-element.42.refs_3_.refs_10_.refs_7_.refs_8_.refs_4_.refs_5_, ...), custom_call_target="tpu_custom_call" | custom-call | flops 1000 | bytes 1000 | tf_op jit(solution)/shard_map/pallas_call | solution.py:113
  19.2 1.8 %collective-permute-start.8 = (bf16[256,768]{1,0:T(8,128)(2,1)S(1)}, bf16[256,768]{1,0:T(8,128)(2,1)S(1)}, u32[]{:S(2)}, u32[]{:S(2)}) collective-permute-start(bf16[256,768]{1,0:T(8,128)(2,1)S(1)} %get-tuple-element.48.refs_7_), channel_id=1, source_target_pairs={{0,2},{1,5},{2,0},{3,7},{4,6},{5,1},{6,4},{7,3},{8,10},{9,13},{10,... | collective-permute-start | bytes 1179656 | tf_op jit(solution)/shard_map/ppermute | solution.py:383
  21.1 2.2 %shard_map.100.refs_2_.refs_4_.refs_3_ = bf16[512,1024]{1,0:T(8,128)(2,1)S(1)} custom-call(s32[4]{0:T(128)S(1)} %pad_add_fusion.refs_0_, s32[2]{0:T(128)S(1)} %copy-done.5, bf16[256,1152]{1,0:T(8,128)(2,1)S(1)} %shard_map.98.refs_6_.refs_2_, bf16[256,1152]{1,0:T(8,128)(2,1)S(1)} %collective-permute-done.2.refs_3_.refs_7_, ...), custom_call_target="tpu_custom_call" | custom-call | flops 99999997952 | bytes 1000 | tf_op jit(solution)/shard_map/pallas_call | solution.py:113
  23.2 1.4 %shard_map.101 = (bf16[128,1152]{1,0:T(8,128)(2,1)S(1)}, bf16[128,1152]{1,0:T(8,128)(2,1)S(1)}) custom-call(s32[4]{0:T(128)S(1)} %pad_add_fusion.refs_0_, s32[2]{0:T(128)S(1)} %copy-done.5, bf16[512,1024]{1,0:T(8,128)(2,1)S(1)} %shard_map.100.refs_2_.refs_4_.refs_3_, ...), custom_call_target="tpu_custom_call" | custom-call | flops 1000 | bytes 1000 | tf_op jit(solution)/shard_map/pallas_call | solution.py:113
  25.2 1.3 %collective-permute-start.5 = (bf16[256,384]{1,0:T(8,128)(2,1)S(1)}, bf16[256,384]{1,0:T(8,128)(2,1)S(1)}, u32[]{:S(2)}, u32[]{:S(2)}) collective-permute-start(bf16[256,384]{1,0:T(8,128)(2,1)S(1)} %get-tuple-element.49), channel_id=1, source_target_pairs={{0,2},{1,5},{2,0},{3,7},{4,6},{5,1},{6,4},{7,3},{8,10},{9,13},{10,... | collective-permute-start | bytes 589832 | tf_op jit(solution)/shard_map/ppermute | solution.py:383
  26.5 1.4 %shard_map.102.refs_7_.refs_10_ = f32[256,1152]{1,0:T(8,128)S(1)} custom-call(s32[4]{0:T(128)S(1)} %pad_add_fusion.refs_0_, s32[2]{0:T(128)S(1)} %copy-done.5, bf16[512,1024]{1,0:T(8,128)(2,1)S(1)} %shard_map.100.refs_2_.refs_4_.refs_3_, bf16[1,2,1024,1152]{3,2,1,0:T(8,128)(2,1)S(1)} %get-tuple-element.42.refs_3_.refs_10_.refs_7_.refs_8_.refs_4_.refs_5_, ...), custom_call_target="tpu_custom_call" | custom-call | flops 1000 | bytes 1000 | tf_op jit(solution)/shard_map/pallas_call | solution.py:113
  28.8 1.5 %collective-permute-start.16 = (bf16[256,768]{1,0:T(8,128)(2,1)S(1)}, bf16[256,768]{1,0:T(8,128)(2,1)S(1)}, u32[]{:S(2)}, u32[]{:S(2)}) collective-permute-start(bf16[256,768]{1,0:T(8,128)(2,1)S(1)} %get-tuple-element.59), channel_id=1, source_target_pairs={{0,4},{1,3},{2,6},{3,1},{4,0},{5,7},{6,2},{7,5},{8,12},{9,11},{10,... | collective-permute-start | bytes 1179656 | tf_op jit(solution)/shard_map/ppermute | solution.py:383
  32.0 1.4 %shard_map.105 = (bf16[64,1152]{1,0:T(8,128)(2,1)S(1)}, bf16[64,1152]{1,0:T(8,128)(2,1)S(1)}, bf16[64,1152]{1,0:T(8,128)(2,1)S(1)}, bf16[64,1152]{1,0:T(8,128)(2,1)S(1)}) custom-call(s32[4]{0:T(128)S(1)} %pad_add_fusion.refs_0_, s32[2]{0:T(128)S(1)} %copy-done.5, bf16[512,1024]{1,0:T(8,128)(2,1)S(1)} %shard_map.100.refs_2_.refs_4_.refs_3_, ...), custom_call_target="tpu_custom_call" | custom-call | flops 1000 | bytes 1000 | tf_op jit(solution)/shard_map/pallas_call | solution.py:113
  35.0 1.4 %shard_map.106.refs_8_.refs_2_ = f32[256,1152]{1,0:T(8,128)S(1)} custom-call(s32[4]{0:T(128)S(1)} %pad_add_fusion.refs_0_, s32[2]{0:T(128)S(1)} %copy-done.5, bf16[512,1024]{1,0:T(8,128)(2,1)S(1)} %shard_map.100.refs_2_.refs_4_.refs_3_, bf16[1,2,1024,1152]{3,2,1,0:T(8,128)(2,1)S(1)} %get-tuple-element.42.refs_3_.refs_10_.refs_7_.refs_8_.refs_4_.refs_5_, ...), custom_call_target="tpu_custom_call" | custom-call | flops 1000 | bytes 1000 | tf_op jit(solution)/shard_map/pallas_call | solution.py:113
  36.4 1.8 %shard_map.107 = (bf16[1024,1024]{1,0:T(8,128)(2,1)S(1)}, bf16[1152,1024]{1,0:T(8,128)(2,1)S(1)}) custom-call(s32[4]{0:T(128)S(1)} %pad_add_fusion.refs_0_, s32[2]{0:T(128)S(1)} %copy-done.5, bf16[512,1024]{1,0:T(8,128)(2,1)S(1)} %copy-done.1, bf16[512,1024]{1,0:T(8,128)(2,1)S(1)} %shard_map.100.refs_2_.refs_4_.refs_3_, bf16[256,1152]{1,0:T(8,128)(2,1)S(1)} %bitcast.8, ...), custom_call_target="tpu_custom_call" | custom-call | flops 1000 | bytes 1000 | tf_op jit(solution)/shard_map/pallas_call | solution.py:113
  38.3 2.5 %collective-permute-done.16.refs_8_ = bf16[256,768]{1,0:T(8,128)(2,1)S(1)} collective-permute-done((bf16[256,768]{1,0:T(8,128)(2,1)S(1)}, bf16[256,768]{1,0:T(8,128)(2,1)S(1)}, u32[]{:S(2)}, u32[]{:S(2)}) %collective-permute-start.16) | collective-permute-done | bytes 393248 | tf_op jit(solution)/shard_map/ppermute | solution.py:383
  41.7 1.6 %collective-permute-start.17 = (bf16[64,768]{1,0:T(8,128)(2,1)S(1)}, bf16[64,768]{1,0:T(8,128)(2,1)S(1)}, u32[]{:S(2)}, u32[]{:S(2)}) collective-permute-start(bf16[64,768]{1,0:T(8,128)(2,1)S(1)} %get-tuple-element.63), channel_id=1, source_target_pairs={{0,8},{8,0},{16,24},{24,16},{1,9},{9,1},{17,25},{25,17},{2,10},{10... | collective-permute-start | bytes 294920 | tf_op jit(solution)/shard_map/ppermute | solution.py:395
  43.4 2.6 %collective-permute-start.18 = (bf16[64,768]{1,0:T(8,128)(2,1)S(1)}, bf16[64,768]{1,0:T(8,128)(2,1)S(1)}, u32[]{:S(2)}, u32[]{:S(2)}) collective-permute-start(bf16[64,768]{1,0:T(8,128)(2,1)S(1)} %get-tuple-element.64), channel_id=1, source_target_pairs={{0,16},{8,24},{16,0},{24,8},{1,17},{9,25},{17,1},{25,9},{2,18},{10... | collective-permute-start | bytes 294920 | tf_op jit(solution)/shard_map/ppermute | solution.py:395
  47.7 6.4 %collective-permute-done.18.refs_4_ = bf16[64,768]{1,0:T(8,128)(2,1)S(1)} collective-permute-done((bf16[64,768]{1,0:T(8,128)(2,1)S(1)}, bf16[64,768]{1,0:T(8,128)(2,1)S(1)}, u32[]{:S(2)}, u32[]{:S(2)}) %collective-permute-start.18) | collective-permute-done | bytes 98336 | tf_op jit(solution)/shard_map/ppermute | solution.py:395
  54.7 2.6 %collective-permute-start.25 = (bf16[64,768]{1,0:T(8,128)(2,1)S(1)}, bf16[64,768]{1,0:T(8,128)(2,1)S(1)}, u32[]{:S(2)}, u32[]{:S(2)}) collective-permute-start(bf16[64,768]{1,0:T(8,128)(2,1)S(1)} %shard_map.109.refs_9_.refs_2_), channel_id=1, source_target_pairs={{0,24},{8,16},{16,8},{24,0},{1,25},{9,17},{17,9},{25,1},{2,26},{10... | collective-permute-start | bytes 294920 | tf_op jit(solution)/shard_map/ppermute | solution.py:395
  57.9 1.2 %collective-permute-start.23 = (bf16[64,768]{1,0:T(8,128)(2,1)S(1)}, bf16[64,768]{1,0:T(8,128)(2,1)S(1)}, u32[]{:S(2)}, u32[]{:S(2)}) collective-permute-start(bf16[64,768]{1,0:T(8,128)(2,1)S(1)} %shard_map.109.refs_9_.refs_2_), channel_id=1, source_target_pairs={{0,8},{8,0},{16,24},{24,16},{1,9},{9,1},{17,25},{25,17},{2,10},{10... | collective-permute-start | bytes 294920 | tf_op jit(solution)/shard_map/ppermute | solution.py:395
  60.7 2.3 %collective-permute-start.21 = (bf16[64,384]{1,0:T(8,128)(2,1)S(1)}, bf16[64,384]{1,0:T(8,128)(2,1)S(1)}, u32[]{:S(2)}, u32[]{:S(2)}) collective-permute-start(bf16[64,384]{1,0:T(8,128)(2,1)S(1)} %get-tuple-element.68), channel_id=1, source_target_pairs={{0,16},{8,24},{16,0},{24,8},{1,17},{9,25},{17,1},{25,9},{2,18},{10... | collective-permute-start | bytes 147464 | tf_op jit(solution)/shard_map/ppermute | solution.py:395
  63.0 1.8 %collective-permute-start.22 = (bf16[64,384]{1,0:T(8,128)(2,1)S(1)}, bf16[64,384]{1,0:T(8,128)(2,1)S(1)}, u32[]{:S(2)}, u32[]{:S(2)}) collective-permute-start(bf16[64,384]{1,0:T(8,128)(2,1)S(1)} %get-tuple-element.69), channel_id=1, source_target_pairs={{0,24},{8,16},{16,8},{24,0},{1,25},{9,17},{17,9},{25,1},{2,26},{10... | collective-permute-start | bytes 147464 | tf_op jit(solution)/shard_map/ppermute | solution.py:395
  64.8 3.6 %collective-permute-done.24.refs_4_ = bf16[64,768]{1,0:T(8,128)(2,1)S(1)} collective-permute-done((bf16[64,768]{1,0:T(8,128)(2,1)S(1)}, bf16[64,768]{1,0:T(8,128)(2,1)S(1)}, u32[]{:S(2)}, u32[]{:S(2)}) %collective-permute-start.24) | collective-permute-done | bytes 98336 | tf_op jit(solution)/shard_map/ppermute | solution.py:395
  70.4 1.3 %collective-permute-start.28 = (bf16[64,384]{1,0:T(8,128)(2,1)S(1)}, bf16[64,384]{1,0:T(8,128)(2,1)S(1)}, u32[]{:S(2)}, u32[]{:S(2)}) collective-permute-start(bf16[64,384]{1,0:T(8,128)(2,1)S(1)} %shard_map.112.refs_2_.refs_6_), channel_id=1, source_target_pairs={{0,24},{8,16},{16,8},{24,0},{1,25},{9,17},{17,9},{25,1},{2,26},{10... | collective-permute-start | bytes 147464 | tf_op jit(solution)/shard_map/ppermute | solution.py:395
  72.6 2.3 %collective-permute-start.26 = (bf16[64,384]{1,0:T(8,128)(2,1)S(1)}, bf16[64,384]{1,0:T(8,128)(2,1)S(1)}, u32[]{:S(2)}, u32[]{:S(2)}) collective-permute-start(bf16[64,384]{1,0:T(8,128)(2,1)S(1)} %shard_map.112.refs_2_.refs_6_), channel_id=1, source_target_pairs={{0,8},{8,0},{16,24},{24,16},{1,9},{9,1},{17,25},{25,17},{2,10},{10... | collective-permute-start | bytes 147464 | tf_op jit(solution)/shard_map/ppermute | solution.py:395
  74.9 4.7 %collective-permute-done.33.refs_3_ = bf16[256,768]{1,0:T(8,128)(2,1)S(1)} collective-permute-done((bf16[256,768]{1,0:T(8,128)(2,1)S(1)}, bf16[256,768]{1,0:T(8,128)(2,1)S(1)}, u32[]{:S(2)}, u32[]{:S(2)}) %collective-permute-start.33) | collective-permute-done | bytes 393248 | tf_op jit(solution)/shard_map/ppermute | solution.py:383
  79.5 1.6 %collective-permute-start.34 = (bf16[256,768]{1,0:T(8,128)(2,1)S(1)}, bf16[256,768]{1,0:T(8,128)(2,1)S(1)}, u32[]{:S(2)}, u32[]{:S(2)}) collective-permute-start(bf16[256,768]{1,0:T(8,128)(2,1)S(1)} %collective-permute-done.33.refs_3_), channel_id=1, source_target_pairs={{0,2},{1,5},{2,0},{3,7},{4,6},{5,1},{6,4},{7,3},{8,10},{9,13},{10,... | collective-permute-start | bytes 1179656 | tf_op jit(solution)/shard_map/ppermute | solution.py:383
  82.5 5.3 %collective-permute-done.30.refs_3_ = bf16[256,384]{1,0:T(8,128)(2,1)S(1)} collective-permute-done((bf16[256,384]{1,0:T(8,128)(2,1)S(1)}, bf16[256,384]{1,0:T(8,128)(2,1)S(1)}, u32[]{:S(2)}, u32[]{:S(2)}) %collective-permute-start.30) | collective-permute-done | bytes 196640 | tf_op jit(solution)/shard_map/ppermute | solution.py:383
  87.8 1.2 %collective-permute-start.32 = (bf16[256,384]{1,0:T(8,128)(2,1)S(1)}, bf16[256,384]{1,0:T(8,128)(2,1)S(1)}, u32[]{:S(2)}, u32[]{:S(2)}) collective-permute-start(bf16[256,384]{1,0:T(8,128)(2,1)S(1)} %collective-permute-done.30.refs_3_), channel_id=1, source_target_pairs={{0,2},{1,5},{2,0},{3,7},{4,6},{5,1},{6,4},{7,3},{8,10},{9,13},{10,... | collective-permute-start | bytes 589832 | tf_op jit(solution)/shard_map/ppermute | solution.py:383
  89.7 5.3 %shard_map.115 = (bf16[1,2,1024,1152]{3,2,1,0:T(8,128)(2,1)}, f32[1024,1024]{1,0:T(8,128)S(1)}) custom-call(s32[4]{0:T(128)S(1)} %pad_add_fusion.refs_0_, s32[2]{0:T(128)S(1)} %copy-done.5, bf16[1024,768]{1,0:T(8,128)(2,1)S(1)} %shard_map.114.refs_2_.refs_5_, bf16[1024,1024]{1,0:T(8,128)(2,1)S(1)} %get-tuple-element.60.refs_9_.refs_12_.refs_10_.refs_3_.refs_4_, ...), custom_call_target="tpu_custom_call" | custom-call | flops 1000 | bytes 1000 | tf_op jit(solution)/shard_map/pallas_call | solution.py:113
  96.3 5.2 %shard_map.117 = (bf16[1,2,1024,1152]{3,2,1,0:T(8,128)(2,1)}, f32[1024,1024]{1,0:T(8,128)S(1)}) custom-call(s32[4]{0:T(128)S(1)} %pad_add_fusion.refs_0_, s32[2]{0:T(128)S(1)} %copy-done.5, bf16[1024,768]{1,0:T(8,128)(2,1)S(1)} %collective-permute-done.36.refs_2_, ...), custom_call_target="tpu_custom_call", output_to_operand_aliasing={{0}: (6, {})} | custom-call | flops 1000 | bytes 1000 | tf_op jit(solution)/shard_map/pallas_call | solution.py:113
  101.5 9.4 %shard_map.118 = (bf16[1,2,1024,1152]{3,2,1,0:T(8,128)(2,1)}, bf16[1,1152,1024]{2,1,0:T(8,128)(2,1)}, f32[1,1024]{1,0:T(1,128)}) custom-call(s32[4]{0:T(128)S(1)} %pad_add_fusion.refs_0_, s32[2]{0:T(128)S(1)} %copy-done.5, bf16[1024,384]{1,0:T(8,128)(2,1)S(1)} %shard_map.116.refs_7_.refs_2_, ...), custom_call_target="tpu_custom_call", output_to_operand_aliasing={{0}: (9, {})} | custom-call | flops 1000 | bytes 1000 | tf_op jit(solution)/shard_map/pallas_call | solution.py:113
  (82 shorter events, 20.7 us)
Async XLA Ops:
  0.6 9.1 %collective-permute-start.1 = (bf16[256,1152]{1,0:T(8,128)(2,1)}, bf16[256,1152]{1,0:T(8,128)(2,1)S(1)}, u32[]{:S(2)}, u32[]{:S(2)}) collective-permute-start(bf16[256,1152]{1,0:T(8,128)(2,1)} %bitcast.5), channel_id=1, source_target_pairs={{0,1},{1,0},{2,3},{3,2},{4,5},{5,4},{6,7},{7,6},{8,9},{9,8},{10,11... | collective-permute-start | bytes 1769480 | tf_op jit(solution)/shard_map/ppermute | solution.py:371
  1.1 16.7 %collective-permute-start = (bf16[256,1152]{1,0:T(8,128)(2,1)}, bf16[256,1152]{1,0:T(8,128)(2,1)S(1)}, u32[]{:S(2)}, u32[]{:S(2)}) collective-permute-start(bf16[256,1152]{1,0:T(8,128)(2,1)} %bitcast.6), channel_id=1, source_target_pairs={{0,2},{1,3},{2,0},{3,1},{4,6},{5,7},{6,4},{7,5},{8,10},{9,11},{10,... | collective-permute-start | bytes 1769480 | tf_op jit(solution)/shard_map/ppermute | solution.py:374
  14.1 4.4 %collective-permute-start.4 = (bf16[256,1152]{1,0:T(8,128)(2,1)S(1)}, bf16[256,1152]{1,0:T(8,128)(2,1)S(1)}, u32[]{:S(2)}, u32[]{:S(2)}) collective-permute-start(bf16[256,1152]{1,0:T(8,128)(2,1)S(1)} %get-tuple-element.47), channel_id=1, source_target_pairs={{0,1},{1,0},{2,3},{3,2},{4,5},{5,4},{6,7},{7,6},{8,9},{9,8},{10,11... | collective-permute-start | bytes 1769480 | tf_op jit(solution)/shard_map/ppermute | solution.py:371
  14.3 4.2 %collective-permute-start.3 = (bf16[256,1152]{1,0:T(8,128)(2,1)S(1)}, bf16[256,1152]{1,0:T(8,128)(2,1)S(1)}, u32[]{:S(2)}, u32[]{:S(2)}) collective-permute-start(bf16[256,1152]{1,0:T(8,128)(2,1)S(1)} %get-tuple-element.44.refs_5_), channel_id=1, source_target_pairs={{0,1},{1,0},{2,3},{3,2},{4,5},{5,4},{6,7},{7,6},{8,9},{9,8},{10,11... | collective-permute-start | bytes 1769480 | tf_op jit(solution)/shard_map/ppermute | solution.py:371
  19.2 8.7 %collective-permute-start.8 = (bf16[256,768]{1,0:T(8,128)(2,1)S(1)}, bf16[256,768]{1,0:T(8,128)(2,1)S(1)}, u32[]{:S(2)}, u32[]{:S(2)}) collective-permute-start(bf16[256,768]{1,0:T(8,128)(2,1)S(1)} %get-tuple-element.48.refs_7_), channel_id=1, source_target_pairs={{0,2},{1,5},{2,0},{3,7},{4,6},{5,1},{6,4},{7,3},{8,10},{9,13},{10,... | collective-permute-start | bytes 1179656 | tf_op jit(solution)/shard_map/ppermute | solution.py:383
  25.2 6.1 %collective-permute-start.5 = (bf16[256,384]{1,0:T(8,128)(2,1)S(1)}, bf16[256,384]{1,0:T(8,128)(2,1)S(1)}, u32[]{:S(2)}, u32[]{:S(2)}) collective-permute-start(bf16[256,384]{1,0:T(8,128)(2,1)S(1)} %get-tuple-element.49), channel_id=1, source_target_pairs={{0,2},{1,5},{2,0},{3,7},{4,6},{5,1},{6,4},{7,3},{8,10},{9,13},{10,... | collective-permute-start | bytes 589832 | tf_op jit(solution)/shard_map/ppermute | solution.py:383
  28.8 12.0 %collective-permute-start.16 = (bf16[256,768]{1,0:T(8,128)(2,1)S(1)}, bf16[256,768]{1,0:T(8,128)(2,1)S(1)}, u32[]{:S(2)}, u32[]{:S(2)}) collective-permute-start(bf16[256,768]{1,0:T(8,128)(2,1)S(1)} %get-tuple-element.59), channel_id=1, source_target_pairs={{0,4},{1,3},{2,6},{3,1},{4,0},{5,7},{6,2},{7,5},{8,12},{9,11},{10,... | collective-permute-start | bytes 1179656 | tf_op jit(solution)/shard_map/ppermute | solution.py:383
  30.3 10.6 %collective-permute-start.15 = (bf16[256,768]{1,0:T(8,128)(2,1)S(1)}, bf16[256,768]{1,0:T(8,128)(2,1)S(1)}, u32[]{:S(2)}, u32[]{:S(2)}) collective-permute-start(bf16[256,768]{1,0:T(8,128)(2,1)S(1)} %get-tuple-element.52.refs_10_), channel_id=1, source_target_pairs={{0,2},{1,5},{2,0},{3,7},{4,6},{5,1},{6,4},{7,3},{8,10},{9,13},{10,... | collective-permute-start | bytes 1179656 | tf_op jit(solution)/shard_map/ppermute | solution.py:383
  33.5 4.8 %collective-permute-start.11 = (bf16[64,1152]{1,0:T(8,128)(2,1)S(1)}, bf16[64,1152]{1,0:T(8,128)(2,1)S(1)}, u32[]{:S(2)}, u32[]{:S(2)}) collective-permute-start(bf16[64,1152]{1,0:T(8,128)(2,1)S(1)} %get-tuple-element.56), channel_id=1, source_target_pairs={{0,1},{1,0},{2,3},{3,2},{4,5},{5,4},{6,7},{7,6},{8,9},{9,8},{10,11... | collective-permute-start | bytes 442376 | tf_op jit(solution)/shard_map/ppermute | solution.py:371
  34.0 4.3 %collective-permute-start.12 = (bf16[64,1152]{1,0:T(8,128)(2,1)S(1)}, bf16[64,1152]{1,0:T(8,128)(2,1)S(1)}, u32[]{:S(2)}, u32[]{:S(2)}) collective-permute-start(bf16[64,1152]{1,0:T(8,128)(2,1)S(1)} %get-tuple-element.57), channel_id=1, source_target_pairs={{0,1},{1,0},{2,3},{3,2},{4,5},{5,4},{6,7},{7,6},{8,9},{9,8},{10,11... | collective-permute-start | bytes 442376 | tf_op jit(solution)/shard_map/ppermute | solution.py:371
  41.7 5.9 %collective-permute-start.17 = (bf16[64,768]{1,0:T(8,128)(2,1)S(1)}, bf16[64,768]{1,0:T(8,128)(2,1)S(1)}, u32[]{:S(2)}, u32[]{:S(2)}) collective-permute-start(bf16[64,768]{1,0:T(8,128)(2,1)S(1)} %get-tuple-element.63), channel_id=1, source_target_pairs={{0,8},{8,0},{16,24},{24,16},{1,9},{9,1},{17,25},{25,17},{2,10},{10... | collective-permute-start | bytes 294920 | tf_op jit(solution)/shard_map/ppermute | solution.py:395
  43.4 10.7 %collective-permute-start.18 = (bf16[64,768]{1,0:T(8,128)(2,1)S(1)}, bf16[64,768]{1,0:T(8,128)(2,1)S(1)}, u32[]{:S(2)}, u32[]{:S(2)}) collective-permute-start(bf16[64,768]{1,0:T(8,128)(2,1)S(1)} %get-tuple-element.64), channel_id=1, source_target_pairs={{0,16},{8,24},{16,0},{24,8},{1,17},{9,25},{17,1},{25,9},{2,18},{10... | collective-permute-start | bytes 294920 | tf_op jit(solution)/shard_map/ppermute | solution.py:395
  46.0 8.1 %collective-permute-start.19 = (bf16[64,768]{1,0:T(8,128)(2,1)S(1)}, bf16[64,768]{1,0:T(8,128)(2,1)S(1)}, u32[]{:S(2)}, u32[]{:S(2)}) collective-permute-start(bf16[64,768]{1,0:T(8,128)(2,1)S(1)} %get-tuple-element.65), channel_id=1, source_target_pairs={{0,24},{8,16},{16,8},{24,0},{1,25},{9,17},{17,9},{25,1},{2,26},{10... | collective-permute-start | bytes 294920 | tf_op jit(solution)/shard_map/ppermute | solution.py:395
  46.2 12.9 %collective-permute-start.13 = (bf16[256,384]{1,0:T(8,128)(2,1)S(1)}, bf16[256,384]{1,0:T(8,128)(2,1)S(1)}, u32[]{:S(2)}, u32[]{:S(2)}) collective-permute-start(bf16[256,384]{1,0:T(8,128)(2,1)S(1)} %get-tuple-element.53.refs_4_), channel_id=1, source_target_pairs={{0,2},{1,5},{2,0},{3,7},{4,6},{5,1},{6,4},{7,3},{8,10},{9,13},{10,... | collective-permute-start | bytes 589832 | tf_op jit(solution)/shard_map/ppermute | solution.py:383
  47.0 12.1 %collective-permute-start.14 = (bf16[256,384]{1,0:T(8,128)(2,1)S(1)}, bf16[256,384]{1,0:T(8,128)(2,1)S(1)}, u32[]{:S(2)}, u32[]{:S(2)}) collective-permute-start(bf16[256,384]{1,0:T(8,128)(2,1)S(1)} %get-tuple-element.58), channel_id=1, source_target_pairs={{0,4},{1,3},{2,6},{3,1},{4,0},{5,7},{6,2},{7,5},{8,12},{9,11},{10,... | collective-permute-start | bytes 589832 | tf_op jit(solution)/shard_map/ppermute | solution.py:383
  54.7 8.3 %collective-permute-start.25 = (bf16[64,768]{1,0:T(8,128)(2,1)S(1)}, bf16[64,768]{1,0:T(8,128)(2,1)S(1)}, u32[]{:S(2)}, u32[]{:S(2)}) collective-permute-start(bf16[64,768]{1,0:T(8,128)(2,1)S(1)} %shard_map.109.refs_9_.refs_2_), channel_id=1, source_target_pairs={{0,24},{8,16},{16,8},{24,0},{1,25},{9,17},{17,9},{25,1},{2,26},{10... | collective-permute-start | bytes 294920 | tf_op jit(solution)/shard_map/ppermute | solution.py:395
  57.3 11.1 %collective-permute-start.24 = (bf16[64,768]{1,0:T(8,128)(2,1)S(1)}, bf16[64,768]{1,0:T(8,128)(2,1)S(1)}, u32[]{:S(2)}, u32[]{:S(2)}) collective-permute-start(bf16[64,768]{1,0:T(8,128)(2,1)S(1)} %shard_map.109.refs_9_.refs_2_), channel_id=1, source_target_pairs={{0,16},{8,24},{16,0},{24,8},{1,17},{9,25},{17,1},{25,9},{2,18},{10... | collective-permute-start | bytes 294920 | tf_op jit(solution)/shard_map/ppermute | solution.py:395
  57.9 10.5 %collective-permute-start.23 = (bf16[64,768]{1,0:T(8,128)(2,1)S(1)}, bf16[64,768]{1,0:T(8,128)(2,1)S(1)}, u32[]{:S(2)}, u32[]{:S(2)}) collective-permute-start(bf16[64,768]{1,0:T(8,128)(2,1)S(1)} %shard_map.109.refs_9_.refs_2_), channel_id=1, source_target_pairs={{0,8},{8,0},{16,24},{24,16},{1,9},{9,1},{17,25},{25,17},{2,10},{10... | collective-permute-start | bytes 294920 | tf_op jit(solution)/shard_map/ppermute | solution.py:395
  59.8 10.0 %collective-permute-start.20 = (bf16[64,384]{1,0:T(8,128)(2,1)S(1)}, bf16[64,384]{1,0:T(8,128)(2,1)S(1)}, u32[]{:S(2)}, u32[]{:S(2)}) collective-permute-start(bf16[64,384]{1,0:T(8,128)(2,1)S(1)} %get-tuple-element.67), channel_id=1, source_target_pairs={{0,8},{8,0},{16,24},{24,16},{1,9},{9,1},{17,25},{25,17},{2,10},{10... | collective-permute-start | bytes 147464 | tf_op jit(solution)/shard_map/ppermute | solution.py:395
  60.7 9.2 %collective-permute-start.21 = (bf16[64,384]{1,0:T(8,128)(2,1)S(1)}, bf16[64,384]{1,0:T(8,128)(2,1)S(1)}, u32[]{:S(2)}, u32[]{:S(2)}) collective-permute-start(bf16[64,384]{1,0:T(8,128)(2,1)S(1)} %get-tuple-element.68), channel_id=1, source_target_pairs={{0,16},{8,24},{16,0},{24,8},{1,17},{9,25},{17,1},{25,9},{2,18},{10... | collective-permute-start | bytes 147464 | tf_op jit(solution)/shard_map/ppermute | solution.py:395
  63.0 6.9 %collective-permute-start.22 = (bf16[64,384]{1,0:T(8,128)(2,1)S(1)}, bf16[64,384]{1,0:T(8,128)(2,1)S(1)}, u32[]{:S(2)}, u32[]{:S(2)}) collective-permute-start(bf16[64,384]{1,0:T(8,128)(2,1)S(1)} %get-tuple-element.69), channel_id=1, source_target_pairs={{0,24},{8,16},{16,8},{24,0},{1,25},{9,17},{17,9},{25,1},{2,26},{10... | collective-permute-start | bytes 147464 | tf_op jit(solution)/shard_map/ppermute | solution.py:395
  68.9 10.6 %collective-permute-start.33 = (bf16[256,768]{1,0:T(8,128)(2,1)S(1)}, bf16[256,768]{1,0:T(8,128)(2,1)S(1)}, u32[]{:S(2)}, u32[]{:S(2)}) collective-permute-start(bf16[256,768]{1,0:T(8,128)(2,1)S(1)} %shard_map.111.refs_6_.refs_2_), channel_id=1, source_target_pairs={{0,4},{1,3},{2,6},{3,1},{4,0},{5,7},{6,2},{7,5},{8,12},{9,11},{10,... | collective-permute-start | bytes 1179656 | tf_op jit(solution)/shard_map/ppermute | solution.py:383
  69.3 11.8 %collective-permute-start.29 = (bf16[256,768]{1,0:T(8,128)(2,1)S(1)}, bf16[256,768]{1,0:T(8,128)(2,1)S(1)}, u32[]{:S(2)}, u32[]{:S(2)}) collective-permute-start(bf16[256,768]{1,0:T(8,128)(2,1)S(1)} %shard_map.111.refs_6_.refs_2_), channel_id=1, source_target_pairs={{0,2},{1,5},{2,0},{3,7},{4,6},{5,1},{6,4},{7,3},{8,10},{9,13},{10,... | collective-permute-start | bytes 1179656 | tf_op jit(solution)/shard_map/ppermute | solution.py:383
  70.4 10.7 %collective-permute-start.28 = (bf16[64,384]{1,0:T(8,128)(2,1)S(1)}, bf16[64,384]{1,0:T(8,128)(2,1)S(1)}, u32[]{:S(2)}, u32[]{:S(2)}) collective-permute-start(bf16[64,384]{1,0:T(8,128)(2,1)S(1)} %shard_map.112.refs_2_.refs_6_), channel_id=1, source_target_pairs={{0,24},{8,16},{16,8},{24,0},{1,25},{9,17},{17,9},{25,1},{2,26},{10... | collective-permute-start | bytes 147464 | tf_op jit(solution)/shard_map/ppermute | solution.py:395
  71.7 9.3 %collective-permute-start.27 = (bf16[64,384]{1,0:T(8,128)(2,1)S(1)}, bf16[64,384]{1,0:T(8,128)(2,1)S(1)}, u32[]{:S(2)}, u32[]{:S(2)}) collective-permute-start(bf16[64,384]{1,0:T(8,128)(2,1)S(1)} %shard_map.112.refs_2_.refs_6_), channel_id=1, source_target_pairs={{0,16},{8,24},{16,0},{24,8},{1,17},{9,25},{17,1},{25,9},{2,18},{10... | collective-permute-start | bytes 147464 | tf_op jit(solution)/shard_map/ppermute | solution.py:395
  72.6 8.5 %collective-permute-start.26 = (bf16[64,384]{1,0:T(8,128)(2,1)S(1)}, bf16[64,384]{1,0:T(8,128)(2,1)S(1)}, u32[]{:S(2)}, u32[]{:S(2)}) collective-permute-start(bf16[64,384]{1,0:T(8,128)(2,1)S(1)} %shard_map.112.refs_2_.refs_6_), channel_id=1, source_target_pairs={{0,8},{8,0},{16,24},{24,16},{1,9},{9,1},{17,25},{25,17},{2,10},{10... | collective-permute-start | bytes 147464 | tf_op jit(solution)/shard_map/ppermute | solution.py:395
  79.5 9.4 %collective-permute-start.34 = (bf16[256,768]{1,0:T(8,128)(2,1)S(1)}, bf16[256,768]{1,0:T(8,128)(2,1)S(1)}, u32[]{:S(2)}, u32[]{:S(2)}) collective-permute-start(bf16[256,768]{1,0:T(8,128)(2,1)S(1)} %collective-permute-done.33.refs_3_), channel_id=1, source_target_pairs={{0,2},{1,5},{2,0},{3,7},{4,6},{5,1},{6,4},{7,3},{8,10},{9,13},{10,... | collective-permute-start | bytes 1179656 | tf_op jit(solution)/shard_map/ppermute | solution.py:383
  81.7 6.1 %collective-permute-start.30 = (bf16[256,384]{1,0:T(8,128)(2,1)S(1)}, bf16[256,384]{1,0:T(8,128)(2,1)S(1)}, u32[]{:S(2)}, u32[]{:S(2)}) collective-permute-start(bf16[256,384]{1,0:T(8,128)(2,1)S(1)} %shard_map.113.refs_6_.refs_2_), channel_id=1, source_target_pairs={{0,4},{1,3},{2,6},{3,1},{4,0},{5,7},{6,2},{7,5},{8,12},{9,11},{10,... | collective-permute-start | bytes 589832 | tf_op jit(solution)/shard_map/ppermute | solution.py:383
  82.0 13.0 %collective-permute-start.31 = (bf16[256,384]{1,0:T(8,128)(2,1)S(1)}, bf16[256,384]{1,0:T(8,128)(2,1)S(1)}, u32[]{:S(2)}, u32[]{:S(2)}) collective-permute-start(bf16[256,384]{1,0:T(8,128)(2,1)S(1)} %shard_map.113.refs_6_.refs_2_), channel_id=1, source_target_pairs={{0,2},{1,5},{2,0},{3,7},{4,6},{5,1},{6,4},{7,3},{8,10},{9,13},{10,... | collective-permute-start | bytes 589832 | tf_op jit(solution)/shard_map/ppermute | solution.py:383
  87.8 7.3 %collective-permute-start.32 = (bf16[256,384]{1,0:T(8,128)(2,1)S(1)}, bf16[256,384]{1,0:T(8,128)(2,1)S(1)}, u32[]{:S(2)}, u32[]{:S(2)}) collective-permute-start(bf16[256,384]{1,0:T(8,128)(2,1)S(1)} %collective-permute-done.30.refs_3_), channel_id=1, source_target_pairs={{0,2},{1,5},{2,0},{3,7},{4,6},{5,1},{6,4},{7,3},{8,10},{9,13},{10,... | collective-permute-start | bytes 589832 | tf_op jit(solution)/shard_map/ppermute | solution.py:383
  89.6 6.6 %collective-permute-start.36 = (bf16[1024,768]{1,0:T(8,128)(2,1)S(1)}, bf16[1024,768]{1,0:T(8,128)(2,1)S(1)}, u32[]{:S(2)}, u32[]{:S(2)}) collective-permute-start(bf16[1024,768]{1,0:T(8,128)(2,1)S(1)} %shard_map.114.refs_2_.refs_5_), channel_id=1, source_target_pairs={{0,1},{1,0},{2,3},{3,2},{4,5},{5,4},{6,7},{7,6},{8,9},{9,8},{10,11... | collective-permute-start | bytes 4718600 | tf_op jit(solution)/shard_map/ppermute | solution.py:371
  95.7 5.8 %collective-permute-start.35 = (bf16[1024,384]{1,0:T(8,128)(2,1)S(1)}, bf16[1024,384]{1,0:T(8,128)(2,1)S(1)}, u32[]{:S(2)}, u32[]{:S(2)}) collective-permute-start(bf16[1024,384]{1,0:T(8,128)(2,1)S(1)} %shard_map.116.refs_7_.refs_2_), channel_id=1, source_target_pairs={{0,1},{1,0},{2,3},{3,2},{4,5},{5,4},{6,7},{7,6},{8,9},{9,8},{10,11... | collective-permute-start | bytes 2359304 | tf_op jit(solution)/shard_map/ppermute | solution.py:371
  (12 other events, 36.2 us)

commit v7 on v6

--- a/solution.py
+++ b/solution.py
@@ -128,13 +128,6 @@
         )(*self.scalars, *operands, *waits, *keep)
         self.last = results[0]
         return results
-
-    def pass_on(self, value):
-        def kernel(*refs):
-            pass
-
-        like = array(value.shape, value.dtype)
-        return self(kernel, [value], [like], [ANYWHERE], [ANYWHERE], aliases=[(0, 0)])[0]
 
 
 def load(order, *operands):
@@ -411,15 +404,21 @@
     away = decode_near(order, True, act_near, writeout, hidden)
     here_got = [to_core(a) for a in away]
     here = [*decode_near(order, False, act_near, writeout, hidden), *here_got]
-    far = order.pass_on(far)
-
-    def first_kernel(w, d, kept0, kept1, got0, got1, *outs):
+
+    def first_kernel(w, d, kept0, kept1, got0, got1, far_ref, *outs):
         y1 = w[FEAT] == 1
         other = pick(y1, kept0[...], kept1[...]) + pick(y1, got0[...], got1[...]).astype(F32)
         for (lo, hi), out in zip(chunks, outs):
             out[...] = other[:, lo:hi].astype(BF)
 
-    sends = order(first_kernel, here, [held((rows, hi - lo), BF) for lo, hi in chunks])
+    *sends, far = order(
+        first_kernel,
+        [*here, far],
+        [held((rows, hi - lo), BF) for lo, hi in chunks] + [array(far.shape, BF)],
+        [HELD] * len(here) + [ANYWHERE],
+        [HELD] * len(chunks) + [ANYWHERE],
+        aliases=[(len(here), len(chunks))],
+    )
     got_first = [to_first(send) for send in sends]
 
     far_near = to_core(far)
@@ -485,7 +484,7 @@
                 value = value + ref[...].astype(F32)
             out[...] = (value * inverse).astype(BF)
 
-        scaled = order(kernel, (mine, *pieces), [held(mine.shape, BF)], heavy=True)[0]
+        scaled = order(kernel, (mine, *pieces[::-1]), [held(mine.shape, BF)], heavy=True)[0]
         return scaled, [to_layer(scaled, s) for s in range(1, layers)]
 
     def join_pieces(scaled, pieces, wait):
@@ -494,11 +493,11 @@
         def kernel(w, d, *refs):
             *refs, out = refs
             out[span(w[LAYER], piece), :] = refs[0][...]
-            for s, ref in enumerate(refs[1:], 1):
+            for s, ref in enumerate(refs[:0:-1], 1):
                 out[span(layer_source(w[LAYER], s), piece), :] = ref[...]
 
         outs = [held((rows, size), BF)]
-        done = order(kernel, (scaled, *pieces), outs, heavy=True, wait=wait)[0]
+        done = order(kernel, (scaled, *pieces[::-1]), outs, heavy=True, wait=wait)[0]
         got_second, got_first = to_second(done), to_first(done)
         return done, got_second, got_first, to_first(got_second)
 

time: 111 us -> 110 us (level); the launches traced: 111 us -> 108 us
  waiting for transfers between devices: 24.4 us -> 22.3 us
    ppermute x12, waiting for transfers between devices: 12.5 us -> 7.05 us  [mixed(): return lambda a: lax.ppermute(a, ('feat', 'tok'), pairs)]
    ppermute x12, waiting for transfers between devices: 9.98 us -> 13.8 us  [to_layer(): lax.ppermute(a, 'layer', [(l, l ^ s if binary else (l + s) % layers) for...]
    pallas_call x25 -> x24, Pallas kernels: 49.2 us -> 48.6 us  [__call__(): pl.pallas_call(body, grid_spec=pltpu.PrefetchScalarGridSpec(num_scalar_pr...]
  transfers between devices with their start and end apart: 37 -> 37, of which waited for: 7 -> 12; matrix products, arithmetic and copies ran while one was open for 0% -> 0% of each run, Pallas kernels for 35% -> 35%
where the time goes in v7:
time: 110 us; the launch traced here: 108 us
  Pallas kernels  48.6 us (44%)
  starting transfers between devices  35.6 us (32%)
  waiting for transfers between devices  22.3 us (20%)
    pallas_call x24, Pallas kernels, __call__(): pl.pallas_call(body, grid_spec=pltpu.PrefetchScalarGridSpec(num_scalar_pr...  48.6 us
    ppermute x12, starting transfers between devices, to_layer(): lax.ppermute(a, 'layer', [(l, l ^ s if binary else (l + s) % layers) for...  17.8 us
    ppermute x12, waiting for transfers between devices, to_layer(): lax.ppermute(a, 'layer', [(l, l ^ s if binary else (l + s) % layers) for...  13.8 us
    ppermute x12, starting transfers between devices, mixed(): return lambda a: lax.ppermute(a, ('feat', 'tok'), pairs)  11.9 us
    ppermute x12, waiting for transfers between devices, mixed(): return lambda a: lax.ppermute(a, ('feat', 'tok'), pairs)  7.05 us
    ppermute x1, starting transfers between devices, to_side(): return lax.ppermute(a, 'tok', [(t, t ^ 2) for t in range(toks)])  3 us
    ppermute x12, starting transfers between devices, to_core(): return lax.ppermute(a, 'tok', [(t, t ^ 1) for t in range(toks)])  2.95 us
  transfers between devices with their start and end apart: 37, of which 12 were waited for; matrix products, arithmetic and copies ran while one was open for 0% of the time, Pallas kernels for 35%

profile of v7, /device:TPU:0, one launch (start us, length us, event | category | flops | bytes accessed | tf_op | source)
XLA Modules:
  0.0 108.3 jit_solution(17745130283064798749)
XLA Ops:
  0.6 3.0 %collective-permute-start.3 = (bf16[256,1152]{1,0:T(8,128)(2,1)}, bf16[256,1152]{1,0:T(8,128)(2,1)S(1)}, u32[]{:S(2)}, u32[]{:S(2)}) collective-permute-start(bf16[256,1152]{1,0:T(8,128)(2,1)} %bitcast.5), channel_id=1, source_target_pairs={{0,2},{1,3},{2,0},{3,1},{4,6},{5,7},{6,4},{7,5},{8,10},{9,11},{10,... | collective-permute-start | bytes 1769480 | tf_op jit(solution)/shard_map/ppermute | solution.py:367
  4.4 5.3 %shard_map.94 = (bf16[1,1152,1024]{2,1,0:T(8,128)(2,1)S(1)}, s32[1,1024,1024]{2,1,0:T(8,128)S(1)}, bf16[1,2,1024,1152]{3,2,1,0:T(8,128)(2,1)S(1)}, bf16[2,256,1152]{2,1,0:T(8,128)(2,1)S(1)}) custom-call(s32[4]{0:T(128)S(1)} %pad_add_fusion.refs_0_, s32[2]{0:T(128)S(1)} %copy-done.4, bf16[1,1152,1024]{2,1,0:T(8,128)(2,1)} %refs_2_.1, ...), custom_call_target="tpu_custom_call" | custom-call | flops 99999997952 | bytes 1000 | tf_op jit(solution)/shard_map/pallas_call | solution.py:113
  9.7 2.2 %shard_map.95.refs_2_.refs_5_ = bf16[512,1024]{1,0:T(8,128)(2,1)S(1)} custom-call(s32[4]{0:T(128)S(1)} %pad_add_fusion.refs_0_, s32[2]{0:T(128)S(1)} %copy-done.5, bf16[256,1152]{1,0:T(8,128)(2,1)S(1)} %bitcast.7, bf16[256,1152]{1,0:T(8,128)(2,1)S(1)} %collective-permute-done.refs_3_.refs_5_, bf16[1,1152,1024]{2,1,0:T(8,128)(2,1)S(1)} %get-tuple-element.41.refs_4_.refs_7_, ...), custom_call_target="tpu_custom_call" | custom-call | flops 1000 | bytes 1000 | tf_op jit(solution)/shard_map/pallas_call | solution.py:113
  11.9 2.1 %shard_map.96 = (bf16[256,1152]{1,0:T(8,128)(2,1)S(1)}, bf16[256,1152]{1,0:T(8,128)(2,1)S(1)}) custom-call(s32[4]{0:T(128)S(1)} %pad_add_fusion.refs_0_, s32[2]{0:T(128)S(1)} %copy-done.5, bf16[512,1024]{1,0:T(8,128)(2,1)S(1)} %shard_map.95.refs_2_.refs_5_, bf16[1,2,1024,1152]{3,2,1,0:T(8,128)(2,1)S(1)} %get-tuple-element.43.refs_3_.refs_10_.refs_7_.refs_8_.refs_4_.refs_5_, ...), custom_call_target="tpu_custom_call" | custom-call | flops 1000 | bytes 1000 | tf_op jit(solution)/shard_map/pallas_call | solution.py:113
  14.7 2.1 %shard_map.97 = (f32[256,1152]{1,0:T(8,128)S(1)}, f32[256,1152]{1,0:T(8,128)S(1)}) custom-call(s32[4]{0:T(128)S(1)} %pad_add_fusion.refs_0_, s32[2]{0:T(128)S(1)} %copy-done.5, bf16[512,1024]{1,0:T(8,128)(2,1)S(1)} %shard_map.95.refs_2_.refs_5_, bf16[1,2,1024,1152]{3,2,1,0:T(8,128)(2,1)S(1)} %get-tuple-element.43.refs_3_.refs_10_.refs_7_.refs_8_.refs_4_.refs_5_, ...), custom_call_target="tpu_custom_call" | custom-call | flops 1000 | bytes 1000 | tf_op jit(solution)/shard_map/pallas_call | solution.py:113
  18.2 1.6 %collective-permute-start.8 = (bf16[256,768]{1,0:T(8,128)(2,1)S(1)}, bf16[256,768]{1,0:T(8,128)(2,1)S(1)}, u32[]{:S(2)}, u32[]{:S(2)}) collective-permute-start(bf16[256,768]{1,0:T(8,128)(2,1)S(1)} %get-tuple-element.50.refs_7_), channel_id=1, source_target_pairs={{0,2},{1,5},{2,0},{3,7},{4,6},{5,1},{6,4},{7,3},{8,10},{9,13},{10,... | collective-permute-start | bytes 1179656 | tf_op jit(solution)/shard_map/ppermute | solution.py:376
  20.0 2.2 %shard_map.99.refs_2_.refs_4_.refs_3_ = bf16[512,1024]{1,0:T(8,128)(2,1)S(1)} custom-call(s32[4]{0:T(128)S(1)} %pad_add_fusion.refs_0_, s32[2]{0:T(128)S(1)} %copy-done.5, bf16[256,1152]{1,0:T(8,128)(2,1)S(1)} %get-tuple-element.49.refs_2_.refs_6_, bf16[256,1152]{1,0:T(8,128)(2,1)S(1)} %collective-permute-done.4.refs_3_.refs_7_, ...), custom_call_target="tpu_custom_call" | custom-call | flops 99999997952 | bytes 1000 | tf_op jit(solution)/shard_map/pallas_call | solution.py:113
  22.2 1.4 %shard_map.100 = (bf16[128,1152]{1,0:T(8,128)(2,1)S(1)}, bf16[128,1152]{1,0:T(8,128)(2,1)S(1)}) custom-call(s32[4]{0:T(128)S(1)} %pad_add_fusion.refs_0_, s32[2]{0:T(128)S(1)} %copy-done.5, bf16[512,1024]{1,0:T(8,128)(2,1)S(1)} %shard_map.99.refs_2_.refs_4_.refs_3_, ...), custom_call_target="tpu_custom_call" | custom-call | flops 1000 | bytes 1000 | tf_op jit(solution)/shard_map/pallas_call | solution.py:113
  24.1 1.7 %collective-permute-start.5 = (bf16[256,384]{1,0:T(8,128)(2,1)S(1)}, bf16[256,384]{1,0:T(8,128)(2,1)S(1)}, u32[]{:S(2)}, u32[]{:S(2)}) collective-permute-start(bf16[256,384]{1,0:T(8,128)(2,1)S(1)} %get-tuple-element.51), channel_id=1, source_target_pairs={{0,2},{1,5},{2,0},{3,7},{4,6},{5,1},{6,4},{7,3},{8,10},{9,13},{10,... | collective-permute-start | bytes 589832 | tf_op jit(solution)/shard_map/ppermute | solution.py:376
  25.9 1.4 %shard_map.101.refs_7_.refs_10_ = f32[256,1152]{1,0:T(8,128)S(1)} custom-call(s32[4]{0:T(128)S(1)} %pad_add_fusion.refs_0_, s32[2]{0:T(128)S(1)} %copy-done.5, bf16[512,1024]{1,0:T(8,128)(2,1)S(1)} %shard_map.99.refs_2_.refs_4_.refs_3_, bf16[1,2,1024,1152]{3,2,1,0:T(8,128)(2,1)S(1)} %get-tuple-element.43.refs_3_.refs_10_.refs_7_.refs_8_.refs_4_.refs_5_, ...), custom_call_target="tpu_custom_call" | custom-call | flops 1000 | bytes 1000 | tf_op jit(solution)/shard_map/pallas_call | solution.py:113
  28.2 1.6 %collective-permute-start.16 = (bf16[256,768]{1,0:T(8,128)(2,1)S(1)}, bf16[256,768]{1,0:T(8,128)(2,1)S(1)}, u32[]{:S(2)}, u32[]{:S(2)}) collective-permute-start(bf16[256,768]{1,0:T(8,128)(2,1)S(1)} %get-tuple-element.61), channel_id=1, source_target_pairs={{0,4},{1,3},{2,6},{3,1},{4,0},{5,7},{6,2},{7,5},{8,12},{9,11},{10,... | collective-permute-start | bytes 1179656 | tf_op jit(solution)/shard_map/ppermute | solution.py:376
  31.0 1.4 %shard_map.104 = (bf16[64,1152]{1,0:T(8,128)(2,1)S(1)}, bf16[64,1152]{1,0:T(8,128)(2,1)S(1)}, bf16[64,1152]{1,0:T(8,128)(2,1)S(1)}, bf16[64,1152]{1,0:T(8,128)(2,1)S(1)}) custom-call(s32[4]{0:T(128)S(1)} %pad_add_fusion.refs_0_, s32[2]{0:T(128)S(1)} %copy-done.5, bf16[512,1024]{1,0:T(8,128)(2,1)S(1)} %shard_map.99.refs_2_.refs_4_.refs_3_, ...), custom_call_target="tpu_custom_call" | custom-call | flops 1000 | bytes 1000 | tf_op jit(solution)/shard_map/pallas_call | solution.py:113
  34.0 1.4 %shard_map.105.refs_8_.refs_2_ = f32[256,1152]{1,0:T(8,128)S(1)} custom-call(s32[4]{0:T(128)S(1)} %pad_add_fusion.refs_0_, s32[2]{0:T(128)S(1)} %copy-done.5, bf16[512,1024]{1,0:T(8,128)(2,1)S(1)} %shard_map.99.refs_2_.refs_4_.refs_3_, bf16[1,2,1024,1152]{3,2,1,0:T(8,128)(2,1)S(1)} %get-tuple-element.43.refs_3_.refs_10_.refs_7_.refs_8_.refs_4_.refs_5_, ...), custom_call_target="tpu_custom_call" | custom-call | flops 1000 | bytes 1000 | tf_op jit(solution)/shard_map/pallas_call | solution.py:113
  35.4 1.8 %shard_map.106 = (bf16[1024,1024]{1,0:T(8,128)(2,1)S(1)}, bf16[1152,1024]{1,0:T(8,128)(2,1)S(1)}) custom-call(s32[4]{0:T(128)S(1)} %pad_add_fusion.refs_0_, s32[2]{0:T(128)S(1)} %copy-done.5, bf16[512,1024]{1,0:T(8,128)(2,1)S(1)} %copy-done.1, bf16[512,1024]{1,0:T(8,128)(2,1)S(1)} %shard_map.99.refs_2_.refs_4_.refs_3_, bf16[256,1152]{1,0:T(8,128)(2,1)S(1)} %bitcast.8, ...), custom_call_target="tpu_custom_call" | custom-call | flops 1000 | bytes 1000 | tf_op jit(solution)/shard_map/pallas_call | solution.py:113
  37.3 2.8 %collective-permute-done.16.refs_8_ = bf16[256,768]{1,0:T(8,128)(2,1)S(1)} collective-permute-done((bf16[256,768]{1,0:T(8,128)(2,1)S(1)}, bf16[256,768]{1,0:T(8,128)(2,1)S(1)}, u32[]{:S(2)}, u32[]{:S(2)}) %collective-permute-start.16) | collective-permute-done | bytes 393248 | tf_op jit(solution)/shard_map/ppermute | solution.py:376
  41.0 3.7 %collective-permute-start.17 = (bf16[64,768]{1,0:T(8,128)(2,1)S(1)}, bf16[64,768]{1,0:T(8,128)(2,1)S(1)}, u32[]{:S(2)}, u32[]{:S(2)}) collective-permute-start(bf16[64,768]{1,0:T(8,128)(2,1)S(1)} %get-tuple-element.65), channel_id=1, source_target_pairs={{0,24},{8,16},{16,8},{24,0},{1,25},{9,17},{17,9},{25,1},{2,26},{10... | collective-permute-start | bytes 294920 | tf_op jit(solution)/shard_map/ppermute | solution.py:388
  46.8 1.8 %collective-permute-done.17.refs_3_ = bf16[64,768]{1,0:T(8,128)(2,1)S(1)} collective-permute-done((bf16[64,768]{1,0:T(8,128)(2,1)S(1)}, bf16[64,768]{1,0:T(8,128)(2,1)S(1)}, u32[]{:S(2)}, u32[]{:S(2)}) %collective-permute-start.17) | collective-permute-done | bytes 98336 | tf_op jit(solution)/shard_map/ppermute | solution.py:388
  48.6 4.6 %collective-permute-done.18.refs_4_ = bf16[64,768]{1,0:T(8,128)(2,1)S(1)} collective-permute-done((bf16[64,768]{1,0:T(8,128)(2,1)S(1)}, bf16[64,768]{1,0:T(8,128)(2,1)S(1)}, u32[]{:S(2)}, u32[]{:S(2)}) %collective-permute-start.18) | collective-permute-done | bytes 98336 | tf_op jit(solution)/shard_map/ppermute | solution.py:388
  54.4 2.5 %collective-permute-start.24 = (bf16[64,768]{1,0:T(8,128)(2,1)S(1)}, bf16[64,768]{1,0:T(8,128)(2,1)S(1)}, u32[]{:S(2)}, u32[]{:S(2)}) collective-permute-start(bf16[64,768]{1,0:T(8,128)(2,1)S(1)} %shard_map.108.refs_9_.refs_2_), channel_id=1, source_target_pairs={{0,16},{8,24},{16,0},{24,8},{1,17},{9,25},{17,1},{25,9},{2,18},{10... | collective-permute-start | bytes 294920 | tf_op jit(solution)/shard_map/ppermute | solution.py:388
  56.9 1.3 %collective-permute-start.23 = (bf16[64,768]{1,0:T(8,128)(2,1)S(1)}, bf16[64,768]{1,0:T(8,128)(2,1)S(1)}, u32[]{:S(2)}, u32[]{:S(2)}) collective-permute-start(bf16[64,768]{1,0:T(8,128)(2,1)S(1)} %shard_map.108.refs_9_.refs_2_), channel_id=1, source_target_pairs={{0,24},{8,16},{16,8},{24,0},{1,25},{9,17},{17,9},{25,1},{2,26},{10... | collective-permute-start | bytes 294920 | tf_op jit(solution)/shard_map/ppermute | solution.py:388
  59.0 2.5 %collective-permute-start.20 = (bf16[64,384]{1,0:T(8,128)(2,1)S(1)}, bf16[64,384]{1,0:T(8,128)(2,1)S(1)}, u32[]{:S(2)}, u32[]{:S(2)}) collective-permute-start(bf16[64,384]{1,0:T(8,128)(2,1)S(1)} %get-tuple-element.69), channel_id=1, source_target_pairs={{0,24},{8,16},{16,8},{24,0},{1,25},{9,17},{17,9},{25,1},{2,26},{10... | collective-permute-start | bytes 147464 | tf_op jit(solution)/shard_map/ppermute | solution.py:388
  61.5 1.9 %collective-permute-start.22 = (bf16[64,384]{1,0:T(8,128)(2,1)S(1)}, bf16[64,384]{1,0:T(8,128)(2,1)S(1)}, u32[]{:S(2)}, u32[]{:S(2)}) collective-permute-start(bf16[64,384]{1,0:T(8,128)(2,1)S(1)} %get-tuple-element.71), channel_id=1, source_target_pairs={{0,8},{8,0},{16,24},{24,16},{1,9},{9,1},{17,25},{25,17},{2,10},{10... | collective-permute-start | bytes 147464 | tf_op jit(solution)/shard_map/ppermute | solution.py:388
  63.4 3.3 %collective-permute-done.24.refs_4_ = bf16[64,768]{1,0:T(8,128)(2,1)S(1)} collective-permute-done((bf16[64,768]{1,0:T(8,128)(2,1)S(1)}, bf16[64,768]{1,0:T(8,128)(2,1)S(1)}, u32[]{:S(2)}, u32[]{:S(2)}) %collective-permute-start.24) | collective-permute-done | bytes 98336 | tf_op jit(solution)/shard_map/ppermute | solution.py:388
  68.1 1.5 %collective-permute-done.21.refs_4_ = bf16[64,384]{1,0:T(8,128)(2,1)S(1)} collective-permute-done((bf16[64,384]{1,0:T(8,128)(2,1)S(1)}, bf16[64,384]{1,0:T(8,128)(2,1)S(1)}, u32[]{:S(2)}, u32[]{:S(2)}) %collective-permute-start.21) | collective-permute-done | bytes 49184 | tf_op jit(solution)/shard_map/ppermute | solution.py:388
  71.0 2.1 %collective-permute-start.27 = (bf16[64,384]{1,0:T(8,128)(2,1)S(1)}, bf16[64,384]{1,0:T(8,128)(2,1)S(1)}, u32[]{:S(2)}, u32[]{:S(2)}) collective-permute-start(bf16[64,384]{1,0:T(8,128)(2,1)S(1)} %shard_map.111.refs_2_.refs_6_), channel_id=1, source_target_pairs={{0,16},{8,24},{16,0},{24,8},{1,17},{9,25},{17,1},{25,9},{2,18},{10... | collective-permute-start | bytes 147464 | tf_op jit(solution)/shard_map/ppermute | solution.py:388
  73.1 1.5 %collective-permute-start.26 = (bf16[64,384]{1,0:T(8,128)(2,1)S(1)}, bf16[64,384]{1,0:T(8,128)(2,1)S(1)}, u32[]{:S(2)}, u32[]{:S(2)}) collective-permute-start(bf16[64,384]{1,0:T(8,128)(2,1)S(1)} %shard_map.111.refs_2_.refs_6_), channel_id=1, source_target_pairs={{0,24},{8,16},{16,8},{24,0},{1,25},{9,17},{17,9},{25,1},{2,26},{10... | collective-permute-start | bytes 147464 | tf_op jit(solution)/shard_map/ppermute | solution.py:388
  76.9 2.1 %collective-permute-done.26.refs_3_ = bf16[64,384]{1,0:T(8,128)(2,1)S(1)} collective-permute-done((bf16[64,384]{1,0:T(8,128)(2,1)S(1)}, bf16[64,384]{1,0:T(8,128)(2,1)S(1)}, u32[]{:S(2)}, u32[]{:S(2)}) %collective-permute-start.26) | collective-permute-done | bytes 49184 | tf_op jit(solution)/shard_map/ppermute | solution.py:388
  80.5 1.5 %collective-permute-start.31 = (bf16[256,384]{1,0:T(8,128)(2,1)S(1)}, bf16[256,384]{1,0:T(8,128)(2,1)S(1)}, u32[]{:S(2)}, u32[]{:S(2)}) collective-permute-start(bf16[256,384]{1,0:T(8,128)(2,1)S(1)} %shard_map.112.refs_6_.refs_2_), channel_id=1, source_target_pairs={{0,2},{1,5},{2,0},{3,7},{4,6},{5,1},{6,4},{7,3},{8,10},{9,13},{10,... | collective-permute-start | bytes 589832 | tf_op jit(solution)/shard_map/ppermute | solution.py:376
  82.0 3.3 %collective-permute-done.30.refs_3_ = bf16[256,384]{1,0:T(8,128)(2,1)S(1)} collective-permute-done((bf16[256,384]{1,0:T(8,128)(2,1)S(1)}, bf16[256,384]{1,0:T(8,128)(2,1)S(1)}, u32[]{:S(2)}, u32[]{:S(2)}) %collective-permute-start.30) | collective-permute-done | bytes 196640 | tf_op jit(solution)/shard_map/ppermute | solution.py:376
  87.1 5.3 %shard_map.114 = (bf16[1,2,1024,1152]{3,2,1,0:T(8,128)(2,1)}, f32[1024,1024]{1,0:T(8,128)S(1)}) custom-call(s32[4]{0:T(128)S(1)} %pad_add_fusion.refs_0_, s32[2]{0:T(128)S(1)} %copy-done.5, bf16[1024,768]{1,0:T(8,128)(2,1)S(1)} %shard_map.113.refs_2_.refs_5_, bf16[1024,1024]{1,0:T(8,128)(2,1)S(1)} %get-tuple-element.62.refs_9_.refs_12_.refs_10_.refs_3_.refs_4_, ...), custom_call_target="tpu_custom_call" | custom-call | flops 1000 | bytes 1000 | tf_op jit(solution)/shard_map/pallas_call | solution.py:113
  93.6 5.2 %shard_map.116 = (bf16[1,2,1024,1152]{3,2,1,0:T(8,128)(2,1)}, f32[1024,1024]{1,0:T(8,128)S(1)}) custom-call(s32[4]{0:T(128)S(1)} %pad_add_fusion.refs_0_, s32[2]{0:T(128)S(1)} %copy-done.5, bf16[1024,768]{1,0:T(8,128)(2,1)S(1)} %collective-permute-done.36.refs_2_, ...), custom_call_target="tpu_custom_call", output_to_operand_aliasing={{0}: (6, {})} | custom-call | flops 1000 | bytes 1000 | tf_op jit(solution)/shard_map/pallas_call | solution.py:113
  98.9 9.4 %shard_map.117 = (bf16[1,2,1024,1152]{3,2,1,0:T(8,128)(2,1)}, bf16[1,1152,1024]{2,1,0:T(8,128)(2,1)}, f32[1,1024]{1,0:T(1,128)}) custom-call(s32[4]{0:T(128)S(1)} %pad_add_fusion.refs_0_, s32[2]{0:T(128)S(1)} %copy-done.5, bf16[1024,384]{1,0:T(8,128)(2,1)S(1)} %shard_map.115.refs_7_.refs_2_, ...), custom_call_target="tpu_custom_call", output_to_operand_aliasing={{0}: (9, {})} | custom-call | flops 1000 | bytes 1000 | tf_op jit(solution)/shard_map/pallas_call | solution.py:113
  (81 shorter events, 21.9 us)
Async XLA Ops:
  0.6 16.5 %collective-permute-start.3 = (bf16[256,1152]{1,0:T(8,128)(2,1)}, bf16[256,1152]{1,0:T(8,128)(2,1)S(1)}, u32[]{:S(2)}, u32[]{:S(2)}) collective-permute-start(bf16[256,1152]{1,0:T(8,128)(2,1)} %bitcast.5), channel_id=1, source_target_pairs={{0,2},{1,3},{2,0},{3,1},{4,6},{5,7},{6,4},{7,5},{8,10},{9,11},{10,... | collective-permute-start | bytes 1769480 | tf_op jit(solution)/shard_map/ppermute | solution.py:367
  3.6 6.1 %collective-permute-start = (bf16[256,1152]{1,0:T(8,128)(2,1)}, bf16[256,1152]{1,0:T(8,128)(2,1)S(1)}, u32[]{:S(2)}, u32[]{:S(2)}) collective-permute-start(bf16[256,1152]{1,0:T(8,128)(2,1)} %bitcast.6), channel_id=1, source_target_pairs={{0,1},{1,0},{2,3},{3,2},{4,5},{5,4},{6,7},{7,6},{8,9},{9,8},{10,11... | collective-permute-start | bytes 1769480 | tf_op jit(solution)/shard_map/ppermute | solution.py:364
  18.2 9.1 %collective-permute-start.8 = (bf16[256,768]{1,0:T(8,128)(2,1)S(1)}, bf16[256,768]{1,0:T(8,128)(2,1)S(1)}, u32[]{:S(2)}, u32[]{:S(2)}) collective-permute-start(bf16[256,768]{1,0:T(8,128)(2,1)S(1)} %get-tuple-element.50.refs_7_), channel_id=1, source_target_pairs={{0,2},{1,5},{2,0},{3,7},{4,6},{5,1},{6,4},{7,3},{8,10},{9,13},{10,... | collective-permute-start | bytes 1179656 | tf_op jit(solution)/shard_map/ppermute | solution.py:376
  23.6 3.7 %collective-permute-start.7 = (bf16[128,1152]{1,0:T(8,128)(2,1)S(1)}, bf16[128,1152]{1,0:T(8,128)(2,1)S(1)}, u32[]{:S(2)}, u32[]{:S(2)}) collective-permute-start(bf16[128,1152]{1,0:T(8,128)(2,1)S(1)} %get-tuple-element.53), channel_id=1, source_target_pairs={{0,1},{1,0},{2,3},{3,2},{4,5},{5,4},{6,7},{7,6},{8,9},{9,8},{10,11... | collective-permute-start | bytes 884744 | tf_op jit(solution)/shard_map/ppermute | solution.py:364
  24.1 6.2 %collective-permute-start.5 = (bf16[256,384]{1,0:T(8,128)(2,1)S(1)}, bf16[256,384]{1,0:T(8,128)(2,1)S(1)}, u32[]{:S(2)}, u32[]{:S(2)}) collective-permute-start(bf16[256,384]{1,0:T(8,128)(2,1)S(1)} %get-tuple-element.51), channel_id=1, source_target_pairs={{0,2},{1,5},{2,0},{3,7},{4,6},{5,1},{6,4},{7,3},{8,10},{9,13},{10,... | collective-permute-start | bytes 589832 | tf_op jit(solution)/shard_map/ppermute | solution.py:376
  28.2 11.9 %collective-permute-start.16 = (bf16[256,768]{1,0:T(8,128)(2,1)S(1)}, bf16[256,768]{1,0:T(8,128)(2,1)S(1)}, u32[]{:S(2)}, u32[]{:S(2)}) collective-permute-start(bf16[256,768]{1,0:T(8,128)(2,1)S(1)} %get-tuple-element.61), channel_id=1, source_target_pairs={{0,4},{1,3},{2,6},{3,1},{4,0},{5,7},{6,2},{7,5},{8,12},{9,11},{10,... | collective-permute-start | bytes 1179656 | tf_op jit(solution)/shard_map/ppermute | solution.py:376
  29.8 10.3 %collective-permute-start.15 = (bf16[256,768]{1,0:T(8,128)(2,1)S(1)}, bf16[256,768]{1,0:T(8,128)(2,1)S(1)}, u32[]{:S(2)}, u32[]{:S(2)}) collective-permute-start(bf16[256,768]{1,0:T(8,128)(2,1)S(1)} %get-tuple-element.54.refs_10_), channel_id=1, source_target_pairs={{0,2},{1,5},{2,0},{3,7},{4,6},{5,1},{6,4},{7,3},{8,10},{9,13},{10,... | collective-permute-start | bytes 1179656 | tf_op jit(solution)/shard_map/ppermute | solution.py:376
  32.5 4.8 %collective-permute-start.11 = (bf16[64,1152]{1,0:T(8,128)(2,1)S(1)}, bf16[64,1152]{1,0:T(8,128)(2,1)S(1)}, u32[]{:S(2)}, u32[]{:S(2)}) collective-permute-start(bf16[64,1152]{1,0:T(8,128)(2,1)S(1)} %get-tuple-element.58), channel_id=1, source_target_pairs={{0,1},{1,0},{2,3},{3,2},{4,5},{5,4},{6,7},{7,6},{8,9},{9,8},{10,11... | collective-permute-start | bytes 442376 | tf_op jit(solution)/shard_map/ppermute | solution.py:364
  33.0 4.3 %collective-permute-start.12 = (bf16[64,1152]{1,0:T(8,128)(2,1)S(1)}, bf16[64,1152]{1,0:T(8,128)(2,1)S(1)}, u32[]{:S(2)}, u32[]{:S(2)}) collective-permute-start(bf16[64,1152]{1,0:T(8,128)(2,1)S(1)} %get-tuple-element.59), channel_id=1, source_target_pairs={{0,1},{1,0},{2,3},{3,2},{4,5},{5,4},{6,7},{7,6},{8,9},{9,8},{10,11... | collective-permute-start | bytes 442376 | tf_op jit(solution)/shard_map/ppermute | solution.py:364
  33.9 3.4 %collective-permute-start.9 = (bf16[64,1152]{1,0:T(8,128)(2,1)S(1)}, bf16[64,1152]{1,0:T(8,128)(2,1)S(1)}, u32[]{:S(2)}, u32[]{:S(2)}) collective-permute-start(bf16[64,1152]{1,0:T(8,128)(2,1)S(1)} %get-tuple-element.56.refs_4_), channel_id=1, source_target_pairs={{0,1},{1,0},{2,3},{3,2},{4,5},{5,4},{6,7},{7,6},{8,9},{9,8},{10,11... | collective-permute-start | bytes 442376 | tf_op jit(solution)/shard_map/ppermute | solution.py:364
  41.0 7.6 %collective-permute-start.17 = (bf16[64,768]{1,0:T(8,128)(2,1)S(1)}, bf16[64,768]{1,0:T(8,128)(2,1)S(1)}, u32[]{:S(2)}, u32[]{:S(2)}) collective-permute-start(bf16[64,768]{1,0:T(8,128)(2,1)S(1)} %get-tuple-element.65), channel_id=1, source_target_pairs={{0,24},{8,16},{16,8},{24,0},{1,25},{9,17},{17,9},{25,1},{2,26},{10... | collective-permute-start | bytes 294920 | tf_op jit(solution)/shard_map/ppermute | solution.py:388
  44.7 8.6 %collective-permute-start.18 = (bf16[64,768]{1,0:T(8,128)(2,1)S(1)}, bf16[64,768]{1,0:T(8,128)(2,1)S(1)}, u32[]{:S(2)}, u32[]{:S(2)}) collective-permute-start(bf16[64,768]{1,0:T(8,128)(2,1)S(1)} %get-tuple-element.66), channel_id=1, source_target_pairs={{0,16},{8,24},{16,0},{24,8},{1,17},{9,25},{17,1},{25,9},{2,18},{10... | collective-permute-start | bytes 294920 | tf_op jit(solution)/shard_map/ppermute | solution.py:388
  44.7 8.6 %collective-permute-start.19 = (bf16[64,768]{1,0:T(8,128)(2,1)S(1)}, bf16[64,768]{1,0:T(8,128)(2,1)S(1)}, u32[]{:S(2)}, u32[]{:S(2)}) collective-permute-start(bf16[64,768]{1,0:T(8,128)(2,1)S(1)} %get-tuple-element.67), channel_id=1, source_target_pairs={{0,8},{8,0},{16,24},{24,16},{1,9},{9,1},{17,25},{25,17},{2,10},{10... | collective-permute-start | bytes 294920 | tf_op jit(solution)/shard_map/ppermute | solution.py:388
  45.4 12.8 %collective-permute-start.13 = (bf16[256,384]{1,0:T(8,128)(2,1)S(1)}, bf16[256,384]{1,0:T(8,128)(2,1)S(1)}, u32[]{:S(2)}, u32[]{:S(2)}) collective-permute-start(bf16[256,384]{1,0:T(8,128)(2,1)S(1)} %get-tuple-element.55.refs_4_), channel_id=1, source_target_pairs={{0,2},{1,5},{2,0},{3,7},{4,6},{5,1},{6,4},{7,3},{8,10},{9,13},{10,... | collective-permute-start | bytes 589832 | tf_op jit(solution)/shard_map/ppermute | solution.py:376
  46.0 12.3 %collective-permute-start.14 = (bf16[256,384]{1,0:T(8,128)(2,1)S(1)}, bf16[256,384]{1,0:T(8,128)(2,1)S(1)}, u32[]{:S(2)}, u32[]{:S(2)}) collective-permute-start(bf16[256,384]{1,0:T(8,128)(2,1)S(1)} %get-tuple-element.60), channel_id=1, source_target_pairs={{0,4},{1,3},{2,6},{3,1},{4,0},{5,7},{6,2},{7,5},{8,12},{9,11},{10,... | collective-permute-start | bytes 589832 | tf_op jit(solution)/shard_map/ppermute | solution.py:376
  53.8 7.7 %collective-permute-start.25 = (bf16[64,768]{1,0:T(8,128)(2,1)S(1)}, bf16[64,768]{1,0:T(8,128)(2,1)S(1)}, u32[]{:S(2)}, u32[]{:S(2)}) collective-permute-start(bf16[64,768]{1,0:T(8,128)(2,1)S(1)} %shard_map.108.refs_9_.refs_2_), channel_id=1, source_target_pairs={{0,8},{8,0},{16,24},{24,16},{1,9},{9,1},{17,25},{25,17},{2,10},{10... | collective-permute-start | bytes 294920 | tf_op jit(solution)/shard_map/ppermute | solution.py:388
  54.4 12.3 %collective-permute-start.24 = (bf16[64,768]{1,0:T(8,128)(2,1)S(1)}, bf16[64,768]{1,0:T(8,128)(2,1)S(1)}, u32[]{:S(2)}, u32[]{:S(2)}) collective-permute-start(bf16[64,768]{1,0:T(8,128)(2,1)S(1)} %shard_map.108.refs_9_.refs_2_), channel_id=1, source_target_pairs={{0,16},{8,24},{16,0},{24,8},{1,17},{9,25},{17,1},{25,9},{2,18},{10... | collective-permute-start | bytes 294920 | tf_op jit(solution)/shard_map/ppermute | solution.py:388
  56.9 9.8 %collective-permute-start.23 = (bf16[64,768]{1,0:T(8,128)(2,1)S(1)}, bf16[64,768]{1,0:T(8,128)(2,1)S(1)}, u32[]{:S(2)}, u32[]{:S(2)}) collective-permute-start(bf16[64,768]{1,0:T(8,128)(2,1)S(1)} %shard_map.108.refs_9_.refs_2_), channel_id=1, source_target_pairs={{0,24},{8,16},{16,8},{24,0},{1,25},{9,17},{17,9},{25,1},{2,26},{10... | collective-permute-start | bytes 294920 | tf_op jit(solution)/shard_map/ppermute | solution.py:388
  59.0 9.1 %collective-permute-start.20 = (bf16[64,384]{1,0:T(8,128)(2,1)S(1)}, bf16[64,384]{1,0:T(8,128)(2,1)S(1)}, u32[]{:S(2)}, u32[]{:S(2)}) collective-permute-start(bf16[64,384]{1,0:T(8,128)(2,1)S(1)} %get-tuple-element.69), channel_id=1, source_target_pairs={{0,24},{8,16},{16,8},{24,0},{1,25},{9,17},{17,9},{25,1},{2,26},{10... | collective-permute-start | bytes 147464 | tf_op jit(solution)/shard_map/ppermute | solution.py:388
  61.5 8.0 %collective-permute-start.21 = (bf16[64,384]{1,0:T(8,128)(2,1)S(1)}, bf16[64,384]{1,0:T(8,128)(2,1)S(1)}, u32[]{:S(2)}, u32[]{:S(2)}) collective-permute-start(bf16[64,384]{1,0:T(8,128)(2,1)S(1)} %get-tuple-element.70), channel_id=1, source_target_pairs={{0,16},{8,24},{16,0},{24,8},{1,17},{9,25},{17,1},{25,9},{2,18},{10... | collective-permute-start | bytes 147464 | tf_op jit(solution)/shard_map/ppermute | solution.py:388
  61.5 8.0 %collective-permute-start.22 = (bf16[64,384]{1,0:T(8,128)(2,1)S(1)}, bf16[64,384]{1,0:T(8,128)(2,1)S(1)}, u32[]{:S(2)}, u32[]{:S(2)}) collective-permute-start(bf16[64,384]{1,0:T(8,128)(2,1)S(1)} %get-tuple-element.71), channel_id=1, source_target_pairs={{0,8},{8,0},{16,24},{24,16},{1,9},{9,1},{17,25},{25,17},{2,10},{10... | collective-permute-start | bytes 147464 | tf_op jit(solution)/shard_map/ppermute | solution.py:388
  67.3 8.2 %collective-permute-start.33 = (bf16[256,768]{1,0:T(8,128)(2,1)S(1)}, bf16[256,768]{1,0:T(8,128)(2,1)S(1)}, u32[]{:S(2)}, u32[]{:S(2)}) collective-permute-start(bf16[256,768]{1,0:T(8,128)(2,1)S(1)} %shard_map.110.refs_6_.refs_2_), channel_id=1, source_target_pairs={{0,4},{1,3},{2,6},{3,1},{4,0},{5,7},{6,2},{7,5},{8,12},{9,11},{10,... | collective-permute-start | bytes 1179656 | tf_op jit(solution)/shard_map/ppermute | solution.py:376
  67.4 11.6 %collective-permute-start.29 = (bf16[256,768]{1,0:T(8,128)(2,1)S(1)}, bf16[256,768]{1,0:T(8,128)(2,1)S(1)}, u32[]{:S(2)}, u32[]{:S(2)}) collective-permute-start(bf16[256,768]{1,0:T(8,128)(2,1)S(1)} %shard_map.110.refs_6_.refs_2_), channel_id=1, source_target_pairs={{0,2},{1,5},{2,0},{3,7},{4,6},{5,1},{6,4},{7,3},{8,10},{9,13},{10,... | collective-permute-start | bytes 1179656 | tf_op jit(solution)/shard_map/ppermute | solution.py:376
  70.1 6.2 %collective-permute-start.28 = (bf16[64,384]{1,0:T(8,128)(2,1)S(1)}, bf16[64,384]{1,0:T(8,128)(2,1)S(1)}, u32[]{:S(2)}, u32[]{:S(2)}) collective-permute-start(bf16[64,384]{1,0:T(8,128)(2,1)S(1)} %shard_map.111.refs_2_.refs_6_), channel_id=1, source_target_pairs={{0,8},{8,0},{16,24},{24,16},{1,9},{9,1},{17,25},{25,17},{2,10},{10... | collective-permute-start | bytes 147464 | tf_op jit(solution)/shard_map/ppermute | solution.py:388
  71.0 6.0 %collective-permute-start.27 = (bf16[64,384]{1,0:T(8,128)(2,1)S(1)}, bf16[64,384]{1,0:T(8,128)(2,1)S(1)}, u32[]{:S(2)}, u32[]{:S(2)}) collective-permute-start(bf16[64,384]{1,0:T(8,128)(2,1)S(1)} %shard_map.111.refs_2_.refs_6_), channel_id=1, source_target_pairs={{0,16},{8,24},{16,0},{24,8},{1,17},{9,25},{17,1},{25,9},{2,18},{10... | collective-permute-start | bytes 147464 | tf_op jit(solution)/shard_map/ppermute | solution.py:388
  73.1 5.9 %collective-permute-start.26 = (bf16[64,384]{1,0:T(8,128)(2,1)S(1)}, bf16[64,384]{1,0:T(8,128)(2,1)S(1)}, u32[]{:S(2)}, u32[]{:S(2)}) collective-permute-start(bf16[64,384]{1,0:T(8,128)(2,1)S(1)} %shard_map.111.refs_2_.refs_6_), channel_id=1, source_target_pairs={{0,24},{8,16},{16,8},{24,0},{1,25},{9,17},{17,9},{25,1},{2,26},{10... | collective-permute-start | bytes 147464 | tf_op jit(solution)/shard_map/ppermute | solution.py:388
  75.5 10.9 %collective-permute-start.34 = (bf16[256,768]{1,0:T(8,128)(2,1)S(1)}, bf16[256,768]{1,0:T(8,128)(2,1)S(1)}, u32[]{:S(2)}, u32[]{:S(2)}) collective-permute-start(bf16[256,768]{1,0:T(8,128)(2,1)S(1)} %collective-permute-done.33.refs_3_), channel_id=1, source_target_pairs={{0,2},{1,5},{2,0},{3,7},{4,6},{5,1},{6,4},{7,3},{8,10},{9,13},{10,... | collective-permute-start | bytes 1179656 | tf_op jit(solution)/shard_map/ppermute | solution.py:376
  79.5 5.7 %collective-permute-start.30 = (bf16[256,384]{1,0:T(8,128)(2,1)S(1)}, bf16[256,384]{1,0:T(8,128)(2,1)S(1)}, u32[]{:S(2)}, u32[]{:S(2)}) collective-permute-start(bf16[256,384]{1,0:T(8,128)(2,1)S(1)} %shard_map.112.refs_6_.refs_2_), channel_id=1, source_target_pairs={{0,4},{1,3},{2,6},{3,1},{4,0},{5,7},{6,2},{7,5},{8,12},{9,11},{10,... | collective-permute-start | bytes 589832 | tf_op jit(solution)/shard_map/ppermute | solution.py:376
  80.5 12.0 %collective-permute-start.31 = (bf16[256,384]{1,0:T(8,128)(2,1)S(1)}, bf16[256,384]{1,0:T(8,128)(2,1)S(1)}, u32[]{:S(2)}, u32[]{:S(2)}) collective-permute-start(bf16[256,384]{1,0:T(8,128)(2,1)S(1)} %shard_map.112.refs_6_.refs_2_), channel_id=1, source_target_pairs={{0,2},{1,5},{2,0},{3,7},{4,6},{5,1},{6,4},{7,3},{8,10},{9,13},{10,... | collective-permute-start | bytes 589832 | tf_op jit(solution)/shard_map/ppermute | solution.py:376
  85.3 7.2 %collective-permute-start.32 = (bf16[256,384]{1,0:T(8,128)(2,1)S(1)}, bf16[256,384]{1,0:T(8,128)(2,1)S(1)}, u32[]{:S(2)}, u32[]{:S(2)}) collective-permute-start(bf16[256,384]{1,0:T(8,128)(2,1)S(1)} %collective-permute-done.30.refs_3_), channel_id=1, source_target_pairs={{0,2},{1,5},{2,0},{3,7},{4,6},{5,1},{6,4},{7,3},{8,10},{9,13},{10,... | collective-permute-start | bytes 589832 | tf_op jit(solution)/shard_map/ppermute | solution.py:376
  87.0 6.6 %collective-permute-start.36 = (bf16[1024,768]{1,0:T(8,128)(2,1)S(1)}, bf16[1024,768]{1,0:T(8,128)(2,1)S(1)}, u32[]{:S(2)}, u32[]{:S(2)}) collective-permute-start(bf16[1024,768]{1,0:T(8,128)(2,1)S(1)} %shard_map.113.refs_2_.refs_5_), channel_id=1, source_target_pairs={{0,1},{1,0},{2,3},{3,2},{4,5},{5,4},{6,7},{7,6},{8,9},{9,8},{10,11... | collective-permute-start | bytes 4718600 | tf_op jit(solution)/shard_map/ppermute | solution.py:364
  93.1 5.8 %collective-permute-start.35 = (bf16[1024,384]{1,0:T(8,128)(2,1)S(1)}, bf16[1024,384]{1,0:T(8,128)(2,1)S(1)}, u32[]{:S(2)}, u32[]{:S(2)}) collective-permute-start(bf16[1024,384]{1,0:T(8,128)(2,1)S(1)} %shard_map.115.refs_7_.refs_2_), channel_id=1, source_target_pairs={{0,1},{1,0},{2,3},{3,2},{4,5},{5,4},{6,7},{7,6},{8,9},{9,8},{10,11... | collective-permute-start | bytes 2359304 | tf_op jit(solution)/shard_map/ppermute | solution.py:364
  (12 other events, 35.3 us)
